TPU v7x, 256 devices: a whole 4x4x8 slice. The times are simulated.
256 devices in a mesh: prow: 8 (over y, core), pcol: 32 (over x, z).
Axes of the slice: x: 4, y: 4, z: 8, core: 2. Of those that a mesh axis runs over, the one named last changes fastest.
Arguments:
- matrix: bfloat16 [4096, 32768], P('prow', 'pcol'), may hold values from -4 to 4
- scales: float32 [8, 64], replicated, may hold values from 0.5 to 2
Outputs:
- factored: bfloat16 [4096, 32768], P('prow', 'pcol')
All inputs are finite; a program needn't handle non-finite values.
Results may differ from a plain program's by a relative error of at most 0.0046.
Values may be sent and summed in bfloat16 or wider, within the bound.
No kernel may reach another device: no remote copies, remote signals or barrier semaphores. Data moves between devices by JAX's collectives and lax.ppermute only.
A program may use at most 64 MiB of HBM per device.

v0:
```python
import jax
import jax.numpy as jnp
from jax import lax
from jax.sharding import PartitionSpec as P

NB = 512


def broadcast(value, axis, source):
    kept = jnp.where(lax.axis_index(axis) == source, value, 0).astype(value.dtype)
    return lax.psum(kept, axis)


def on_device(matrix, scales):
    rows_dev, cols_dev = matrix.shape
    prow_count = lax.axis_size("prow")
    pcol_count = lax.axis_size("pcol")
    prow_at = lax.axis_index("prow")
    pcol_at = lax.axis_index("pcol")
    row_tiles = rows_dev // NB
    col_tiles = cols_dev // NB
    scale_grid = scales.reshape(row_tiles, prow_count, col_tiles, pcol_count)
    local_scales = lax.dynamic_slice(
        scale_grid, (0, prow_at, 0, pcol_at), (row_tiles, 1, col_tiles, 1)
    ).reshape(row_tiles, col_tiles)
    panel_scales = lax.dynamic_slice(scale_grid, (0, prow_at, 0, 0), (row_tiles, 1, 1, 1)).reshape(
        row_tiles
    )
    row_scale = jnp.repeat(panel_scales, NB)
    head_scale = jnp.repeat(local_scales[0], NB)[None, :]
    panel_block = broadcast(matrix[:, :NB], "pcol", 0)
    lower_unit = jnp.tril(panel_block.astype(jnp.float32) * scales[0, 0], -1) + jnp.eye(
        NB, dtype=jnp.float32
    )
    head_block = matrix.astype(jnp.float32) * head_scale
    upper_rows = lax.linalg.triangular_solve(
        lower_unit, head_block, left_side=True, lower=True, unit_diagonal=True
    )
    u_wire = broadcast(upper_rows.astype(jnp.bfloat16), "prow", 0)
    product = jnp.dot(panel_block, u_wire, preferred_element_type=jnp.float32) * row_scale[:, None]
    full_scale = jnp.repeat(jnp.repeat(local_scales, NB, axis=0), NB, axis=1)
    current = matrix.astype(jnp.float32) * full_scale
    updated = ((current - product) / full_scale).astype(jnp.bfloat16)
    head_tiles = (upper_rows / head_scale).astype(jnp.bfloat16)
    updated = updated.at[:NB].set(jnp.where(prow_at == 0, head_tiles, updated))
    col_ids = lax.broadcasted_iota(jnp.int32, (1, cols_dev), 1)
    in_panel = (pcol_at == 0) & (col_ids < NB)
    return jnp.where(in_panel, matrix, updated)


def solution(mesh):
    placed = (P("prow", "pcol"), P())
    return jax.shard_map(
        on_device, mesh=mesh, in_specs=placed, out_specs=P("prow", "pcol"), check_vma=False
    )
```

profile of v0, /device:TPU:64, one launch (start us, length us, event | category | flops | bytes accessed | tf_op | source)
XLA Modules:
  0.0 298.5 jit_solution(674851261228918036)
XLA Ops:
  6.5 0.0 copy-start.2
  6.5 0.0 all-reduce.3.cloned.1.call-start
  6.5 2.0 slice_select_fusion
  8.5 0.0 all-reduce.3.cloned.1.call-update
  8.5 0.0 all-reduce.5.cloned.1.call-start
  8.6 1.2 slice.43
  9.8 0.8 reshape.55
  10.6 0.1 constant_dynamic-slice_fusion.2
  10.6 0.1 copy.4
  10.7 0.1 broadcast_bitcast_fusion
  10.8 0.0 copy-done.2
  10.8 0.3 convert_multiply_fusion
  11.1 148.1 %all-reduce.3.cloned.1.call-done = bf16[512,512]{1,0:T(8,128)(2,1)} async-done(((bf16[512,512]{1,0:T(8,128)(2,1)}), bf16[512,512]{1,0:T(8,128)(2,1)}) %all-reduce.3.cloned.1.call-update) | async-done | bytes 524304 | tf_op jit(solution)/shard_map/psum | solution.py:11
  159.2 1.9 convert_add_fusion
  161.1 10.4 %while.3 = (s32[]{:T(128)}, f32[512,512]{1,0:T(8,128)S(1)}, s32[4,2]{0,1:T(2,128)S(1)}, f32[4,128,128]{2,1,0:T(8,128)}, s32[]{:T(128)}) while((s32[]{:T(128)}, f32[512,512]{1,0:T(8,128)S(1)}, s32[4,2]{0,1:T(2,128)S(1)}, f32[4,128,128]{2,1,0:T(8,128)}, s32[]{:T(128)}) %tuple.26), condition=%wide.while_cond.1, body=%wide.while_body.1.sunk | while | flops 2 | bytes 132205 | solution.py:36
  161.2 0.1 constant_dynamic-slice_fusion.4
  161.2 0.5 fusion.35
  161.8 2.0 bitcast_dynamic-update-slice_fusion.2
  163.7 0.1 constant_dynamic-slice_fusion.4
  163.8 0.5 fusion.35
  164.3 2.0 bitcast_dynamic-update-slice_fusion.2
  166.3 0.1 constant_dynamic-slice_fusion.4
  166.4 0.5 fusion.35
  166.9 2.0 bitcast_dynamic-update-slice_fusion.2
  168.9 0.1 constant_dynamic-slice_fusion.4
  169.0 0.5 fusion.35
  169.5 2.0 bitcast_dynamic-update-slice_fusion.2
  171.5 0.0 copy-start.1
  171.5 1.0 copy-done.1
  172.5 40.1 %custom-call.3 = f32[4,128,128]{1,2,0:T(8,128)S(1)} custom-call(f32[4,128,128]{2,1,0:T(8,128)} %get-tuple-element.32), custom_call_target="InvertDiagBlocksLowerTriangular" | custom-call | tf_op jit(solution)/shard_map/triangular_solve | solution.py:36
  212.6 0.6 fusion.16
  213.2 1.4 convolution_subtract_fusion.1
  214.7 0.6 fusion.23
  215.3 1.6 convolution_subtract_fusion
  216.9 0.6 fusion.21
  217.6 0.0 copy-start
  217.6 2.2 fusion.6
  219.8 0.6 fusion.20
  220.5 0.0 copy-done
  220.5 0.0 copy-start.3
  220.5 0.0 copy-start.4
  220.5 1.2 fusion.12
  221.7 0.0 all-reduce.5.cloned.1.call-update
  221.7 0.6 constant_dynamic-slice_fusion.1
  222.3 65.3 %all-reduce.5.cloned.1.call-done = bf16[512,1024]{1,0:T(8,128)(2,1)} async-done(((bf16[512,1024]{1,0:T(8,128)(2,1)}), bf16[512,1024]{1,0:T(8,128)(2,1)}) %all-reduce.5.cloned.1.call-update) | async-done | bytes 1048592 | tf_op jit(solution)/shard_map/psum | solution.py:11
  287.6 0.0 copy-done.3
  287.6 0.0 copy-done.4
  287.6 4.1 %fusion.11 = bf16[512,1024]{1,0:T(8,128)(2,1)} fusion(bf16[512,1024]{1,0:T(8,128)(2,1)S(1)} %copy-done.3, bf16[512,512]{1,0:T(8,128)(2,1)S(1)} %copy-done.4, bf16[512,1024]{1,0:T(8,128)(2,1)} %all-reduce.5.cloned.1.call-done, f32[128,1024]{1,0:T(8,128)S(1)} %fusion.20, f32[128,1024]{1,0:T(8,128)} %copy-done, f32[128,1024]{1,0:T(8,128)S(1)} %fusion.23, ...), kind=kOutput, calls=%fused_computation.17 | convolution fusion | flops 543686656 | bytes 5772293 | tf_op jit(solution)/shard_map/dot_general | solution.py:40
  (6 shorter events, 0.0 us)
Async XLA Ops:
  6.5 4.3 %copy-start.2 = (bf16[512,1024]{1,0:T(8,128)(2,1)S(1)}, bf16[512,1024]{1,0:T(8,128)(2,1)}, u32[]{:S(2)}) copy-start(bf16[512,1024]{1,0:T(8,128)(2,1)} %param.6) | copy-start | bytes 3145732
  6.5 152.7 %all-reduce.3.cloned.1.call-start = ((), (), s32[]{:S(2)}) async-start(), calls=%async_computation | async-start | bytes 1048576 | tf_op jit(solution)/shard_map/psum | solution.py:11
  8.5 279.1 %all-reduce.5.cloned.1.call-start = ((), (), s32[]{:S(2)}) async-start(), calls=%async_computation.1 | async-start | bytes 2097152 | tf_op jit(solution)/shard_map/psum | solution.py:11
  171.5 1.0 copy-start.1
  217.6 2.9 copy-start
  220.5 67.2 %copy-start.3 = (bf16[512,1024]{1,0:T(8,128)(2,1)S(1)}, bf16[512,1024]{1,0:T(8,128)(2,1)}, u32[]{:S(2)}) copy-start(bf16[512,1024]{1,0:T(8,128)(2,1)} %param.6) | copy-start | bytes 3145732
  220.5 67.1 %copy-start.4 = (bf16[512,512]{1,0:T(8,128)(2,1)S(1)}, bf16[512,512]{1,0:T(8,128)(2,1)}, u32[]{:S(2)}) copy-start(bf16[512,512]{1,0:T(8,128)(2,1)} %all-reduce.3.cloned.1.call-done) | copy-start | bytes 1572868
Sparse Core Ops, SparseCore 0:
  10.7 148.4 all-reduce.2
  221.8 65.7 all-reduce.4
where the time goes:
time: 300 us; the launch traced here: 299 us
  waiting for transfers between devices  213 us (71%)
  other arithmetic  45.5 us (15%)
  local copies, waits for them, and re-layouts  14.1 us (5%)
  between operations  13.5 us (4%)
  matrix products  11.9 us (4%)
    psum x2, waiting for transfers between devices, broadcast(): return lax.psum(kept, axis)  213 us
    another operation x4, other arithmetic, on_device(): lax.linalg.triangular_solve(lower_unit, head_block, left_side=True, lower...  42.1 us
    another operation x12, local copies, waits for them, and re-layouts  10.3 us
    another operation x7, matrix products, on_device(): lax.linalg.triangular_solve(lower_unit, head_block, left_side=True, lower...  7.79 us
  transfers between devices with their start and end apart: 2, of which 2 were waited for; matrix products, arithmetic and copies ran while one was open for 1% of the time, Pallas kernels for 0%

commit v1 on v0

v1 whole, which is shorter than its diff:
```python
import functools

import jax
import jax.numpy as jnp
from jax import lax
from jax.experimental import pallas as pl
from jax.experimental.pallas import tpu as pltpu
from jax.sharding import PartitionSpec as P

NB = 512
BASE = 128
XS = 4
ZS = 8
BF = jnp.bfloat16
F32 = jnp.float32


def bdot(a, b):
    return jnp.dot(a, b, preferred_element_type=F32)


def split3(x):
    high = x.astype(BF)
    rest = x - high.astype(F32)
    mid = rest.astype(BF)
    low = (rest - mid.astype(F32)).astype(BF)
    return high, mid, low


def dot_exact_left(t, x):
    high, mid, low = split3(x)
    return bdot(t, high) + (bdot(t, mid) + bdot(t, low))


def dot_full(a, b):
    ah, am, al = split3(a)
    bh, bm, bl = split3(b)
    return bdot(ah, bh) + (
        (bdot(ah, bm) + bdot(am, bh)) + (bdot(am, bm) + (bdot(ah, bl) + bdot(al, bh)))
    )


def invert_diagonal(tiles, s):
    n = BASE
    r = lax.broadcasted_iota(jnp.int32, (n, n), 0)
    c = lax.broadcasted_iota(jnp.int32, (n, n), 1)
    eye = (r == c).astype(F32)

    def mask(k):
        return ((r // (2 * k)) == (c // (2 * k))) & ((r // k) % 2 == 1) & ((c // k) % 2 == 0)

    first = mask(1)
    inverses = [eye - jnp.where(first, t.astype(F32) * s, 0.0) for t in tiles]
    k = 2
    while k < n:
        at = mask(k)
        inner = [
            dot_exact_left(jnp.where(at, t, jnp.zeros_like(t)), x) * s
            for t, x in zip(tiles, inverses)
        ]
        inverses = [x - dot_full(x, y) for x, y in zip(inverses, inner)]
        k *= 2
    return inverses


def solve_kernel(scales_ref, low_ref, swap_ref, matrix_ref, w0_ref, w1_ref, w2_ref, w3_ref, inv_ref):
    outs = (w0_ref, w1_ref, w2_ref, w3_ref)
    holder = lax.axis_index("pcol") == 0
    prow_at = lax.axis_index("prow")

    @pl.when(jnp.logical_not(holder))
    def _():
        for ref in outs:
            ref[...] = jnp.zeros_like(ref)

    @pl.when(holder)
    def _():
        s = scales_ref[0, 0]
        packed = low_ref[...] + swap_ref[...]
        t = [[None] * 4 for _ in range(4)]
        for j in range(4):
            t[2][j] = packed[:128, 128 * j : 128 * (j + 1)]
            t[3][j] = packed[128:256, 128 * j : 128 * (j + 1)]
        t[0][0], t[0][1] = packed[256:, :128], packed[256:, 128:256]
        t[1][0], t[1][1] = packed[256:, 256:384], packed[256:, 384:]
        x = invert_diagonal([t[i][i] for i in range(4)], s)
        halves = []
        for h in (0, 2):
            off = -dot_full(x[h + 1], dot_exact_left(t[h + 1][h], x[h]) * s)
            top = jnp.concatenate([x[h], jnp.zeros_like(x[h])], 1)
            halves.append(jnp.concatenate([top, jnp.concatenate([off, x[h + 1]], 1)], 0))
        corner = jnp.concatenate(
            [jnp.concatenate([t[2][0], t[2][1]], 1), jnp.concatenate([t[3][0], t[3][1]], 1)], 0
        )
        off = -dot_full(halves[1], dot_exact_left(corner, halves[0]) * s)
        inv_ref[:256, :256] = halves[0]
        inv_ref[:256, 256:] = jnp.zeros_like(off)
        inv_ref[256:, :256] = off
        inv_ref[256:, 256:] = halves[1]
        inverse = inv_ref[...]
        high = inverse.astype(BF)
        low = (inverse - high.astype(F32)).astype(BF)
        for i, ref in enumerate(outs):
            a = matrix_ref[128 * i : 128 * (i + 1), :NB]
            w = (bdot(a, high) + bdot(a, low)).astype(BF)
            ref[...] = jnp.where(prow_at == 0, high[128 * i : 128 * (i + 1)], w)


def solve(scales, low, swap, matrix):
    chunk = jax.ShapeDtypeStruct((128, NB), BF)
    vmem = pl.BlockSpec(memory_space=pltpu.VMEM)
    return pl.pallas_call(
        solve_kernel,
        out_shape=[chunk] * 4,
        in_specs=[pl.BlockSpec(memory_space=pltpu.SMEM), vmem, vmem, vmem],
        out_specs=[vmem] * 4,
        scratch_shapes=[pltpu.VMEM((NB, NB), F32)],
        compiler_params=pltpu.CompilerParams(vmem_limit_bytes=40 * 2**20),
        cost_estimate=pl.CostEstimate(flops=4 * 10**9, bytes_accessed=4 * 2**20, transcendentals=0),
    )(scales, low, swap, matrix)


def update_kernel(
    scales_ref, matrix_ref, mine_ref, swap_ref, extra_ref, q0_ref, q1_ref, q3_ref, q2_ref, out_ref,
    head_ref, w_ref, sems,
):
    prow_at = lax.axis_index("prow")
    pcol_at = lax.axis_index("pcol")
    x_at = pcol_at // ZS

    def place(src, dst, at):
        return pltpu.make_async_copy(src, dst, sems.at[at])

    copies = []
    for at, (ref, shift) in enumerate(((q0_ref, 0), (q1_ref, 3), (q3_ref, 1), (q2_ref, 2))):
        row = pl.multiple_of(lax.rem(x_at + shift, XS) * 128, 128)
        copies.append(place(ref, w_ref.at[pl.ds(row, 128), :], at))
        copies[-1].start()

    @pl.when(prow_at == 0)
    def _():
        head_ref[...] = matrix_ref[...]

    @pl.when(prow_at == 1)
    def _():
        one = place(swap_ref, head_ref.at[:256], 4)
        two = place(extra_ref, head_ref.at[256:], 5)
        one.start()
        two.start()
        one.wait()
        two.wait()

    first = (prow_at == 2) | (prow_at == 4) | (prow_at == 7)

    @pl.when(first)
    def _():
        one = place(mine_ref, head_ref.at[:256], 4)
        two = place(swap_ref, head_ref.at[256:], 5)
        one.start()
        two.start()
        one.wait()
        two.wait()

    @pl.when((prow_at > 1) & jnp.logical_not(first))
    def _():
        one = place(swap_ref, head_ref.at[:256], 4)
        two = place(mine_ref, head_ref.at[256:], 5)
        one.start()
        two.start()
        one.wait()
        two.wait()

    for copy in copies:
        copy.wait()

    for t in range(2):
        cols = slice(NB * t, NB * (t + 1))
        col = NB // 16 * t + pcol_at
        scale = jnp.full((1, NB), scales_ref[prow_at, col], F32)
        factor = (scales_ref[prow_at, 0] * scales_ref[0, col]) / scale
        for i in range(4):
            rows = slice(128 * i, 128 * (i + 1))
            product = bdot(w_ref[rows, :], head_ref[:, cols])
            own = matrix_ref[rows, cols]
            updated = (own.astype(F32) - factor * product).astype(BF)
            result = jnp.where(prow_at == 0, product.astype(BF), updated)
            if t == 0:
                result = jnp.where(pcol_at == 0, own, result)
            out_ref[rows, cols] = result


def update(scales, matrix, heads, chunks):
    vmem = pl.BlockSpec(memory_space=pltpu.VMEM)
    anywhere = pl.BlockSpec(memory_space=pl.ANY)
    return pl.pallas_call(
        update_kernel,
        out_shape=jax.ShapeDtypeStruct(matrix.shape, BF),
        in_specs=[pl.BlockSpec(memory_space=pltpu.SMEM), vmem] + [anywhere] * 7,
        out_specs=vmem,
        scratch_shapes=[
            pltpu.VMEM((NB, 2 * NB), BF),
            pltpu.VMEM((NB, NB), BF),
            pltpu.SemaphoreType.DMA((6,)),
        ],
        compiler_params=pltpu.CompilerParams(vmem_limit_bytes=40 * 2**20),
        cost_estimate=pl.CostEstimate(flops=2**29, bytes_accessed=4 * 2**20, transcendentals=0),
    )(scales, matrix, *heads, *chunks)


def send(value, pairs):
    flat = [
        tuple(p * XS * ZS + x * ZS + z for p, x, z in (source, target)) for source, target in pairs
    ]
    return lax.ppermute(value, ("prow", "pcol"), flat)


def along_prow(value, pairs, columns):
    return send(value, [((a, x, z), (b, x, z)) for a, b in pairs for x, z in columns])


def along_x(value, pairs, depths):
    return send(
        value, [((p, a, z), (p, b, z)) for a, b in pairs for p in range(8) for z in depths]
    )


def along_z(value, pairs):
    return send(
        value, [((p, x, a), (p, x, b)) for a, b in pairs for p in range(8) for x in range(XS)]
    )


def on_device(matrix, scales):
    everywhere = [(x, z) for x in range(XS) for z in range(ZS)]
    corner = [(0, 0)]
    prow_at = lax.axis_index("prow")
    low = jnp.concatenate(
        [
            matrix[256:, :NB],
            jnp.concatenate([matrix[:128, :256], matrix[128:256, :256]], 1),
        ],
        0,
    )
    low = jnp.where((prow_at == 0) & (lax.axis_index("pcol") == 0), low, 0).astype(BF)
    low_y = [along_prow(low, [(0, p)], corner) for p in (4, 2, 6)]
    low = low + low_y[0] + low_y[1] + low_y[2]
    low_swap = along_prow(low, [(0, 1), (2, 3), (4, 5), (6, 7)], corner)

    upper, lower = matrix[:256], matrix[256:]
    to2 = along_prow(upper, [(0, 2)], everywhere)
    to6 = along_prow(lower, [(0, 6)], everywhere)
    to3 = along_prow(lower, [(0, 3)], everywhere)
    to7 = along_prow(upper, [(0, 7)], everywhere)
    mine = to2 + to6
    to45 = along_prow(mine, [(2, 4), (6, 5)], everywhere)
    mine = jnp.where(prow_at == 0, upper, mine + to3 + to7 + to45)
    swap = along_prow(mine, [(0, 1)] + [(p, p ^ 1) for p in range(2, 8)], everywhere)
    extra = along_prow(lower, [(0, 1)], everywhere)

    w = solve(scales, low, low_swap, matrix)
    w_x = [along_x(w[k], [(0, k)], [0]) for k in (2, 1, 3)]
    q = w[0] + w_x[0] + w_x[1] + w_x[2]
    q3, q5 = along_z(q, [(0, 3)]), along_z(q, [(0, 5)])
    q = q + q3 + q5
    up, down = along_z(q, [(0, 1), (3, 4), (5, 6)]), along_z(q, [(0, 7), (3, 2)])
    q = q + up + down
    q2 = along_x(q, [(a, (a + 2) % XS) for a in range(XS)], range(ZS))
    q1 = along_x(q, [(a, (a + 1) % XS) for a in range(XS)], range(ZS))
    q3 = along_x(q, [(a, (a + 3) % XS) for a in range(XS)], range(ZS))
    return update(scales, matrix, (mine, swap, extra), (q, q1, q3, q2))


def solution(mesh):
    placed = (P("prow", "pcol"), P())
    return jax.shard_map(
        on_device, mesh=mesh, in_specs=placed, out_specs=P("prow", "pcol"), check_vma=False
    )
```

time: 300 us -> 64.2 us (0.21)
  the two profiles are of different devices: /device:TPU:64 before, /device:TPU:42 now
where the time goes in v1:
time: 64.2 us; the launch traced here: 63.7 us
  waiting for transfers between devices  36.7 us (57%)
  starting transfers between devices  20.2 us (31%)
  Pallas kernels  3.89 us (6%)
  local copies, waits for them, and re-layouts  2.02 us (3%)
    ppermute x21, waiting for transfers between devices, send(): return lax.ppermute(value, ('prow', 'pcol'), flat)  36.7 us
    ppermute x21, starting transfers between devices, send(): return lax.ppermute(value, ('prow', 'pcol'), flat)  20.2 us
    pallas_call x1, Pallas kernels, update(): pl.pallas_call(update_kernel, out_shape=jax.ShapeDtypeStruct(matrix.shape...  3.24 us
  transfers between devices with their start and end apart: 21, of which 5 were waited for; matrix products, arithmetic and copies ran while one was open for 1% of the time, Pallas kernels for 1%

profile of v1, /device:TPU:42, one launch (start us, length us, event | category | flops | bytes accessed | tf_op | source)
XLA Modules:
  0.0 63.7 jit_solution(11648763649697775625)
XLA Ops:
  0.0 1.0 %fusion = (bf16[128,256]{1,0:T(8,128)(2,1)S(1)}, bf16[128,256]{1,0:T(8,128)(2,1)S(1)}) fusion(bf16[512,1024]{1,0:T(8,128)(2,1)} %matrix_ref.3), kind=kLoop, calls=%fused_computation.6 | loop fusion | bytes 262144 | tf_op jit(solution)/shard_map/slice | solution.py:240
  1.0 1.0 %slice.17 = bf16[256,512]{1,0:T(8,128)(2,1)S(1)} slice(bf16[512,1024]{1,0:T(8,128)(2,1)} %matrix_ref.3), slice={[256:512], [0:512]} | slice | bytes 524288 | tf_op jit(solution)/shard_map/slice | solution.py:239
  2.0 0.1 maximum_select_fusion
  2.0 0.7 %collective-permute-start.9 = (bf16[384,512]{1,0:T(8,128)(2,1)S(1)}, bf16[384,512]{1,0:T(8,128)(2,1)S(1)}, u32[]{:S(2)}, u32[]{:S(2)}) collective-permute-start(bf16[384,512]{1,0:T(8,128)(2,1)S(1)} %maximum_select_fusion), channel_id=1, source_target_pairs={{0,192}} | collective-permute-start | bytes 1179656 | tf_op jit(solution)/shard_map/ppermute | solution.py:214
  2.7 0.7 %collective-permute-start.8 = (bf16[384,512]{1,0:T(8,128)(2,1)S(1)}, bf16[384,512]{1,0:T(8,128)(2,1)S(1)}, u32[]{:S(2)}, u32[]{:S(2)}) collective-permute-start(bf16[384,512]{1,0:T(8,128)(2,1)S(1)} %maximum_select_fusion), channel_id=1, source_target_pairs={{0,64}} | collective-permute-start | bytes 1179656 | tf_op jit(solution)/shard_map/ppermute | solution.py:214
  3.4 0.7 %collective-permute-start.7 = (bf16[384,512]{1,0:T(8,128)(2,1)S(1)}, bf16[384,512]{1,0:T(8,128)(2,1)S(1)}, u32[]{:S(2)}, u32[]{:S(2)}) collective-permute-start(bf16[384,512]{1,0:T(8,128)(2,1)S(1)} %maximum_select_fusion), channel_id=1, source_target_pairs={{0,128}} | collective-permute-start | bytes 1179656 | tf_op jit(solution)/shard_map/ppermute | solution.py:214
  4.1 0.1 fusion.1
  4.2 1.3 %collective-permute-start = (bf16[256,1024]{1,0:T(8,128)(2,1)S(1)}, bf16[256,1024]{1,0:T(8,128)(2,1)S(1)}, u32[]{:S(2)}, u32[]{:S(2)}) collective-permute-start(bf16[256,1024]{1,0:T(8,128)(2,1)S(1)} %get-tuple-element.16), channel_id=1, source_target_pairs={{0,64},{1,65},{2,66},{3,67},{4,68},{5,69},{6,70},{7,71},{8,72},{9,... | collective-permute-start | bytes 1572872 | tf_op jit(solution)/shard_map/ppermute | solution.py:214
  5.5 0.7 %collective-permute-start.1 = (bf16[256,1024]{1,0:T(8,128)(2,1)S(1)}, bf16[256,1024]{1,0:T(8,128)(2,1)S(1)}, u32[]{:S(2)}, u32[]{:S(2)}) collective-permute-start(bf16[256,1024]{1,0:T(8,128)(2,1)S(1)} %get-tuple-element.15), channel_id=1, source_target_pairs={{0,192},{1,193},{2,194},{3,195},{4,196},{5,197},{6,198},{7,199},{8... | collective-permute-start | bytes 1572872 | tf_op jit(solution)/shard_map/ppermute | solution.py:214
  6.2 0.0 collective-permute-done.9
  6.2 0.0 collective-permute-done.7
  6.2 0.1 add_add_fusion.low_ref
  6.3 0.0 copy-start.1
  6.3 0.7 %collective-permute-start.10 = (bf16[384,512]{1,0:T(8,128)(2,1)S(1)}, bf16[384,512]{1,0:T(8,128)(2,1)S(1)}, u32[]{:S(2)}, u32[]{:S(2)}) collective-permute-start(bf16[384,512]{1,0:T(8,128)(2,1)S(1)} %add_add_fusion.low_ref), channel_id=1, source_target_pairs={{0,32},{64,96},{128,160},{192,224}} | collective-permute-start | bytes 1179656 | tf_op jit(solution)/shard_map/ppermute | solution.py:214
  7.0 0.7 %collective-permute-start.3 = (bf16[256,1024]{1,0:T(8,128)(2,1)S(1)}, bf16[256,1024]{1,0:T(8,128)(2,1)S(1)}, u32[]{:S(2)}, u32[]{:S(2)}) collective-permute-start(bf16[256,1024]{1,0:T(8,128)(2,1)S(1)} %get-tuple-element.16), channel_id=1, source_target_pairs={{0,224},{1,225},{2,226},{3,227},{4,228},{5,229},{6,230},{7,231},{8... | collective-permute-start | bytes 1572872 | tf_op jit(solution)/shard_map/ppermute | solution.py:214
  7.7 0.7 %collective-permute-start.2 = (bf16[256,1024]{1,0:T(8,128)(2,1)S(1)}, bf16[256,1024]{1,0:T(8,128)(2,1)S(1)}, u32[]{:S(2)}, u32[]{:S(2)}) collective-permute-start(bf16[256,1024]{1,0:T(8,128)(2,1)S(1)} %get-tuple-element.15), channel_id=1, source_target_pairs={{0,96},{1,97},{2,98},{3,99},{4,100},{5,101},{6,102},{7,103},{8,104... | collective-permute-start | bytes 1572872 | tf_op jit(solution)/shard_map/ppermute | solution.py:214
  8.4 6.8 %collective-permute-done = bf16[256,1024]{1,0:T(8,128)(2,1)S(1)} collective-permute-done((bf16[256,1024]{1,0:T(8,128)(2,1)S(1)}, bf16[256,1024]{1,0:T(8,128)(2,1)S(1)}, u32[]{:S(2)}, u32[]{:S(2)}) %collective-permute-start) | collective-permute-done | bytes 524320 | tf_op jit(solution)/shard_map/ppermute | solution.py:214
  15.3 0.0 collective-permute-done.1
  15.3 0.2 add.42
  15.5 1.3 %collective-permute-start.4 = (bf16[256,1024]{1,0:T(8,128)(2,1)S(1)}, bf16[256,1024]{1,0:T(8,128)(2,1)S(1)}, u32[]{:S(2)}, u32[]{:S(2)}) collective-permute-start(bf16[256,1024]{1,0:T(8,128)(2,1)S(1)} %add.42), channel_id=1, source_target_pairs={{64,128},{65,129},{66,130},{67,131},{68,132},{69,133},{70,134},{71... | collective-permute-start | bytes 1572872 | tf_op jit(solution)/shard_map/ppermute | solution.py:214
  16.8 0.0 collective-permute-done.10.swap_ref
  16.8 0.6 %shard_map.28 = (bf16[128,512]{1,0:T(8,128)(2,1)S(1)}, bf16[128,512]{1,0:T(8,128)(2,1)S(1)}, bf16[128,512]{1,0:T(8,128)(2,1)S(1)}, bf16[128,512]{1,0:T(8,128)(2,1)S(1)}) custom-call(f32[8,64]{1,0:T(8,128)S(1)} %copy-done.1, bf16[384,512]{1,0:T(8,128)(2,1)S(1)} %add_add_fusion.low_ref, bf16[384,512]{1,0:T(8,128)(2,1)S(1)} %collective-permute-done.10.swap_ref, ...), custom_call_target="tpu_custom_call" | custom-call | flops 4000000000 | bytes 4194304 | tf_op jit(solution)/shard_map/pallas_call | solution.py:112
  17.5 0.7 %collective-permute-start.13 = (bf16[128,512]{1,0:T(8,128)(2,1)S(1)}, bf16[128,512]{1,0:T(8,128)(2,1)S(1)}, u32[]{:S(2)}, u32[]{:S(2)}) collective-permute-start(bf16[128,512]{1,0:T(8,128)(2,1)S(1)} %get-tuple-element.12), channel_id=1, source_target_pairs={{0,24},{32,56},{64,88},{96,120},{128,152},{160,184},{192,216},{224... | collective-permute-start | bytes 393224 | tf_op jit(solution)/shard_map/ppermute | solution.py:214
  18.2 0.7 %collective-permute-start.12 = (bf16[128,512]{1,0:T(8,128)(2,1)S(1)}, bf16[128,512]{1,0:T(8,128)(2,1)S(1)}, u32[]{:S(2)}, u32[]{:S(2)}) collective-permute-start(bf16[128,512]{1,0:T(8,128)(2,1)S(1)} %get-tuple-element.11), channel_id=1, source_target_pairs={{0,8},{32,40},{64,72},{96,104},{128,136},{160,168},{192,200},{224,... | collective-permute-start | bytes 393224 | tf_op jit(solution)/shard_map/ppermute | solution.py:214
  18.8 0.0 collective-permute-done.13
  18.9 0.7 %collective-permute-start.11 = (bf16[128,512]{1,0:T(8,128)(2,1)S(1)}, bf16[128,512]{1,0:T(8,128)(2,1)S(1)}, u32[]{:S(2)}, u32[]{:S(2)}) collective-permute-start(bf16[128,512]{1,0:T(8,128)(2,1)S(1)} %get-tuple-element.10), channel_id=1, source_target_pairs={{0,16},{32,48},{64,80},{96,112},{128,144},{160,176},{192,208},{224... | collective-permute-start | bytes 393224 | tf_op jit(solution)/shard_map/ppermute | solution.py:214
  19.5 0.7 %collective-permute-start.6 = (bf16[256,1024]{1,0:T(8,128)(2,1)S(1)}, bf16[256,1024]{1,0:T(8,128)(2,1)S(1)}, u32[]{:S(2)}, u32[]{:S(2)}) collective-permute-start(bf16[256,1024]{1,0:T(8,128)(2,1)S(1)} %get-tuple-element.15), channel_id=1, source_target_pairs={{0,32},{1,33},{2,34},{3,35},{4,36},{5,37},{6,38},{7,39},{8,40},{9,... | collective-permute-start | bytes 1572872 | tf_op jit(solution)/shard_map/ppermute | solution.py:214
  20.2 0.0 collective-permute-done.11
  20.3 0.7 %collective-permute-start.15 = (bf16[128,512]{1,0:T(8,128)(2,1)S(1)}, bf16[128,512]{1,0:T(8,128)(2,1)S(1)}, u32[]{:S(2)}, u32[]{:S(2)}) collective-permute-start(bf16[128,512]{1,0:T(8,128)(2,1)S(1)} %add_add_fusion.3), channel_id=1, source_target_pairs={{0,5},{8,13},{16,21},{24,29},{32,37},{40,45},{48,53},{56,61},{64,6... | collective-permute-start | bytes 393224 | tf_op jit(solution)/shard_map/ppermute | solution.py:214
  21.0 0.7 %collective-permute-start.14 = (bf16[128,512]{1,0:T(8,128)(2,1)S(1)}, bf16[128,512]{1,0:T(8,128)(2,1)S(1)}, u32[]{:S(2)}, u32[]{:S(2)}) collective-permute-start(bf16[128,512]{1,0:T(8,128)(2,1)S(1)} %add_add_fusion.3), channel_id=1, source_target_pairs={{0,3},{8,11},{16,19},{24,27},{32,35},{40,43},{48,51},{56,59},{64,6... | collective-permute-start | bytes 393224 | tf_op jit(solution)/shard_map/ppermute | solution.py:214
  21.7 0.0 collective-permute-done.2
  21.7 1.8 %collective-permute-done.4 = bf16[256,1024]{1,0:T(8,128)(2,1)S(1)} collective-permute-done((bf16[256,1024]{1,0:T(8,128)(2,1)S(1)}, bf16[256,1024]{1,0:T(8,128)(2,1)S(1)}, u32[]{:S(2)}, u32[]{:S(2)}) %collective-permute-start.4) | collective-permute-done | bytes 524320 | tf_op jit(solution)/shard_map/ppermute | solution.py:214
  23.5 0.1 add_select_fusion.mine_ref
  23.6 1.9 %collective-permute-start.5 = (bf16[256,1024]{1,0:T(8,128)(2,1)S(1)}, bf16[256,1024]{1,0:T(8,128)(2,1)S(1)}, u32[]{:S(2)}, u32[]{:S(2)}) collective-permute-start(bf16[256,1024]{1,0:T(8,128)(2,1)S(1)} %add_select_fusion.mine_ref), channel_id=1, source_target_pairs={{0,32},{1,33},{2,34},{3,35},{4,36},{5,37},{6,38},{7,39},{8,40},{9,... | collective-permute-start | bytes 1572872 | tf_op jit(solution)/shard_map/ppermute | solution.py:214
  25.5 0.0 collective-permute-done.15
  25.6 0.0 collective-permute-done.14
  25.6 0.7 %collective-permute-start.17 = (bf16[128,512]{1,0:T(8,128)(2,1)S(1)}, bf16[128,512]{1,0:T(8,128)(2,1)S(1)}, u32[]{:S(2)}, u32[]{:S(2)}) collective-permute-start(bf16[128,512]{1,0:T(8,128)(2,1)S(1)} %add_add_fusion.2), channel_id=1, source_target_pairs={{0,7},{8,15},{16,23},{24,31},{32,39},{40,47},{48,55},{56,63},{64,7... | collective-permute-start | bytes 393224 | tf_op jit(solution)/shard_map/ppermute | solution.py:214
  26.3 1.3 %collective-permute-start.16 = (bf16[128,512]{1,0:T(8,128)(2,1)S(1)}, bf16[128,512]{1,0:T(8,128)(2,1)S(1)}, u32[]{:S(2)}, u32[]{:S(2)}) collective-permute-start(bf16[128,512]{1,0:T(8,128)(2,1)S(1)} %add_add_fusion.2), channel_id=1, source_target_pairs={{0,1},{8,9},{16,17},{24,25},{32,33},{40,41},{48,49},{56,57},{64,65... | collective-permute-start | bytes 393224 | tf_op jit(solution)/shard_map/ppermute | solution.py:214
  27.6 0.0 collective-permute-done.17
  27.6 21.9 %collective-permute-done.16 = bf16[128,512]{1,0:T(8,128)(2,1)S(1)} collective-permute-done((bf16[128,512]{1,0:T(8,128)(2,1)S(1)}, bf16[128,512]{1,0:T(8,128)(2,1)S(1)}, u32[]{:S(2)}, u32[]{:S(2)}) %collective-permute-start.16) | collective-permute-done | bytes 131104 | tf_op jit(solution)/shard_map/ppermute | solution.py:214
  49.5 3.3 %collective-permute-start.18 = (bf16[128,512]{1,0:T(8,128)(2,1)S(1)}, bf16[128,512]{1,0:T(8,128)(2,1)S(1)}, u32[]{:S(2)}, u32[]{:S(2)}) collective-permute-start(bf16[128,512]{1,0:T(8,128)(2,1)S(1)} %add_add_fusion.1.q0_ref), channel_id=1, source_target_pairs={{0,8},{1,9},{2,10},{3,11},{4,12},{5,13},{6,14},{7,15},{32,40},{33,... | collective-permute-start | bytes 393224 | tf_op jit(solution)/shard_map/ppermute | solution.py:214
  52.8 0.0 collective-permute-start.19
  52.8 1.6 %collective-permute-start.20 = (bf16[128,512]{1,0:T(8,128)(2,1)S(1)}, bf16[128,512]{1,0:T(8,128)(2,1)S(1)}, u32[]{:S(2)}, u32[]{:S(2)}) collective-permute-start(bf16[128,512]{1,0:T(8,128)(2,1)S(1)} %add_add_fusion.1.q0_ref), channel_id=1, source_target_pairs={{0,16},{1,17},{2,18},{3,19},{4,20},{5,21},{6,22},{7,23},{32,48},{3... | collective-permute-start | bytes 393224 | tf_op jit(solution)/shard_map/ppermute | solution.py:214
  54.3 0.0 collective-permute-done.6.extra_ref
  54.3 1.0 %collective-permute-done.18.q1_ref = bf16[128,512]{1,0:T(8,128)(2,1)S(1)} collective-permute-done((bf16[128,512]{1,0:T(8,128)(2,1)S(1)}, bf16[128,512]{1,0:T(8,128)(2,1)S(1)}, u32[]{:S(2)}, u32[]{:S(2)}) %collective-permute-start.18) | collective-permute-done | bytes 131104 | tf_op jit(solution)/shard_map/ppermute | solution.py:214
  55.3 5.2 %collective-permute-done.19.q3_ref = bf16[128,512]{1,0:T(8,128)(2,1)S(1)} collective-permute-done((bf16[128,512]{1,0:T(8,128)(2,1)S(1)}, bf16[128,512]{1,0:T(8,128)(2,1)S(1)}, u32[]{:S(2)}, u32[]{:S(2)}) %collective-permute-start.19) | collective-permute-done | bytes 131104 | tf_op jit(solution)/shard_map/ppermute | solution.py:214
  60.5 0.0 collective-permute-done.20.q2_ref
  60.5 3.2 %shard_map.29 = bf16[512,1024]{1,0:T(8,128)(2,1)} custom-call(f32[8,64]{1,0:T(8,128)S(1)} %copy-done.1, bf16[512,1024]{1,0:T(8,128)(2,1)S(1)} %copy-done, bf16[256,1024]{1,0:T(8,128)(2,1)S(1)} %add_select_fusion.mine_ref, bf16[256,1024]{1,0:T(8,128)(2,1)S(1)} %collective-permute-done.5.swap_ref, bf16[256,1024]{1,0:T(8,128)(2,1)S(1)} %collective-permute-done.6.extra_ref, ...), custom_call_target="tpu_custom_call" | custom-call | flops 536870912 | bytes 4194304 | tf_op jit(solution)/shard_map/pallas_call | solution.py:195
  (10 shorter events, 0.1 us)
Async XLA Ops:
  0.0 4.1 %copy-start = (bf16[512,1024]{1,0:T(8,128)(2,1)S(1)}, bf16[512,1024]{1,0:T(8,128)(2,1)}, u32[]{:S(2)}) copy-start(bf16[512,1024]{1,0:T(8,128)(2,1)} %matrix_ref.3) | copy-start | bytes 3145732
  2.0 4.2 %collective-permute-start.9 = (bf16[384,512]{1,0:T(8,128)(2,1)S(1)}, bf16[384,512]{1,0:T(8,128)(2,1)S(1)}, u32[]{:S(2)}, u32[]{:S(2)}) collective-permute-start(bf16[384,512]{1,0:T(8,128)(2,1)S(1)} %maximum_select_fusion), channel_id=1, source_target_pairs={{0,192}} | collective-permute-start | bytes 1179656 | tf_op jit(solution)/shard_map/ppermute | solution.py:214
  2.7 3.5 %collective-permute-start.8 = (bf16[384,512]{1,0:T(8,128)(2,1)S(1)}, bf16[384,512]{1,0:T(8,128)(2,1)S(1)}, u32[]{:S(2)}, u32[]{:S(2)}) collective-permute-start(bf16[384,512]{1,0:T(8,128)(2,1)S(1)} %maximum_select_fusion), channel_id=1, source_target_pairs={{0,64}} | collective-permute-start | bytes 1179656 | tf_op jit(solution)/shard_map/ppermute | solution.py:214
  3.4 2.8 %collective-permute-start.7 = (bf16[384,512]{1,0:T(8,128)(2,1)S(1)}, bf16[384,512]{1,0:T(8,128)(2,1)S(1)}, u32[]{:S(2)}, u32[]{:S(2)}) collective-permute-start(bf16[384,512]{1,0:T(8,128)(2,1)S(1)} %maximum_select_fusion), channel_id=1, source_target_pairs={{0,128}} | collective-permute-start | bytes 1179656 | tf_op jit(solution)/shard_map/ppermute | solution.py:214
  4.2 11.1 %collective-permute-start = (bf16[256,1024]{1,0:T(8,128)(2,1)S(1)}, bf16[256,1024]{1,0:T(8,128)(2,1)S(1)}, u32[]{:S(2)}, u32[]{:S(2)}) collective-permute-start(bf16[256,1024]{1,0:T(8,128)(2,1)S(1)} %get-tuple-element.16), channel_id=1, source_target_pairs={{0,64},{1,65},{2,66},{3,67},{4,68},{5,69},{6,70},{7,71},{8,72},{9,... | collective-permute-start | bytes 1572872 | tf_op jit(solution)/shard_map/ppermute | solution.py:214
  5.5 9.8 %collective-permute-start.1 = (bf16[256,1024]{1,0:T(8,128)(2,1)S(1)}, bf16[256,1024]{1,0:T(8,128)(2,1)S(1)}, u32[]{:S(2)}, u32[]{:S(2)}) collective-permute-start(bf16[256,1024]{1,0:T(8,128)(2,1)S(1)} %get-tuple-element.15), channel_id=1, source_target_pairs={{0,192},{1,193},{2,194},{3,195},{4,196},{5,197},{6,198},{7,199},{8... | collective-permute-start | bytes 1572872 | tf_op jit(solution)/shard_map/ppermute | solution.py:214
  6.3 10.5 %copy-start.1 = (f32[8,64]{1,0:T(8,128)S(1)}, f32[8,64]{1,0:T(8,128)}, u32[]{:S(2)}) copy-start(f32[8,64]{1,0:T(8,128)} %scales_ref.3) | copy-start | bytes 6148
  6.3 10.5 %collective-permute-start.10 = (bf16[384,512]{1,0:T(8,128)(2,1)S(1)}, bf16[384,512]{1,0:T(8,128)(2,1)S(1)}, u32[]{:S(2)}, u32[]{:S(2)}) collective-permute-start(bf16[384,512]{1,0:T(8,128)(2,1)S(1)} %add_add_fusion.low_ref), channel_id=1, source_target_pairs={{0,32},{64,96},{128,160},{192,224}} | collective-permute-start | bytes 1179656 | tf_op jit(solution)/shard_map/ppermute | solution.py:214
  7.0 13.9 %collective-permute-start.3 = (bf16[256,1024]{1,0:T(8,128)(2,1)S(1)}, bf16[256,1024]{1,0:T(8,128)(2,1)S(1)}, u32[]{:S(2)}, u32[]{:S(2)}) collective-permute-start(bf16[256,1024]{1,0:T(8,128)(2,1)S(1)} %get-tuple-element.16), channel_id=1, source_target_pairs={{0,224},{1,225},{2,226},{3,227},{4,228},{5,229},{6,230},{7,231},{8... | collective-permute-start | bytes 1572872 | tf_op jit(solution)/shard_map/ppermute | solution.py:214
  7.7 13.9 %collective-permute-start.2 = (bf16[256,1024]{1,0:T(8,128)(2,1)S(1)}, bf16[256,1024]{1,0:T(8,128)(2,1)S(1)}, u32[]{:S(2)}, u32[]{:S(2)}) collective-permute-start(bf16[256,1024]{1,0:T(8,128)(2,1)S(1)} %get-tuple-element.15), channel_id=1, source_target_pairs={{0,96},{1,97},{2,98},{3,99},{4,100},{5,101},{6,102},{7,103},{8,104... | collective-permute-start | bytes 1572872 | tf_op jit(solution)/shard_map/ppermute | solution.py:214
  15.5 8.0 %collective-permute-start.4 = (bf16[256,1024]{1,0:T(8,128)(2,1)S(1)}, bf16[256,1024]{1,0:T(8,128)(2,1)S(1)}, u32[]{:S(2)}, u32[]{:S(2)}) collective-permute-start(bf16[256,1024]{1,0:T(8,128)(2,1)S(1)} %add.42), channel_id=1, source_target_pairs={{64,128},{65,129},{66,130},{67,131},{68,132},{69,133},{70,134},{71... | collective-permute-start | bytes 1572872 | tf_op jit(solution)/shard_map/ppermute | solution.py:214
  17.5 1.4 %collective-permute-start.13 = (bf16[128,512]{1,0:T(8,128)(2,1)S(1)}, bf16[128,512]{1,0:T(8,128)(2,1)S(1)}, u32[]{:S(2)}, u32[]{:S(2)}) collective-permute-start(bf16[128,512]{1,0:T(8,128)(2,1)S(1)} %get-tuple-element.12), channel_id=1, source_target_pairs={{0,24},{32,56},{64,88},{96,120},{128,152},{160,184},{192,216},{224... | collective-permute-start | bytes 393224 | tf_op jit(solution)/shard_map/ppermute | solution.py:214
  18.2 1.4 %collective-permute-start.12 = (bf16[128,512]{1,0:T(8,128)(2,1)S(1)}, bf16[128,512]{1,0:T(8,128)(2,1)S(1)}, u32[]{:S(2)}, u32[]{:S(2)}) collective-permute-start(bf16[128,512]{1,0:T(8,128)(2,1)S(1)} %get-tuple-element.11), channel_id=1, source_target_pairs={{0,8},{32,40},{64,72},{96,104},{128,136},{160,168},{192,200},{224,... | collective-permute-start | bytes 393224 | tf_op jit(solution)/shard_map/ppermute | solution.py:214
  18.9 1.4 %collective-permute-start.11 = (bf16[128,512]{1,0:T(8,128)(2,1)S(1)}, bf16[128,512]{1,0:T(8,128)(2,1)S(1)}, u32[]{:S(2)}, u32[]{:S(2)}) collective-permute-start(bf16[128,512]{1,0:T(8,128)(2,1)S(1)} %get-tuple-element.10), channel_id=1, source_target_pairs={{0,16},{32,48},{64,80},{96,112},{128,144},{160,176},{192,208},{224... | collective-permute-start | bytes 393224 | tf_op jit(solution)/shard_map/ppermute | solution.py:214
  19.5 34.8 %collective-permute-start.6 = (bf16[256,1024]{1,0:T(8,128)(2,1)S(1)}, bf16[256,1024]{1,0:T(8,128)(2,1)S(1)}, u32[]{:S(2)}, u32[]{:S(2)}) collective-permute-start(bf16[256,1024]{1,0:T(8,128)(2,1)S(1)} %get-tuple-element.15), channel_id=1, source_target_pairs={{0,32},{1,33},{2,34},{3,35},{4,36},{5,37},{6,38},{7,39},{8,40},{9,... | collective-permute-start | bytes 1572872 | tf_op jit(solution)/shard_map/ppermute | solution.py:214
  20.3 5.2 %collective-permute-start.15 = (bf16[128,512]{1,0:T(8,128)(2,1)S(1)}, bf16[128,512]{1,0:T(8,128)(2,1)S(1)}, u32[]{:S(2)}, u32[]{:S(2)}) collective-permute-start(bf16[128,512]{1,0:T(8,128)(2,1)S(1)} %add_add_fusion.3), channel_id=1, source_target_pairs={{0,5},{8,13},{16,21},{24,29},{32,37},{40,45},{48,53},{56,61},{64,6... | collective-permute-start | bytes 393224 | tf_op jit(solution)/shard_map/ppermute | solution.py:214
  21.0 4.6 %collective-permute-start.14 = (bf16[128,512]{1,0:T(8,128)(2,1)S(1)}, bf16[128,512]{1,0:T(8,128)(2,1)S(1)}, u32[]{:S(2)}, u32[]{:S(2)}) collective-permute-start(bf16[128,512]{1,0:T(8,128)(2,1)S(1)} %add_add_fusion.3), channel_id=1, source_target_pairs={{0,3},{8,11},{16,19},{24,27},{32,35},{40,43},{48,51},{56,59},{64,6... | collective-permute-start | bytes 393224 | tf_op jit(solution)/shard_map/ppermute | solution.py:214
  23.6 36.9 %collective-permute-start.5 = (bf16[256,1024]{1,0:T(8,128)(2,1)S(1)}, bf16[256,1024]{1,0:T(8,128)(2,1)S(1)}, u32[]{:S(2)}, u32[]{:S(2)}) collective-permute-start(bf16[256,1024]{1,0:T(8,128)(2,1)S(1)} %add_select_fusion.mine_ref), channel_id=1, source_target_pairs={{0,32},{1,33},{2,34},{3,35},{4,36},{5,37},{6,38},{7,39},{8,40},{9,... | collective-permute-start | bytes 1572872 | tf_op jit(solution)/shard_map/ppermute | solution.py:214
  25.6 2.0 %collective-permute-start.17 = (bf16[128,512]{1,0:T(8,128)(2,1)S(1)}, bf16[128,512]{1,0:T(8,128)(2,1)S(1)}, u32[]{:S(2)}, u32[]{:S(2)}) collective-permute-start(bf16[128,512]{1,0:T(8,128)(2,1)S(1)} %add_add_fusion.2), channel_id=1, source_target_pairs={{0,7},{8,15},{16,23},{24,31},{32,39},{40,47},{48,55},{56,63},{64,7... | collective-permute-start | bytes 393224 | tf_op jit(solution)/shard_map/ppermute | solution.py:214
  26.3 23.2 %collective-permute-start.16 = (bf16[128,512]{1,0:T(8,128)(2,1)S(1)}, bf16[128,512]{1,0:T(8,128)(2,1)S(1)}, u32[]{:S(2)}, u32[]{:S(2)}) collective-permute-start(bf16[128,512]{1,0:T(8,128)(2,1)S(1)} %add_add_fusion.2), channel_id=1, source_target_pairs={{0,1},{8,9},{16,17},{24,25},{32,33},{40,41},{48,49},{56,57},{64,65... | collective-permute-start | bytes 393224 | tf_op jit(solution)/shard_map/ppermute | solution.py:214
  49.5 5.9 %collective-permute-start.18 = (bf16[128,512]{1,0:T(8,128)(2,1)S(1)}, bf16[128,512]{1,0:T(8,128)(2,1)S(1)}, u32[]{:S(2)}, u32[]{:S(2)}) collective-permute-start(bf16[128,512]{1,0:T(8,128)(2,1)S(1)} %add_add_fusion.1.q0_ref), channel_id=1, source_target_pairs={{0,8},{1,9},{2,10},{3,11},{4,12},{5,13},{6,14},{7,15},{32,40},{33,... | collective-permute-start | bytes 393224 | tf_op jit(solution)/shard_map/ppermute | solution.py:214
  52.8 7.7 %collective-permute-start.19 = (bf16[128,512]{1,0:T(8,128)(2,1)S(1)}, bf16[128,512]{1,0:T(8,128)(2,1)S(1)}, u32[]{:S(2)}, u32[]{:S(2)}) collective-permute-start(bf16[128,512]{1,0:T(8,128)(2,1)S(1)} %add_add_fusion.1.q0_ref), channel_id=1, source_target_pairs={{0,24},{1,25},{2,26},{3,27},{4,28},{5,29},{6,30},{7,31},{32,56},{3... | collective-permute-start | bytes 393224 | tf_op jit(solution)/shard_map/ppermute | solution.py:214
  52.8 7.7 %collective-permute-start.20 = (bf16[128,512]{1,0:T(8,128)(2,1)S(1)}, bf16[128,512]{1,0:T(8,128)(2,1)S(1)}, u32[]{:S(2)}, u32[]{:S(2)}) collective-permute-start(bf16[128,512]{1,0:T(8,128)(2,1)S(1)} %add_add_fusion.1.q0_ref), channel_id=1, source_target_pairs={{0,16},{1,17},{2,18},{3,19},{4,20},{5,21},{6,22},{7,23},{32,48},{3... | collective-permute-start | bytes 393224 | tf_op jit(solution)/shard_map/ppermute | solution.py:214

commit v2 on v1

v2 whole, which is shorter than its diff:
```python
import functools

import jax
import jax.numpy as jnp
from jax import lax
from jax.experimental import pallas as pl
from jax.experimental.pallas import tpu as pltpu
from jax.sharding import PartitionSpec as P

NB = 512
BASE = 128
XS = 4
ZS = 8
TILE_COLS = XS * ZS
SOLVE_FLOPS = 0
BF = jnp.bfloat16
F32 = jnp.float32


def bdot(a, b):
    return jnp.dot(a, b, preferred_element_type=F32)


def split3(x):
    high = x.astype(BF)
    rest = x - high.astype(F32)
    mid = rest.astype(BF)
    low = (rest - mid.astype(F32)).astype(BF)
    return high, mid, low


def dot_exact_left(t, x):
    high, mid, low = split3(x)
    return bdot(t, high) + (bdot(t, mid) + bdot(t, low))


def dot_full(a, b):
    ah, am, al = split3(a)
    bh, bm, bl = split3(b)
    return bdot(ah, bh) + (
        (bdot(ah, bm) + bdot(am, bh)) + (bdot(am, bm) + (bdot(ah, bl) + bdot(al, bh)))
    )


def invert_diagonal(tiles, s):
    n = BASE
    r = lax.broadcasted_iota(jnp.int32, (n, n), 0)
    c = lax.broadcasted_iota(jnp.int32, (n, n), 1)
    eye = (r == c).astype(F32)

    def mask(k):
        return ((r // (2 * k)) == (c // (2 * k))) & ((r // k) % 2 == 1) & ((c // k) % 2 == 0)

    first = mask(1)
    inverses = [eye - jnp.where(first, t.astype(F32) * s, 0.0) for t in tiles]
    k = 2
    while k < n:
        at = mask(k)
        inner = [
            dot_exact_left(jnp.where(at, t, jnp.zeros_like(t)), x) * s
            for t, x in zip(tiles, inverses)
        ]
        inverses = [x - dot_full(x, y) for x, y in zip(inverses, inner)]
        k *= 2
    return inverses


def pack_kernel(matrix_ref, out_ref, sems):
    here = (lax.axis_index("prow") == 0) & (lax.axis_index("pcol") == 0)

    @pl.when(jnp.logical_not(here))
    def _():
        out_ref[...] = jnp.zeros_like(out_ref)

    @pl.when(here)
    def _():
        pieces = [(384, 0, 128, 512, 0, 0), (256, 0, 128, 384, 128, 0), (0, 0, 128, 128, 128, 384)]
        pieces += [
            (128 + 64 * i, 128 * j, 64, 128, 256, 256 * j + 128 * i)
            for j in range(2)
            for i in range(2)
        ]
        copies = [
            pltpu.make_async_copy(
                matrix_ref.at[r : r + h, c : c + w], out_ref.at[to_r : to_r + h, to_c : to_c + w], sems.at[at]
            )
            for at, (r, c, h, w, to_r, to_c) in enumerate(pieces)
        ]
        for copy in copies:
            copy.start()
        for copy in copies:
            copy.wait()


def pack(matrix):
    return pl.pallas_call(
        pack_kernel,
        out_shape=pltpu.VMEM((320, NB), BF),
        in_specs=[pl.BlockSpec(memory_space=pl.ANY)],
        out_specs=pl.BlockSpec(memory_space=pltpu.VMEM),
        scratch_shapes=[pltpu.SemaphoreType.DMA((7,))],
        cost_estimate=pl.CostEstimate(flops=0, bytes_accessed=2**19, transcendentals=0),
    )(matrix)


def solve_kernel(
    scales_ref, low_ref, swap_ref, own_ref, w0_ref, w1_ref, w2_ref, w3_ref, inv_ref
):
    outs = (w0_ref, w1_ref, w2_ref, w3_ref)
    holder = lax.axis_index("pcol") == 0
    prow_at = lax.axis_index("prow")

    @pl.when(jnp.logical_not(holder))
    def _():
        for ref in outs:
            ref[...] = jnp.zeros_like(ref)

    @pl.when(holder)
    def _():
        s = scales_ref[0, 0]
        packed = low_ref[...] + swap_ref[...]
        t = [[None] * 4 for _ in range(4)]
        for j in range(4):
            t[3][j] = packed[:128, 128 * j : 128 * (j + 1)]
        for j in range(3):
            t[2][j] = packed[128:256, 128 * j : 128 * (j + 1)]
        t[0][0] = packed[128:256, 384:]
        for j in range(2):
            t[1][j] = jnp.concatenate(
                [packed[256:, 256 * j : 256 * j + 128], packed[256:, 256 * j + 128 : 256 * (j + 1)]], 0
            )
        x = invert_diagonal([t[i][i] for i in range(4)], s)
        halves = []
        for h in (0, 2):
            off = -dot_full(x[h + 1], dot_exact_left(t[h + 1][h], x[h]) * s)
            top = jnp.concatenate([x[h], jnp.zeros_like(x[h])], 1)
            halves.append(jnp.concatenate([top, jnp.concatenate([off, x[h + 1]], 1)], 0))
        corner = jnp.concatenate(
            [jnp.concatenate([t[2][0], t[2][1]], 1), jnp.concatenate([t[3][0], t[3][1]], 1)], 0
        )
        off = -dot_full(halves[1], dot_exact_left(corner, halves[0]) * s)
        inv_ref[:256, :256] = halves[0]
        inv_ref[:256, 256:] = jnp.zeros_like(off)
        inv_ref[256:, :256] = off
        inv_ref[256:, 256:] = halves[1]
        inverse = inv_ref[...]
        high = inverse.astype(BF)
        low = (inverse - high.astype(F32)).astype(BF)
        for i, ref in enumerate(outs):
            a = own_ref[128 * i : 128 * (i + 1), :NB]
            w = (bdot(a, high) + bdot(a, low)).astype(BF)
            ref[...] = jnp.where(prow_at == 0, high[128 * i : 128 * (i + 1)], w)


def solve(scales, low, swap, own):
    chunk = jax.ShapeDtypeStruct((128, NB), BF)
    vmem = pl.BlockSpec(memory_space=pltpu.VMEM)
    return pl.pallas_call(
        solve_kernel,
        out_shape=[chunk] * 4,
        in_specs=[pl.BlockSpec(memory_space=pltpu.SMEM)] + [vmem] * 3,
        out_specs=[vmem] * 4,
        scratch_shapes=[pltpu.VMEM((NB, NB), F32)],
        compiler_params=pltpu.CompilerParams(vmem_limit_bytes=12 * 2**20),
        cost_estimate=pl.CostEstimate(flops=SOLVE_FLOPS, bytes_accessed=0, transcendentals=0),
    )(scales, low, swap, own)


def update_kernel(
    scales_ref, own_ref, held_ref, far_ref, swap_ref, q0_ref, q1_ref, q3_ref, q2_ref, out_ref,
    w_ref, result_ref, sems,
):
    prow_at = lax.axis_index("prow")
    pcol_at = lax.axis_index("pcol")
    for ref, shift in ((q0_ref, 0), (q1_ref, 3), (q3_ref, 1), (q2_ref, 2)):
        row = pl.multiple_of(lax.rem(pcol_at // ZS + shift, XS) * 128, 128)
        w_ref[pl.ds(row, 128), :] = ref[...]
    copies = [
        pltpu.make_async_copy(
            result_ref.at[:, 256 * t : 256 * (t + 1)], out_ref.at[:, 256 * t : 256 * (t + 1)], sems.at[t]
        )
        for t in range(4)
    ]

    def run(head_ref):
        for t in range(4):
            cols = slice(256 * t, 256 * (t + 1))
            col = TILE_COLS * (t // 2) + pcol_at
            scale = jnp.full((1, 256), scales_ref[prow_at, col], F32)
            factor = (scales_ref[prow_at, 0] * scales_ref[0, col]) / scale
            product = bdot(w_ref[...], head_ref[:, cols])
            own = own_ref[:, cols]
            updated = (own.astype(F32) - factor * product).astype(BF)
            result = jnp.where(prow_at == 0, product.astype(BF), updated)
            if t < 2:
                result = jnp.where(pcol_at == 0, own, result)
            result_ref[:, cols] = result
            copies[t].start()

    cases = (
        ((prow_at == 0) | (prow_at == 2) | (prow_at == 6), held_ref),
        ((prow_at == 4) | (prow_at == 5), far_ref),
        ((prow_at == 1) | (prow_at == 3) | (prow_at == 7), swap_ref),
    )
    for here, head_ref in cases:
        pl.when(here)(functools.partial(run, head_ref))
    for copy in copies:
        copy.wait()


def update(scales, own, heads, chunks):
    vmem = pl.BlockSpec(memory_space=pltpu.VMEM)
    return pl.pallas_call(
        update_kernel,
        out_shape=jax.ShapeDtypeStruct((NB, 2 * NB), BF),
        in_specs=[pl.BlockSpec(memory_space=pltpu.SMEM)] + [vmem] * 8,
        out_specs=pl.BlockSpec(memory_space=pl.ANY),
        scratch_shapes=[
            pltpu.VMEM((NB, NB), BF),
            pltpu.VMEM((NB, 2 * NB), BF),
            pltpu.SemaphoreType.DMA((4,)),
        ],
        compiler_params=pltpu.CompilerParams(vmem_limit_bytes=8 * 2**20),
        cost_estimate=pl.CostEstimate(flops=2**29, bytes_accessed=4 * 2**20, transcendentals=0),
    )(scales, own, *heads, *chunks)


def send(value, pairs):
    flat = [
        tuple(p * XS * ZS + x * ZS + z for p, x, z in (source, target)) for source, target in pairs
    ]
    return lax.ppermute(value, ("prow", "pcol"), flat)


def along_prow(value, pairs, columns):
    return send(value, [((a, x, z), (b, x, z)) for a, b in pairs for x, z in columns])


def along_x(value, pairs, depths):
    return send(
        value, [((p, a, z), (p, b, z)) for a, b in pairs for p in range(8) for z in depths]
    )


def along_z(value, pairs):
    return send(
        value, [((p, x, a), (p, x, b)) for a, b in pairs for p in range(8) for x in range(XS)]
    )


def on_device(matrix, scales):
    everywhere = [(x, z) for x in range(XS) for z in range(ZS)]
    corner = [(0, 0)]
    prow_at = lax.axis_index("prow")
    low = pack(matrix)
    low_y = [along_prow(low, [(0, p)], corner) for p in (4, 2, 6)]
    own, *low_y = lax.optimization_barrier((matrix, *low_y))
    low = low + low_y[0] + low_y[1] + low_y[2]
    low_swap = along_prow(low, [(p, p ^ 1) for p in range(8)], corner)
    low = jnp.where(prow_at % 2 == 0, low, 0).astype(BF)
    y2 = along_prow(own, [(0, 2)], everywhere)
    y6 = along_prow(own, [(0, 6)], everywhere)

    w = solve(scales, low, low_swap, matrix)
    w_x = [along_x(w[k], [(0, k)], [0]) for k in (2, 1, 3)]
    q = w[0] + w_x[0] + w_x[1] + w_x[2]
    q3, q5 = along_z(q, [(0, 3)]), along_z(q, [(0, 5)])
    q = q + q3 + q5
    q, y2, y6 = lax.optimization_barrier((q, y2, y6))
    held = jnp.where(prow_at == 0, matrix, y2 + y6)
    far = along_prow(held, [(2, 4), (6, 5)], everywhere)
    swap = along_prow(held, [(0, 1), (2, 3), (6, 7)], everywhere)
    up_z, down_z = along_z(q, [(0, 1), (3, 4), (5, 6)]), along_z(q, [(0, 7), (3, 2)])
    q = q + up_z + down_z
    q2 = along_x(q, [(a, (a + 2) % XS) for a in range(XS)], range(ZS))
    q1 = along_x(q, [(a, (a + 1) % XS) for a in range(XS)], range(ZS))
    q3 = along_x(q, [(a, (a + 3) % XS) for a in range(XS)], range(ZS))
    return update(scales, matrix, (held, far, swap), (q, q1, q3, q2))


def solution(mesh):
    placed = (P("prow", "pcol"), P())
    return jax.shard_map(
        on_device, mesh=mesh, in_specs=placed, out_specs=P("prow", "pcol"), check_vma=False
    )
```

time: 64.2 us -> 61.9 us (0.964)
  the two profiles are of different devices: /device:TPU:42 before, /device:TPU:72 now
where the time goes in v2:
time: 61.9 us; the launch traced here: 61.5 us
  waiting for transfers between devices  39.7 us (64%)
  starting transfers between devices  18.1 us (29%)
  Pallas kernels  3.05 us (5%)
    ppermute x18, waiting for transfers between devices, send(): return lax.ppermute(value, ('prow', 'pcol'), flat)  39.7 us
    ppermute x18, starting transfers between devices, send(): return lax.ppermute(value, ('prow', 'pcol'), flat)  18.1 us
    pallas_call x1, Pallas kernels, update(): pl.pallas_call(update_kernel, out_shape=jax.ShapeDtypeStruct((NB, 2 * NB)...  2.31 us
  transfers between devices with their start and end apart: 18, of which 5 were waited for; matrix products, arithmetic and copies ran while one was open for 0% of the time, Pallas kernels for 1%

profile of v2, /device:TPU:72, one launch (start us, length us, event | category | flops | bytes accessed | tf_op | source)
XLA Modules:
  0.0 61.5 jit_solution(4167708189539972557)
XLA Ops:
  0.0 0.1 shard_map.28
  0.1 0.0 copy-start
  0.1 0.8 %collective-permute-start.2 = (bf16[320,512]{1,0:T(8,128)(2,1)S(1)}, bf16[320,512]{1,0:T(8,128)(2,1)S(1)}, u32[]{:S(2)}, u32[]{:S(2)}) collective-permute-start(bf16[320,512]{1,0:T(8,128)(2,1)S(1)} %shard_map.28), channel_id=1, source_target_pairs={{0,192}} | collective-permute-start | bytes 983048 | tf_op jit(solution)/shard_map/ppermute | solution.py:232
  0.9 0.7 %collective-permute-start.1 = (bf16[320,512]{1,0:T(8,128)(2,1)S(1)}, bf16[320,512]{1,0:T(8,128)(2,1)S(1)}, u32[]{:S(2)}, u32[]{:S(2)}) collective-permute-start(bf16[320,512]{1,0:T(8,128)(2,1)S(1)} %shard_map.28), channel_id=1, source_target_pairs={{0,64}} | collective-permute-start | bytes 983048 | tf_op jit(solution)/shard_map/ppermute | solution.py:232
  1.6 0.7 %collective-permute-start = (bf16[320,512]{1,0:T(8,128)(2,1)S(1)}, bf16[320,512]{1,0:T(8,128)(2,1)S(1)}, u32[]{:S(2)}, u32[]{:S(2)}) collective-permute-start(bf16[320,512]{1,0:T(8,128)(2,1)S(1)} %shard_map.28), channel_id=1, source_target_pairs={{0,128}} | collective-permute-start | bytes 983048 | tf_op jit(solution)/shard_map/ppermute | solution.py:232
  2.3 0.0 collective-permute-done.2
  2.3 0.0 collective-permute-done.1
  2.3 0.0 collective-permute-done
  2.3 0.0 copy-start.1
  2.4 0.1 broadcast_select_fusion
  2.4 0.7 %collective-permute-start.3 = (bf16[320,512]{1,0:T(8,128)(2,1)S(1)}, bf16[320,512]{1,0:T(8,128)(2,1)S(1)}, u32[]{:S(2)}, u32[]{:S(2)}) collective-permute-start(bf16[320,512]{1,0:T(8,128)(2,1)S(1)} %get-tuple-element.28), channel_id=1, source_target_pairs={{0,32},{32,0},{64,96},{96,64},{128,160},{160,128},{192,224},{224,1... | collective-permute-start | bytes 983048 | tf_op jit(solution)/shard_map/ppermute | solution.py:232
  3.1 0.0 copy-done
  3.1 0.7 %collective-permute-start.10 = (bf16[512,1024]{1,0:T(8,128)(2,1)S(1)}, bf16[512,1024]{1,0:T(8,128)(2,1)S(1)}, u32[]{:S(2)}, u32[]{:S(2)}) collective-permute-start(bf16[512,1024]{1,0:T(8,128)(2,1)S(1)} %copy-done), channel_id=1, source_target_pairs={{0,192},{1,193},{2,194},{3,195},{4,196},{5,197},{6,198},{7,199},{8... | collective-permute-start | bytes 3145736 | tf_op jit(solution)/shard_map/ppermute | solution.py:232
  3.9 1.3 %collective-permute-start.9 = (bf16[512,1024]{1,0:T(8,128)(2,1)S(1)}, bf16[512,1024]{1,0:T(8,128)(2,1)S(1)}, u32[]{:S(2)}, u32[]{:S(2)}) collective-permute-start(bf16[512,1024]{1,0:T(8,128)(2,1)S(1)} %copy-done), channel_id=1, source_target_pairs={{0,64},{1,65},{2,66},{3,67},{4,68},{5,69},{6,70},{7,71},{8,72},{9,... | collective-permute-start | bytes 3145736 | tf_op jit(solution)/shard_map/ppermute | solution.py:232
  5.2 0.0 collective-permute-done.3.swap_ref
  5.2 0.0 copy-done.1
  5.2 0.6 %shard_map.29 = (bf16[128,512]{1,0:T(8,128)(2,1)S(1)}, bf16[128,512]{1,0:T(8,128)(2,1)S(1)}, bf16[128,512]{1,0:T(8,128)(2,1)S(1)}, bf16[128,512]{1,0:T(8,128)(2,1)S(1)}) custom-call(f32[8,64]{1,0:T(8,128)S(1)} %copy-done.1, bf16[320,512]{1,0:T(8,128)(2,1)S(1)} %get-tuple-element.27.low_ref, bf16[320,512]{1,0:T(8,128)(2,1)S(1)} %collective-permute-done.3.swap_ref, ...), custom_call_target="tpu_custom_call" | custom-call | tf_op jit(solution)/shard_map/pallas_call | solution.py:158
  5.9 0.7 %collective-permute-start.4 = (bf16[128,512]{1,0:T(8,128)(2,1)S(1)}, bf16[128,512]{1,0:T(8,128)(2,1)S(1)}, u32[]{:S(2)}, u32[]{:S(2)}) collective-permute-start(bf16[128,512]{1,0:T(8,128)(2,1)S(1)} %get-tuple-element.20), channel_id=1, source_target_pairs={{0,16},{32,48},{64,80},{96,112},{128,144},{160,176},{192,208},{224... | collective-permute-start | bytes 393224 | tf_op jit(solution)/shard_map/ppermute | solution.py:232
  6.5 0.7 %collective-permute-start.5 = (bf16[128,512]{1,0:T(8,128)(2,1)S(1)}, bf16[128,512]{1,0:T(8,128)(2,1)S(1)}, u32[]{:S(2)}, u32[]{:S(2)}) collective-permute-start(bf16[128,512]{1,0:T(8,128)(2,1)S(1)} %get-tuple-element.21), channel_id=1, source_target_pairs={{0,8},{32,40},{64,72},{96,104},{128,136},{160,168},{192,200},{224,... | collective-permute-start | bytes 393224 | tf_op jit(solution)/shard_map/ppermute | solution.py:232
  7.2 0.7 %collective-permute-start.6 = (bf16[128,512]{1,0:T(8,128)(2,1)S(1)}, bf16[128,512]{1,0:T(8,128)(2,1)S(1)}, u32[]{:S(2)}, u32[]{:S(2)}) collective-permute-start(bf16[128,512]{1,0:T(8,128)(2,1)S(1)} %get-tuple-element.22), channel_id=1, source_target_pairs={{0,24},{32,56},{64,88},{96,120},{128,152},{160,184},{192,216},{224... | collective-permute-start | bytes 393224 | tf_op jit(solution)/shard_map/ppermute | solution.py:232
  7.9 0.0 collective-permute-done.4
  7.9 0.0 collective-permute-done.5
  7.9 0.0 collective-permute-done.6
  8.0 0.7 %collective-permute-start.8 = (bf16[128,512]{1,0:T(8,128)(2,1)S(1)}, bf16[128,512]{1,0:T(8,128)(2,1)S(1)}, u32[]{:S(2)}, u32[]{:S(2)}) collective-permute-start(bf16[128,512]{1,0:T(8,128)(2,1)S(1)} %add_add_fusion.3), channel_id=1, source_target_pairs={{0,5},{8,13},{16,21},{24,29},{32,37},{40,45},{48,53},{56,61},{64,6... | collective-permute-start | bytes 393224 | tf_op jit(solution)/shard_map/ppermute | solution.py:232
  8.6 0.7 %collective-permute-start.7 = (bf16[128,512]{1,0:T(8,128)(2,1)S(1)}, bf16[128,512]{1,0:T(8,128)(2,1)S(1)}, u32[]{:S(2)}, u32[]{:S(2)}) collective-permute-start(bf16[128,512]{1,0:T(8,128)(2,1)S(1)} %add_add_fusion.3), channel_id=1, source_target_pairs={{0,3},{8,11},{16,19},{24,27},{32,35},{40,43},{48,51},{56,59},{64,6... | collective-permute-start | bytes 393224 | tf_op jit(solution)/shard_map/ppermute | solution.py:232
  9.3 0.0 collective-permute-done.8
  9.3 0.0 collective-permute-done.7
  9.4 0.0 collective-permute-done.10
  9.4 13.3 %collective-permute-done.9 = bf16[512,1024]{1,0:T(8,128)(2,1)S(1)} collective-permute-done((bf16[512,1024]{1,0:T(8,128)(2,1)S(1)}, bf16[512,1024]{1,0:T(8,128)(2,1)S(1)}, u32[]{:S(2)}, u32[]{:S(2)}) %collective-permute-start.9) | collective-permute-done | bytes 1048608 | tf_op jit(solution)/shard_map/ppermute | solution.py:232
  22.6 0.2 add_select_fusion.held_ref
  22.8 1.4 %collective-permute-start.12 = (bf16[512,1024]{1,0:T(8,128)(2,1)S(1)}, bf16[512,1024]{1,0:T(8,128)(2,1)S(1)}, u32[]{:S(2)}, u32[]{:S(2)}) collective-permute-start(bf16[512,1024]{1,0:T(8,128)(2,1)S(1)} %add_select_fusion.held_ref), channel_id=1, source_target_pairs={{0,32},{1,33},{2,34},{3,35},{4,36},{5,37},{6,38},{7,39},{8,40},{9,... | collective-permute-start | bytes 3145736 | tf_op jit(solution)/shard_map/ppermute | solution.py:232
  24.2 1.4 %collective-permute-start.11 = (bf16[512,1024]{1,0:T(8,128)(2,1)S(1)}, bf16[512,1024]{1,0:T(8,128)(2,1)S(1)}, u32[]{:S(2)}, u32[]{:S(2)}) collective-permute-start(bf16[512,1024]{1,0:T(8,128)(2,1)S(1)} %add_select_fusion.held_ref), channel_id=1, source_target_pairs={{64,128},{65,129},{66,130},{67,131},{68,132},{69,133},{70,134},{71... | collective-permute-start | bytes 3145736 | tf_op jit(solution)/shard_map/ppermute | solution.py:232
  25.5 1.3 %collective-permute-start.14 = (bf16[128,512]{1,0:T(8,128)(2,1)S(1)}, bf16[128,512]{1,0:T(8,128)(2,1)S(1)}, u32[]{:S(2)}, u32[]{:S(2)}) collective-permute-start(bf16[128,512]{1,0:T(8,128)(2,1)S(1)} %add_add_fusion.2), channel_id=1, source_target_pairs={{0,7},{8,15},{16,23},{24,31},{32,39},{40,47},{48,55},{56,63},{64,7... | collective-permute-start | bytes 393224 | tf_op jit(solution)/shard_map/ppermute | solution.py:232
  26.8 0.7 %collective-permute-start.13 = (bf16[128,512]{1,0:T(8,128)(2,1)S(1)}, bf16[128,512]{1,0:T(8,128)(2,1)S(1)}, u32[]{:S(2)}, u32[]{:S(2)}) collective-permute-start(bf16[128,512]{1,0:T(8,128)(2,1)S(1)} %add_add_fusion.2), channel_id=1, source_target_pairs={{0,1},{8,9},{16,17},{24,25},{32,33},{40,41},{48,49},{56,57},{64,65... | collective-permute-start | bytes 393224 | tf_op jit(solution)/shard_map/ppermute | solution.py:232
  27.5 20.3 %collective-permute-done.14 = bf16[128,512]{1,0:T(8,128)(2,1)S(1)} collective-permute-done((bf16[128,512]{1,0:T(8,128)(2,1)S(1)}, bf16[128,512]{1,0:T(8,128)(2,1)S(1)}, u32[]{:S(2)}, u32[]{:S(2)}) %collective-permute-start.14) | collective-permute-done | bytes 131104 | tf_op jit(solution)/shard_map/ppermute | solution.py:232
  47.8 0.0 collective-permute-done.13
  47.8 1.3 %collective-permute-start.17 = (bf16[128,512]{1,0:T(8,128)(2,1)S(1)}, bf16[128,512]{1,0:T(8,128)(2,1)S(1)}, u32[]{:S(2)}, u32[]{:S(2)}) collective-permute-start(bf16[128,512]{1,0:T(8,128)(2,1)S(1)} %add_add_fusion.1.q0_ref), channel_id=1, source_target_pairs={{0,16},{1,17},{2,18},{3,19},{4,20},{5,21},{6,22},{7,23},{32,48},{3... | collective-permute-start | bytes 393224 | tf_op jit(solution)/shard_map/ppermute | solution.py:232
  49.1 4.0 %collective-permute-start.16 = (bf16[128,512]{1,0:T(8,128)(2,1)S(1)}, bf16[128,512]{1,0:T(8,128)(2,1)S(1)}, u32[]{:S(2)}, u32[]{:S(2)}) collective-permute-start(bf16[128,512]{1,0:T(8,128)(2,1)S(1)} %add_add_fusion.1.q0_ref), channel_id=1, source_target_pairs={{0,24},{1,25},{2,26},{3,27},{4,28},{5,29},{6,30},{7,31},{32,56},{3... | collective-permute-start | bytes 393224 | tf_op jit(solution)/shard_map/ppermute | solution.py:232
  53.0 0.0 collective-permute-start.15
  53.0 1.3 %collective-permute-done.17.q2_ref = bf16[128,512]{1,0:T(8,128)(2,1)S(1)} collective-permute-done((bf16[128,512]{1,0:T(8,128)(2,1)S(1)}, bf16[128,512]{1,0:T(8,128)(2,1)S(1)}, u32[]{:S(2)}, u32[]{:S(2)}) %collective-permute-start.17) | collective-permute-done | bytes 131104 | tf_op jit(solution)/shard_map/ppermute | solution.py:232
  54.4 2.2 %collective-permute-done.16.q3_ref = bf16[128,512]{1,0:T(8,128)(2,1)S(1)} collective-permute-done((bf16[128,512]{1,0:T(8,128)(2,1)S(1)}, bf16[128,512]{1,0:T(8,128)(2,1)S(1)}, u32[]{:S(2)}, u32[]{:S(2)}) %collective-permute-start.16) | collective-permute-done | bytes 131104 | tf_op jit(solution)/shard_map/ppermute | solution.py:232
  56.6 2.6 %collective-permute-done.15.q1_ref = bf16[128,512]{1,0:T(8,128)(2,1)S(1)} collective-permute-done((bf16[128,512]{1,0:T(8,128)(2,1)S(1)}, bf16[128,512]{1,0:T(8,128)(2,1)S(1)}, u32[]{:S(2)}, u32[]{:S(2)}) %collective-permute-start.15) | collective-permute-done | bytes 131104 | tf_op jit(solution)/shard_map/ppermute | solution.py:232
  59.2 0.0 collective-permute-done.12.swap_ref
  59.2 0.0 collective-permute-done.11.far_ref
  59.2 2.3 %shard_map.30 = bf16[512,1024]{1,0:T(8,128)(2,1)} custom-call(f32[8,64]{1,0:T(8,128)S(1)} %copy-done.1, bf16[512,1024]{1,0:T(8,128)(2,1)S(1)} %copy-done, bf16[512,1024]{1,0:T(8,128)(2,1)S(1)} %add_select_fusion.held_ref, bf16[512,1024]{1,0:T(8,128)(2,1)S(1)} %collective-permute-done.11.far_ref, bf16[512,1024]{1,0:T(8,128)(2,1)S(1)} %collective-permute-done.12.swap_ref, ...), custom_call_target="tpu_custom_call" | custom-call | flops 536870912 | bytes 4194304 | tf_op jit(solution)/shard_map/pallas_call | solution.py:213
  (3 shorter events, 0.1 us)
Async XLA Ops:
  0.1 3.0 %copy-start = (bf16[512,1024]{1,0:T(8,128)(2,1)S(1)}, bf16[512,1024]{1,0:T(8,128)(2,1)}, u32[]{:S(2)}) copy-start(bf16[512,1024]{1,0:T(8,128)(2,1)} %own_ref.3) | copy-start | bytes 3145732
  0.1 2.2 %collective-permute-start.2 = (bf16[320,512]{1,0:T(8,128)(2,1)S(1)}, bf16[320,512]{1,0:T(8,128)(2,1)S(1)}, u32[]{:S(2)}, u32[]{:S(2)}) collective-permute-start(bf16[320,512]{1,0:T(8,128)(2,1)S(1)} %shard_map.28), channel_id=1, source_target_pairs={{0,192}} | collective-permute-start | bytes 983048 | tf_op jit(solution)/shard_map/ppermute | solution.py:232
  0.9 1.4 %collective-permute-start.1 = (bf16[320,512]{1,0:T(8,128)(2,1)S(1)}, bf16[320,512]{1,0:T(8,128)(2,1)S(1)}, u32[]{:S(2)}, u32[]{:S(2)}) collective-permute-start(bf16[320,512]{1,0:T(8,128)(2,1)S(1)} %shard_map.28), channel_id=1, source_target_pairs={{0,64}} | collective-permute-start | bytes 983048 | tf_op jit(solution)/shard_map/ppermute | solution.py:232
  1.6 0.7 %collective-permute-start = (bf16[320,512]{1,0:T(8,128)(2,1)S(1)}, bf16[320,512]{1,0:T(8,128)(2,1)S(1)}, u32[]{:S(2)}, u32[]{:S(2)}) collective-permute-start(bf16[320,512]{1,0:T(8,128)(2,1)S(1)} %shard_map.28), channel_id=1, source_target_pairs={{0,128}} | collective-permute-start | bytes 983048 | tf_op jit(solution)/shard_map/ppermute | solution.py:232
  2.3 2.8 %copy-start.1 = (f32[8,64]{1,0:T(8,128)S(1)}, f32[8,64]{1,0:T(8,128)}, u32[]{:S(2)}) copy-start(f32[8,64]{1,0:T(8,128)} %scales_ref.3) | copy-start | bytes 6148
  2.4 2.7 %collective-permute-start.3 = (bf16[320,512]{1,0:T(8,128)(2,1)S(1)}, bf16[320,512]{1,0:T(8,128)(2,1)S(1)}, u32[]{:S(2)}, u32[]{:S(2)}) collective-permute-start(bf16[320,512]{1,0:T(8,128)(2,1)S(1)} %get-tuple-element.28), channel_id=1, source_target_pairs={{0,32},{32,0},{64,96},{96,64},{128,160},{160,128},{192,224},{224,1... | collective-permute-start | bytes 983048 | tf_op jit(solution)/shard_map/ppermute | solution.py:232
  3.1 6.2 %collective-permute-start.10 = (bf16[512,1024]{1,0:T(8,128)(2,1)S(1)}, bf16[512,1024]{1,0:T(8,128)(2,1)S(1)}, u32[]{:S(2)}, u32[]{:S(2)}) collective-permute-start(bf16[512,1024]{1,0:T(8,128)(2,1)S(1)} %copy-done), channel_id=1, source_target_pairs={{0,192},{1,193},{2,194},{3,195},{4,196},{5,197},{6,198},{7,199},{8... | collective-permute-start | bytes 3145736 | tf_op jit(solution)/shard_map/ppermute | solution.py:232
  3.9 18.8 %collective-permute-start.9 = (bf16[512,1024]{1,0:T(8,128)(2,1)S(1)}, bf16[512,1024]{1,0:T(8,128)(2,1)S(1)}, u32[]{:S(2)}, u32[]{:S(2)}) collective-permute-start(bf16[512,1024]{1,0:T(8,128)(2,1)S(1)} %copy-done), channel_id=1, source_target_pairs={{0,64},{1,65},{2,66},{3,67},{4,68},{5,69},{6,70},{7,71},{8,72},{9,... | collective-permute-start | bytes 3145736 | tf_op jit(solution)/shard_map/ppermute | solution.py:232
  5.9 2.0 %collective-permute-start.4 = (bf16[128,512]{1,0:T(8,128)(2,1)S(1)}, bf16[128,512]{1,0:T(8,128)(2,1)S(1)}, u32[]{:S(2)}, u32[]{:S(2)}) collective-permute-start(bf16[128,512]{1,0:T(8,128)(2,1)S(1)} %get-tuple-element.20), channel_id=1, source_target_pairs={{0,16},{32,48},{64,80},{96,112},{128,144},{160,176},{192,208},{224... | collective-permute-start | bytes 393224 | tf_op jit(solution)/shard_map/ppermute | solution.py:232
  6.5 1.4 %collective-permute-start.5 = (bf16[128,512]{1,0:T(8,128)(2,1)S(1)}, bf16[128,512]{1,0:T(8,128)(2,1)S(1)}, u32[]{:S(2)}, u32[]{:S(2)}) collective-permute-start(bf16[128,512]{1,0:T(8,128)(2,1)S(1)} %get-tuple-element.21), channel_id=1, source_target_pairs={{0,8},{32,40},{64,72},{96,104},{128,136},{160,168},{192,200},{224,... | collective-permute-start | bytes 393224 | tf_op jit(solution)/shard_map/ppermute | solution.py:232
  7.2 0.7 %collective-permute-start.6 = (bf16[128,512]{1,0:T(8,128)(2,1)S(1)}, bf16[128,512]{1,0:T(8,128)(2,1)S(1)}, u32[]{:S(2)}, u32[]{:S(2)}) collective-permute-start(bf16[128,512]{1,0:T(8,128)(2,1)S(1)} %get-tuple-element.22), channel_id=1, source_target_pairs={{0,24},{32,56},{64,88},{96,120},{128,152},{160,184},{192,216},{224... | collective-permute-start | bytes 393224 | tf_op jit(solution)/shard_map/ppermute | solution.py:232
  8.0 1.4 %collective-permute-start.8 = (bf16[128,512]{1,0:T(8,128)(2,1)S(1)}, bf16[128,512]{1,0:T(8,128)(2,1)S(1)}, u32[]{:S(2)}, u32[]{:S(2)}) collective-permute-start(bf16[128,512]{1,0:T(8,128)(2,1)S(1)} %add_add_fusion.3), channel_id=1, source_target_pairs={{0,5},{8,13},{16,21},{24,29},{32,37},{40,45},{48,53},{56,61},{64,6... | collective-permute-start | bytes 393224 | tf_op jit(solution)/shard_map/ppermute | solution.py:232
  8.6 0.7 %collective-permute-start.7 = (bf16[128,512]{1,0:T(8,128)(2,1)S(1)}, bf16[128,512]{1,0:T(8,128)(2,1)S(1)}, u32[]{:S(2)}, u32[]{:S(2)}) collective-permute-start(bf16[128,512]{1,0:T(8,128)(2,1)S(1)} %add_add_fusion.3), channel_id=1, source_target_pairs={{0,3},{8,11},{16,19},{24,27},{32,35},{40,43},{48,51},{56,59},{64,6... | collective-permute-start | bytes 393224 | tf_op jit(solution)/shard_map/ppermute | solution.py:232
  22.8 36.4 %collective-permute-start.12 = (bf16[512,1024]{1,0:T(8,128)(2,1)S(1)}, bf16[512,1024]{1,0:T(8,128)(2,1)S(1)}, u32[]{:S(2)}, u32[]{:S(2)}) collective-permute-start(bf16[512,1024]{1,0:T(8,128)(2,1)S(1)} %add_select_fusion.held_ref), channel_id=1, source_target_pairs={{0,32},{1,33},{2,34},{3,35},{4,36},{5,37},{6,38},{7,39},{8,40},{9,... | collective-permute-start | bytes 3145736 | tf_op jit(solution)/shard_map/ppermute | solution.py:232
  24.2 35.1 %collective-permute-start.11 = (bf16[512,1024]{1,0:T(8,128)(2,1)S(1)}, bf16[512,1024]{1,0:T(8,128)(2,1)S(1)}, u32[]{:S(2)}, u32[]{:S(2)}) collective-permute-start(bf16[512,1024]{1,0:T(8,128)(2,1)S(1)} %add_select_fusion.held_ref), channel_id=1, source_target_pairs={{64,128},{65,129},{66,130},{67,131},{68,132},{69,133},{70,134},{71... | collective-permute-start | bytes 3145736 | tf_op jit(solution)/shard_map/ppermute | solution.py:232
  25.5 22.3 %collective-permute-start.14 = (bf16[128,512]{1,0:T(8,128)(2,1)S(1)}, bf16[128,512]{1,0:T(8,128)(2,1)S(1)}, u32[]{:S(2)}, u32[]{:S(2)}) collective-permute-start(bf16[128,512]{1,0:T(8,128)(2,1)S(1)} %add_add_fusion.2), channel_id=1, source_target_pairs={{0,7},{8,15},{16,23},{24,31},{32,39},{40,47},{48,55},{56,63},{64,7... | collective-permute-start | bytes 393224 | tf_op jit(solution)/shard_map/ppermute | solution.py:232
  26.8 21.0 %collective-permute-start.13 = (bf16[128,512]{1,0:T(8,128)(2,1)S(1)}, bf16[128,512]{1,0:T(8,128)(2,1)S(1)}, u32[]{:S(2)}, u32[]{:S(2)}) collective-permute-start(bf16[128,512]{1,0:T(8,128)(2,1)S(1)} %add_add_fusion.2), channel_id=1, source_target_pairs={{0,1},{8,9},{16,17},{24,25},{32,33},{40,41},{48,49},{56,57},{64,65... | collective-permute-start | bytes 393224 | tf_op jit(solution)/shard_map/ppermute | solution.py:232
  47.8 6.6 %collective-permute-start.17 = (bf16[128,512]{1,0:T(8,128)(2,1)S(1)}, bf16[128,512]{1,0:T(8,128)(2,1)S(1)}, u32[]{:S(2)}, u32[]{:S(2)}) collective-permute-start(bf16[128,512]{1,0:T(8,128)(2,1)S(1)} %add_add_fusion.1.q0_ref), channel_id=1, source_target_pairs={{0,16},{1,17},{2,18},{3,19},{4,20},{5,21},{6,22},{7,23},{32,48},{3... | collective-permute-start | bytes 393224 | tf_op jit(solution)/shard_map/ppermute | solution.py:232
  49.1 7.5 %collective-permute-start.16 = (bf16[128,512]{1,0:T(8,128)(2,1)S(1)}, bf16[128,512]{1,0:T(8,128)(2,1)S(1)}, u32[]{:S(2)}, u32[]{:S(2)}) collective-permute-start(bf16[128,512]{1,0:T(8,128)(2,1)S(1)} %add_add_fusion.1.q0_ref), channel_id=1, source_target_pairs={{0,24},{1,25},{2,26},{3,27},{4,28},{5,29},{6,30},{7,31},{32,56},{3... | collective-permute-start | bytes 393224 | tf_op jit(solution)/shard_map/ppermute | solution.py:232
  53.0 6.2 %collective-permute-start.15 = (bf16[128,512]{1,0:T(8,128)(2,1)S(1)}, bf16[128,512]{1,0:T(8,128)(2,1)S(1)}, u32[]{:S(2)}, u32[]{:S(2)}) collective-permute-start(bf16[128,512]{1,0:T(8,128)(2,1)S(1)} %add_add_fusion.1.q0_ref), channel_id=1, source_target_pairs={{0,8},{1,9},{2,10},{3,11},{4,12},{5,13},{6,14},{7,15},{32,40},{33,... | collective-permute-start | bytes 393224 | tf_op jit(solution)/shard_map/ppermute | solution.py:232

commit v3 on v2

--- a/solution.py
+++ b/solution.py
@@ -166,8 +166,32 @@
     )(scales, low, swap, own)
 
 
+def merge_kernel(held_ref, far_ref, out_ref, sem):
+    del held_ref
+
+    @pl.when(lax.axis_index("prow") == 4)
+    def _():
+        copy = pltpu.make_async_copy(far_ref, out_ref, sem)
+        copy.start()
+        copy.wait()
+
+
+def merge(held, far):
+    vmem = pl.BlockSpec(memory_space=pltpu.VMEM)
+    return pl.pallas_call(
+        merge_kernel,
+        out_shape=pltpu.VMEM(held.shape, BF),
+        in_specs=[vmem, pl.BlockSpec(memory_space=pl.ANY)],
+        out_specs=vmem,
+        scratch_shapes=[pltpu.SemaphoreType.DMA],
+        input_output_aliases={0: 0},
+        compiler_params=pltpu.CompilerParams(vmem_limit_bytes=2**20),
+        cost_estimate=pl.CostEstimate(flops=0, bytes_accessed=0, transcendentals=0),
+    )(held, far)
+
+
 def update_kernel(
-    scales_ref, own_ref, held_ref, far_ref, swap_ref, q0_ref, q1_ref, q3_ref, q2_ref, out_ref,
+    scales_ref, own_ref, even_ref, odd_ref, q0_ref, q1_ref, q3_ref, q2_ref, out_ref,
     w_ref, result_ref, sems,
 ):
     prow_at = lax.axis_index("prow")
@@ -197,11 +221,8 @@
             result_ref[:, cols] = result
             copies[t].start()
 
-    cases = (
-        ((prow_at == 0) | (prow_at == 2) | (prow_at == 6), held_ref),
-        ((prow_at == 4) | (prow_at == 5), far_ref),
-        ((prow_at == 1) | (prow_at == 3) | (prow_at == 7), swap_ref),
-    )
+    even = lax.rem(prow_at, 2) == 0
+    cases = ((even, even_ref), (jnp.logical_not(even), odd_ref))
     for here, head_ref in cases:
         pl.when(here)(functools.partial(run, head_ref))
     for copy in copies:
@@ -213,7 +234,7 @@
     return pl.pallas_call(
         update_kernel,
         out_shape=jax.ShapeDtypeStruct((NB, 2 * NB), BF),
-        in_specs=[pl.BlockSpec(memory_space=pltpu.SMEM)] + [vmem] * 8,
+        in_specs=[pl.BlockSpec(memory_space=pltpu.SMEM)] + [vmem] * 7,
         out_specs=pl.BlockSpec(memory_space=pl.ANY),
         scratch_shapes=[
             pltpu.VMEM((NB, NB), BF),
@@ -260,6 +281,7 @@
     low = jnp.where(prow_at % 2 == 0, low, 0).astype(BF)
     y2 = along_prow(own, [(0, 2)], everywhere)
     y6 = along_prow(own, [(0, 6)], everywhere)
+    y4 = along_prow(own, [(0, 4)], everywhere)
 
     w = solve(scales, low, low_swap, matrix)
     w_x = [along_x(w[k], [(0, k)], [0]) for k in (2, 1, 3)]
@@ -267,15 +289,16 @@
     q3, q5 = along_z(q, [(0, 3)]), along_z(q, [(0, 5)])
     q = q + q3 + q5
     q, y2, y6 = lax.optimization_barrier((q, y2, y6))
-    held = jnp.where(prow_at == 0, matrix, y2 + y6)
-    far = along_prow(held, [(2, 4), (6, 5)], everywhere)
-    swap = along_prow(held, [(0, 1), (2, 3), (6, 7)], everywhere)
+    even = jnp.where(prow_at == 0, matrix, y2 + y6)
     up_z, down_z = along_z(q, [(0, 1), (3, 4), (5, 6)]), along_z(q, [(0, 7), (3, 2)])
     q = q + up_z + down_z
+    q, even, y4 = lax.optimization_barrier((q, even, y4))
+    even = merge(even, y4)
+    odd = along_prow(even, [(0, 1), (2, 3), (4, 5), (6, 7)], everywhere)
     q2 = along_x(q, [(a, (a + 2) % XS) for a in range(XS)], range(ZS))
     q1 = along_x(q, [(a, (a + 1) % XS) for a in range(XS)], range(ZS))
     q3 = along_x(q, [(a, (a + 3) % XS) for a in range(XS)], range(ZS))
-    return update(scales, matrix, (held, far, swap), (q, q1, q3, q2))
+    return update(scales, matrix, (even, odd), (q, q1, q3, q2))
 
 
 def solution(mesh):

time: 61.9 us -> 60 us (0.969)
  the two profiles are of different devices: /device:TPU:72 before, /device:TPU:64 now
where the time goes in v3:
time: 60 us; the launch traced here: 59.4 us
  waiting for transfers between devices  31.4 us (52%)
  starting transfers between devices  23 us (38%)
  Pallas kernels  3.06 us (5%)
  other arithmetic  1.59 us (3%)
    ppermute x18, waiting for transfers between devices, send(): return lax.ppermute(value, ('prow', 'pcol'), flat)  31.4 us
    ppermute x18, starting transfers between devices, send(): return lax.ppermute(value, ('prow', 'pcol'), flat)  23 us
    pallas_call x1, Pallas kernels, update(): pl.pallas_call(update_kernel, out_shape=jax.ShapeDtypeStruct((NB, 2 * NB)...  2.31 us
    select_n x1, other arithmetic, on_device(): even = jnp.where(prow_at == 0, matrix, y2 + y6)  1.42 us
  transfers between devices with their start and end apart: 18, of which 5 were waited for; matrix products, arithmetic and copies ran while one was open for 3% of the time, Pallas kernels for 1%

profile of v3, /device:TPU:64, one launch (start us, length us, event | category | flops | bytes accessed | tf_op | source)
XLA Modules:
  0.0 59.4 jit_solution(15886215647464263734)
XLA Ops:
  0.0 0.1 shard_map.28
  0.1 0.0 copy-start
  0.1 0.8 %collective-permute-start = (bf16[320,512]{1,0:T(8,128)(2,1)S(1)}, bf16[320,512]{1,0:T(8,128)(2,1)S(1)}, u32[]{:S(2)}, u32[]{:S(2)}) collective-permute-start(bf16[320,512]{1,0:T(8,128)(2,1)S(1)} %shard_map.28), channel_id=1, source_target_pairs={{0,128}} | collective-permute-start | bytes 983048 | tf_op jit(solution)/shard_map/ppermute | solution.py:253
  0.9 0.7 %collective-permute-start.1 = (bf16[320,512]{1,0:T(8,128)(2,1)S(1)}, bf16[320,512]{1,0:T(8,128)(2,1)S(1)}, u32[]{:S(2)}, u32[]{:S(2)}) collective-permute-start(bf16[320,512]{1,0:T(8,128)(2,1)S(1)} %shard_map.28), channel_id=1, source_target_pairs={{0,64}} | collective-permute-start | bytes 983048 | tf_op jit(solution)/shard_map/ppermute | solution.py:253
  1.6 0.7 %collective-permute-start.2 = (bf16[320,512]{1,0:T(8,128)(2,1)S(1)}, bf16[320,512]{1,0:T(8,128)(2,1)S(1)}, u32[]{:S(2)}, u32[]{:S(2)}) collective-permute-start(bf16[320,512]{1,0:T(8,128)(2,1)S(1)} %shard_map.28), channel_id=1, source_target_pairs={{0,192}} | collective-permute-start | bytes 983048 | tf_op jit(solution)/shard_map/ppermute | solution.py:253
  2.3 0.0 collective-permute-done
  2.3 0.0 collective-permute-done.1
  2.3 0.0 collective-permute-done.2
  2.3 0.0 copy-start.1
  2.4 0.1 broadcast_select_fusion
  2.5 0.7 %collective-permute-start.3 = (bf16[320,512]{1,0:T(8,128)(2,1)S(1)}, bf16[320,512]{1,0:T(8,128)(2,1)S(1)}, u32[]{:S(2)}, u32[]{:S(2)}) collective-permute-start(bf16[320,512]{1,0:T(8,128)(2,1)S(1)} %get-tuple-element.34), channel_id=1, source_target_pairs={{0,32},{32,0},{64,96},{96,64},{128,160},{160,128},{192,224},{224,1... | collective-permute-start | bytes 983048 | tf_op jit(solution)/shard_map/ppermute | solution.py:253
  3.1 0.0 copy-done
  3.2 5.0 %collective-permute-start.10 = (bf16[512,1024]{1,0:T(8,128)(2,1)S(1)}, bf16[512,1024]{1,0:T(8,128)(2,1)S(1)}, u32[]{:S(2)}, u32[]{:S(2)}) collective-permute-start(bf16[512,1024]{1,0:T(8,128)(2,1)S(1)} %copy-done), channel_id=1, source_target_pairs={{0,192},{1,193},{2,194},{3,195},{4,196},{5,197},{6,198},{7,199},{8... | collective-permute-start | bytes 3145736 | tf_op jit(solution)/shard_map/ppermute | solution.py:253
  8.2 2.3 %collective-permute-start.9 = (bf16[512,1024]{1,0:T(8,128)(2,1)S(1)}, bf16[512,1024]{1,0:T(8,128)(2,1)}, u32[]{:S(2)}, u32[]{:S(2)}) collective-permute-start(bf16[512,1024]{1,0:T(8,128)(2,1)S(1)} %copy-done), channel_id=1, source_target_pairs={{0,64},{1,65},{2,66},{3,67},{4,68},{5,69},{6,70},{7,71},{8,72},{9,... | collective-permute-start | bytes 3145736 | tf_op jit(solution)/shard_map/ppermute | solution.py:253
  10.4 0.0 collective-permute-done.3.swap_ref
  10.4 0.0 copy-done.1
  10.4 0.6 %shard_map.29 = (bf16[128,512]{1,0:T(8,128)(2,1)S(1)}, bf16[128,512]{1,0:T(8,128)(2,1)S(1)}, bf16[128,512]{1,0:T(8,128)(2,1)S(1)}, bf16[128,512]{1,0:T(8,128)(2,1)S(1)}) custom-call(f32[8,64]{1,0:T(8,128)S(1)} %copy-done.1, bf16[320,512]{1,0:T(8,128)(2,1)S(1)} %get-tuple-element.33.low_ref, bf16[320,512]{1,0:T(8,128)(2,1)S(1)} %collective-permute-done.3.swap_ref, ...), custom_call_target="tpu_custom_call" | custom-call | tf_op jit(solution)/shard_map/pallas_call | solution.py:158
  11.1 0.7 %collective-permute-start.4 = (bf16[128,512]{1,0:T(8,128)(2,1)S(1)}, bf16[128,512]{1,0:T(8,128)(2,1)S(1)}, u32[]{:S(2)}, u32[]{:S(2)}) collective-permute-start(bf16[128,512]{1,0:T(8,128)(2,1)S(1)} %get-tuple-element.23), channel_id=1, source_target_pairs={{0,16},{32,48},{64,80},{96,112},{128,144},{160,176},{192,208},{224... | collective-permute-start | bytes 393224 | tf_op jit(solution)/shard_map/ppermute | solution.py:253
  11.8 0.7 %collective-permute-start.5 = (bf16[128,512]{1,0:T(8,128)(2,1)S(1)}, bf16[128,512]{1,0:T(8,128)(2,1)S(1)}, u32[]{:S(2)}, u32[]{:S(2)}) collective-permute-start(bf16[128,512]{1,0:T(8,128)(2,1)S(1)} %get-tuple-element.24), channel_id=1, source_target_pairs={{0,8},{32,40},{64,72},{96,104},{128,136},{160,168},{192,200},{224,... | collective-permute-start | bytes 393224 | tf_op jit(solution)/shard_map/ppermute | solution.py:253
  12.5 0.7 %collective-permute-start.6 = (bf16[128,512]{1,0:T(8,128)(2,1)S(1)}, bf16[128,512]{1,0:T(8,128)(2,1)S(1)}, u32[]{:S(2)}, u32[]{:S(2)}) collective-permute-start(bf16[128,512]{1,0:T(8,128)(2,1)S(1)} %get-tuple-element.25), channel_id=1, source_target_pairs={{0,24},{32,56},{64,88},{96,120},{128,152},{160,184},{192,216},{224... | collective-permute-start | bytes 393224 | tf_op jit(solution)/shard_map/ppermute | solution.py:253
  13.1 0.0 collective-permute-done.4
  13.1 1.4 %collective-permute-start.13 = (bf16[512,1024]{1,0:T(8,128)(2,1)S(1)}, bf16[512,1024]{1,0:T(8,128)(2,1)S(1)}, u32[]{:S(2)}, u32[]{:S(2)}) collective-permute-start(bf16[512,1024]{1,0:T(8,128)(2,1)S(1)} %copy-done), channel_id=1, source_target_pairs={{0,128},{1,129},{2,130},{3,131},{4,132},{5,133},{6,134},{7,135},{8... | collective-permute-start | bytes 3145736 | tf_op jit(solution)/shard_map/ppermute | solution.py:253
  14.5 0.0 collective-permute-done.5
  14.5 0.0 collective-permute-done.6
  14.6 0.7 %collective-permute-start.7 = (bf16[128,512]{1,0:T(8,128)(2,1)S(1)}, bf16[128,512]{1,0:T(8,128)(2,1)S(1)}, u32[]{:S(2)}, u32[]{:S(2)}) collective-permute-start(bf16[128,512]{1,0:T(8,128)(2,1)S(1)} %add_add_fusion.3), channel_id=1, source_target_pairs={{0,3},{8,11},{16,19},{24,27},{32,35},{40,43},{48,51},{56,59},{64,6... | collective-permute-start | bytes 393224 | tf_op jit(solution)/shard_map/ppermute | solution.py:253
  15.2 0.7 %collective-permute-start.8 = (bf16[128,512]{1,0:T(8,128)(2,1)S(1)}, bf16[128,512]{1,0:T(8,128)(2,1)S(1)}, u32[]{:S(2)}, u32[]{:S(2)}) collective-permute-start(bf16[128,512]{1,0:T(8,128)(2,1)S(1)} %add_add_fusion.3), channel_id=1, source_target_pairs={{0,5},{8,13},{16,21},{24,29},{32,37},{40,45},{48,53},{56,61},{64,6... | collective-permute-start | bytes 393224 | tf_op jit(solution)/shard_map/ppermute | solution.py:253
  15.9 0.0 collective-permute-done.7
  15.9 0.0 collective-permute-done.8
  16.0 4.4 %collective-permute-done.10 = bf16[512,1024]{1,0:T(8,128)(2,1)S(1)} collective-permute-done((bf16[512,1024]{1,0:T(8,128)(2,1)S(1)}, bf16[512,1024]{1,0:T(8,128)(2,1)S(1)}, u32[]{:S(2)}, u32[]{:S(2)}) %collective-permute-start.10) | collective-permute-done | bytes 1048608 | tf_op jit(solution)/shard_map/ppermute | solution.py:253
  20.4 1.4 %collective-permute-done.9 = bf16[512,1024]{1,0:T(8,128)(2,1)} collective-permute-done((bf16[512,1024]{1,0:T(8,128)(2,1)S(1)}, bf16[512,1024]{1,0:T(8,128)(2,1)}, u32[]{:S(2)}, u32[]{:S(2)}) %collective-permute-start.9) | collective-permute-done | bytes 1048608 | tf_op jit(solution)/shard_map/ppermute | solution.py:253
  21.7 0.7 %collective-permute-start.11 = (bf16[128,512]{1,0:T(8,128)(2,1)S(1)}, bf16[128,512]{1,0:T(8,128)(2,1)S(1)}, u32[]{:S(2)}, u32[]{:S(2)}) collective-permute-start(bf16[128,512]{1,0:T(8,128)(2,1)S(1)} %add_add_fusion.2), channel_id=1, source_target_pairs={{0,1},{8,9},{16,17},{24,25},{32,33},{40,41},{48,49},{56,57},{64,65... | collective-permute-start | bytes 393224 | tf_op jit(solution)/shard_map/ppermute | solution.py:253
  22.4 1.3 %collective-permute-start.12 = (bf16[128,512]{1,0:T(8,128)(2,1)S(1)}, bf16[128,512]{1,0:T(8,128)(2,1)S(1)}, u32[]{:S(2)}, u32[]{:S(2)}) collective-permute-start(bf16[128,512]{1,0:T(8,128)(2,1)S(1)} %add_add_fusion.2), channel_id=1, source_target_pairs={{0,7},{8,15},{16,23},{24,31},{32,39},{40,47},{48,55},{56,63},{64,7... | collective-permute-start | bytes 393224 | tf_op jit(solution)/shard_map/ppermute | solution.py:253
  23.7 1.4 %add_select_fusion.held_ref = bf16[512,1024]{1,0:T(8,128)(2,1)S(1)} fusion(bf16[512,1024]{1,0:T(8,128)(2,1)S(1)} %copy-done, bf16[512,1024]{1,0:T(8,128)(2,1)} %collective-permute-done.9, bf16[512,1024]{1,0:T(8,128)(2,1)S(1)} %collective-permute-done.10, pred[]{:T(512)S(6)} %eq.9), kind=kLoop, calls=%fused_computation | loop fusion | flops 1048576 | bytes 4194305 | tf_op jit(solution)/shard_map/jit(_where)/select_n | solution.py:292
  25.1 0.0 collective-permute-done.11
  25.1 20.5 %collective-permute-done.12 = bf16[128,512]{1,0:T(8,128)(2,1)S(1)} collective-permute-done((bf16[128,512]{1,0:T(8,128)(2,1)S(1)}, bf16[128,512]{1,0:T(8,128)(2,1)S(1)}, u32[]{:S(2)}, u32[]{:S(2)}) %collective-permute-start.12) | collective-permute-done | bytes 131104 | tf_op jit(solution)/shard_map/ppermute | solution.py:253
  45.6 0.0 collective-permute-done.13.far_ref
  45.7 1.4 %collective-permute-start.14 = (bf16[512,1024]{1,0:T(8,128)(2,1)S(1)}, bf16[512,1024]{1,0:T(8,128)(2,1)S(1)}, u32[]{:S(2)}, u32[]{:S(2)}) collective-permute-start(bf16[512,1024]{1,0:T(8,128)(2,1)S(1)} %shard_map.30.even_ref), channel_id=1, source_target_pairs={{0,32},{1,33},{2,34},{3,35},{4,36},{5,37},{6,38},{7,39},{8,40},{9,... | collective-permute-start | bytes 3145736 | tf_op jit(solution)/shard_map/ppermute | solution.py:253
  47.0 1.0 %collective-permute-start.15 = (bf16[128,512]{1,0:T(8,128)(2,1)S(1)}, bf16[128,512]{1,0:T(8,128)(2,1)S(1)}, u32[]{:S(2)}, u32[]{:S(2)}) collective-permute-start(bf16[128,512]{1,0:T(8,128)(2,1)S(1)} %add_add_fusion.1.q0_ref), channel_id=1, source_target_pairs={{0,8},{1,9},{2,10},{3,11},{4,12},{5,13},{6,14},{7,15},{32,40},{33,... | collective-permute-start | bytes 393224 | tf_op jit(solution)/shard_map/ppermute | solution.py:253
  48.1 2.5 %collective-permute-start.16 = (bf16[128,512]{1,0:T(8,128)(2,1)S(1)}, bf16[128,512]{1,0:T(8,128)(2,1)S(1)}, u32[]{:S(2)}, u32[]{:S(2)}) collective-permute-start(bf16[128,512]{1,0:T(8,128)(2,1)S(1)} %add_add_fusion.1.q0_ref), channel_id=1, source_target_pairs={{0,24},{1,25},{2,26},{3,27},{4,28},{5,29},{6,30},{7,31},{32,56},{3... | collective-permute-start | bytes 393224 | tf_op jit(solution)/shard_map/ppermute | solution.py:253
  50.6 1.4 %collective-permute-start.17 = (bf16[128,512]{1,0:T(8,128)(2,1)S(1)}, bf16[128,512]{1,0:T(8,128)(2,1)S(1)}, u32[]{:S(2)}, u32[]{:S(2)}) collective-permute-start(bf16[128,512]{1,0:T(8,128)(2,1)S(1)} %add_add_fusion.1.q0_ref), channel_id=1, source_target_pairs={{0,16},{1,17},{2,18},{3,19},{4,20},{5,21},{6,22},{7,23},{32,48},{3... | collective-permute-start | bytes 393224 | tf_op jit(solution)/shard_map/ppermute | solution.py:253
  52.0 1.5 %collective-permute-done.15.q1_ref = bf16[128,512]{1,0:T(8,128)(2,1)S(1)} collective-permute-done((bf16[128,512]{1,0:T(8,128)(2,1)S(1)}, bf16[128,512]{1,0:T(8,128)(2,1)S(1)}, u32[]{:S(2)}, u32[]{:S(2)}) %collective-permute-start.15) | collective-permute-done | bytes 131104 | tf_op jit(solution)/shard_map/ppermute | solution.py:253
  53.4 0.0 collective-permute-done.16.q3_ref
  53.4 3.6 %collective-permute-done.17.q2_ref = bf16[128,512]{1,0:T(8,128)(2,1)S(1)} collective-permute-done((bf16[128,512]{1,0:T(8,128)(2,1)S(1)}, bf16[128,512]{1,0:T(8,128)(2,1)S(1)}, u32[]{:S(2)}, u32[]{:S(2)}) %collective-permute-start.17) | collective-permute-done | bytes 131104 | tf_op jit(solution)/shard_map/ppermute | solution.py:253
  57.1 0.0 collective-permute-done.14.odd_ref
  57.1 2.3 %shard_map.31 = bf16[512,1024]{1,0:T(8,128)(2,1)} custom-call(f32[8,64]{1,0:T(8,128)S(1)} %copy-done.1, bf16[512,1024]{1,0:T(8,128)(2,1)S(1)} %copy-done, bf16[512,1024]{1,0:T(8,128)(2,1)S(1)} %shard_map.30.even_ref, bf16[512,1024]{1,0:T(8,128)(2,1)S(1)} %collective-permute-done.14.odd_ref, bf16[128,512]{1,0:T(8,128)(2,1)S(1)} %add_add_fusion.1.q0_ref, ...), custom_call_target="tpu_custom_call" | custom-call | flops 536870912 | bytes 4194304 | tf_op jit(solution)/shard_map/pallas_call | solution.py:234
  (4 shorter events, 0.1 us)
Async XLA Ops:
  0.1 3.1 %copy-start = (bf16[512,1024]{1,0:T(8,128)(2,1)S(1)}, bf16[512,1024]{1,0:T(8,128)(2,1)}, u32[]{:S(2)}) copy-start(bf16[512,1024]{1,0:T(8,128)(2,1)} %own_ref.3) | copy-start | bytes 3145732
  0.1 2.2 %collective-permute-start = (bf16[320,512]{1,0:T(8,128)(2,1)S(1)}, bf16[320,512]{1,0:T(8,128)(2,1)S(1)}, u32[]{:S(2)}, u32[]{:S(2)}) collective-permute-start(bf16[320,512]{1,0:T(8,128)(2,1)S(1)} %shard_map.28), channel_id=1, source_target_pairs={{0,128}} | collective-permute-start | bytes 983048 | tf_op jit(solution)/shard_map/ppermute | solution.py:253
  0.9 1.4 %collective-permute-start.1 = (bf16[320,512]{1,0:T(8,128)(2,1)S(1)}, bf16[320,512]{1,0:T(8,128)(2,1)S(1)}, u32[]{:S(2)}, u32[]{:S(2)}) collective-permute-start(bf16[320,512]{1,0:T(8,128)(2,1)S(1)} %shard_map.28), channel_id=1, source_target_pairs={{0,64}} | collective-permute-start | bytes 983048 | tf_op jit(solution)/shard_map/ppermute | solution.py:253
  1.6 0.7 %collective-permute-start.2 = (bf16[320,512]{1,0:T(8,128)(2,1)S(1)}, bf16[320,512]{1,0:T(8,128)(2,1)S(1)}, u32[]{:S(2)}, u32[]{:S(2)}) collective-permute-start(bf16[320,512]{1,0:T(8,128)(2,1)S(1)} %shard_map.28), channel_id=1, source_target_pairs={{0,192}} | collective-permute-start | bytes 983048 | tf_op jit(solution)/shard_map/ppermute | solution.py:253
  2.3 8.1 %copy-start.1 = (f32[8,64]{1,0:T(8,128)S(1)}, f32[8,64]{1,0:T(8,128)}, u32[]{:S(2)}) copy-start(f32[8,64]{1,0:T(8,128)} %scales_ref.3) | copy-start | bytes 6148
  2.5 8.0 %collective-permute-start.3 = (bf16[320,512]{1,0:T(8,128)(2,1)S(1)}, bf16[320,512]{1,0:T(8,128)(2,1)S(1)}, u32[]{:S(2)}, u32[]{:S(2)}) collective-permute-start(bf16[320,512]{1,0:T(8,128)(2,1)S(1)} %get-tuple-element.34), channel_id=1, source_target_pairs={{0,32},{32,0},{64,96},{96,64},{128,160},{160,128},{192,224},{224,1... | collective-permute-start | bytes 983048 | tf_op jit(solution)/shard_map/ppermute | solution.py:253
  3.2 17.2 %collective-permute-start.10 = (bf16[512,1024]{1,0:T(8,128)(2,1)S(1)}, bf16[512,1024]{1,0:T(8,128)(2,1)S(1)}, u32[]{:S(2)}, u32[]{:S(2)}) collective-permute-start(bf16[512,1024]{1,0:T(8,128)(2,1)S(1)} %copy-done), channel_id=1, source_target_pairs={{0,192},{1,193},{2,194},{3,195},{4,196},{5,197},{6,198},{7,199},{8... | collective-permute-start | bytes 3145736 | tf_op jit(solution)/shard_map/ppermute | solution.py:253
  8.2 13.6 %collective-permute-start.9 = (bf16[512,1024]{1,0:T(8,128)(2,1)S(1)}, bf16[512,1024]{1,0:T(8,128)(2,1)}, u32[]{:S(2)}, u32[]{:S(2)}) collective-permute-start(bf16[512,1024]{1,0:T(8,128)(2,1)S(1)} %copy-done), channel_id=1, source_target_pairs={{0,64},{1,65},{2,66},{3,67},{4,68},{5,69},{6,70},{7,71},{8,72},{9,... | collective-permute-start | bytes 3145736 | tf_op jit(solution)/shard_map/ppermute | solution.py:253
  11.1 2.0 %collective-permute-start.4 = (bf16[128,512]{1,0:T(8,128)(2,1)S(1)}, bf16[128,512]{1,0:T(8,128)(2,1)S(1)}, u32[]{:S(2)}, u32[]{:S(2)}) collective-permute-start(bf16[128,512]{1,0:T(8,128)(2,1)S(1)} %get-tuple-element.23), channel_id=1, source_target_pairs={{0,16},{32,48},{64,80},{96,112},{128,144},{160,176},{192,208},{224... | collective-permute-start | bytes 393224 | tf_op jit(solution)/shard_map/ppermute | solution.py:253
  11.8 2.7 %collective-permute-start.5 = (bf16[128,512]{1,0:T(8,128)(2,1)S(1)}, bf16[128,512]{1,0:T(8,128)(2,1)S(1)}, u32[]{:S(2)}, u32[]{:S(2)}) collective-permute-start(bf16[128,512]{1,0:T(8,128)(2,1)S(1)} %get-tuple-element.24), channel_id=1, source_target_pairs={{0,8},{32,40},{64,72},{96,104},{128,136},{160,168},{192,200},{224,... | collective-permute-start | bytes 393224 | tf_op jit(solution)/shard_map/ppermute | solution.py:253
  12.5 2.1 %collective-permute-start.6 = (bf16[128,512]{1,0:T(8,128)(2,1)S(1)}, bf16[128,512]{1,0:T(8,128)(2,1)S(1)}, u32[]{:S(2)}, u32[]{:S(2)}) collective-permute-start(bf16[128,512]{1,0:T(8,128)(2,1)S(1)} %get-tuple-element.25), channel_id=1, source_target_pairs={{0,24},{32,56},{64,88},{96,120},{128,152},{160,184},{192,216},{224... | collective-permute-start | bytes 393224 | tf_op jit(solution)/shard_map/ppermute | solution.py:253
  13.1 32.5 %collective-permute-start.13 = (bf16[512,1024]{1,0:T(8,128)(2,1)S(1)}, bf16[512,1024]{1,0:T(8,128)(2,1)S(1)}, u32[]{:S(2)}, u32[]{:S(2)}) collective-permute-start(bf16[512,1024]{1,0:T(8,128)(2,1)S(1)} %copy-done), channel_id=1, source_target_pairs={{0,128},{1,129},{2,130},{3,131},{4,132},{5,133},{6,134},{7,135},{8... | collective-permute-start | bytes 3145736 | tf_op jit(solution)/shard_map/ppermute | solution.py:253
  14.6 1.4 %collective-permute-start.7 = (bf16[128,512]{1,0:T(8,128)(2,1)S(1)}, bf16[128,512]{1,0:T(8,128)(2,1)S(1)}, u32[]{:S(2)}, u32[]{:S(2)}) collective-permute-start(bf16[128,512]{1,0:T(8,128)(2,1)S(1)} %add_add_fusion.3), channel_id=1, source_target_pairs={{0,3},{8,11},{16,19},{24,27},{32,35},{40,43},{48,51},{56,59},{64,6... | collective-permute-start | bytes 393224 | tf_op jit(solution)/shard_map/ppermute | solution.py:253
  15.2 0.7 %collective-permute-start.8 = (bf16[128,512]{1,0:T(8,128)(2,1)S(1)}, bf16[128,512]{1,0:T(8,128)(2,1)S(1)}, u32[]{:S(2)}, u32[]{:S(2)}) collective-permute-start(bf16[128,512]{1,0:T(8,128)(2,1)S(1)} %add_add_fusion.3), channel_id=1, source_target_pairs={{0,5},{8,13},{16,21},{24,29},{32,37},{40,45},{48,53},{56,61},{64,6... | collective-permute-start | bytes 393224 | tf_op jit(solution)/shard_map/ppermute | solution.py:253
  21.7 3.4 %collective-permute-start.11 = (bf16[128,512]{1,0:T(8,128)(2,1)S(1)}, bf16[128,512]{1,0:T(8,128)(2,1)S(1)}, u32[]{:S(2)}, u32[]{:S(2)}) collective-permute-start(bf16[128,512]{1,0:T(8,128)(2,1)S(1)} %add_add_fusion.2), channel_id=1, source_target_pairs={{0,1},{8,9},{16,17},{24,25},{32,33},{40,41},{48,49},{56,57},{64,65... | collective-permute-start | bytes 393224 | tf_op jit(solution)/shard_map/ppermute | solution.py:253
  22.4 23.2 %collective-permute-start.12 = (bf16[128,512]{1,0:T(8,128)(2,1)S(1)}, bf16[128,512]{1,0:T(8,128)(2,1)S(1)}, u32[]{:S(2)}, u32[]{:S(2)}) collective-permute-start(bf16[128,512]{1,0:T(8,128)(2,1)S(1)} %add_add_fusion.2), channel_id=1, source_target_pairs={{0,7},{8,15},{16,23},{24,31},{32,39},{40,47},{48,55},{56,63},{64,7... | collective-permute-start | bytes 393224 | tf_op jit(solution)/shard_map/ppermute | solution.py:253
  45.7 11.4 %collective-permute-start.14 = (bf16[512,1024]{1,0:T(8,128)(2,1)S(1)}, bf16[512,1024]{1,0:T(8,128)(2,1)S(1)}, u32[]{:S(2)}, u32[]{:S(2)}) collective-permute-start(bf16[512,1024]{1,0:T(8,128)(2,1)S(1)} %shard_map.30.even_ref), channel_id=1, source_target_pairs={{0,32},{1,33},{2,34},{3,35},{4,36},{5,37},{6,38},{7,39},{8,40},{9,... | collective-permute-start | bytes 3145736 | tf_op jit(solution)/shard_map/ppermute | solution.py:253
  47.0 6.4 %collective-permute-start.15 = (bf16[128,512]{1,0:T(8,128)(2,1)S(1)}, bf16[128,512]{1,0:T(8,128)(2,1)S(1)}, u32[]{:S(2)}, u32[]{:S(2)}) collective-permute-start(bf16[128,512]{1,0:T(8,128)(2,1)S(1)} %add_add_fusion.1.q0_ref), channel_id=1, source_target_pairs={{0,8},{1,9},{2,10},{3,11},{4,12},{5,13},{6,14},{7,15},{32,40},{33,... | collective-permute-start | bytes 393224 | tf_op jit(solution)/shard_map/ppermute | solution.py:253
  48.1 5.4 %collective-permute-start.16 = (bf16[128,512]{1,0:T(8,128)(2,1)S(1)}, bf16[128,512]{1,0:T(8,128)(2,1)S(1)}, u32[]{:S(2)}, u32[]{:S(2)}) collective-permute-start(bf16[128,512]{1,0:T(8,128)(2,1)S(1)} %add_add_fusion.1.q0_ref), channel_id=1, source_target_pairs={{0,24},{1,25},{2,26},{3,27},{4,28},{5,29},{6,30},{7,31},{32,56},{3... | collective-permute-start | bytes 393224 | tf_op jit(solution)/shard_map/ppermute | solution.py:253
  50.6 6.5 %collective-permute-start.17 = (bf16[128,512]{1,0:T(8,128)(2,1)S(1)}, bf16[128,512]{1,0:T(8,128)(2,1)S(1)}, u32[]{:S(2)}, u32[]{:S(2)}) collective-permute-start(bf16[128,512]{1,0:T(8,128)(2,1)S(1)} %add_add_fusion.1.q0_ref), channel_id=1, source_target_pairs={{0,16},{1,17},{2,18},{3,19},{4,20},{5,21},{6,22},{7,23},{32,48},{3... | collective-permute-start | bytes 393224 | tf_op jit(solution)/shard_map/ppermute | solution.py:253

commit v4 on v3

--- a/solution.py
+++ b/solution.py
@@ -166,28 +166,30 @@
     )(scales, low, swap, own)
 
 
-def merge_kernel(held_ref, far_ref, out_ref, sem):
-    del held_ref
-
-    @pl.when(lax.axis_index("prow") == 4)
-    def _():
-        copy = pltpu.make_async_copy(far_ref, out_ref, sem)
-        copy.start()
-        copy.wait()
-
-
-def merge(held, far):
+def merge_kernel(y2_ref, matrix_ref, y4_ref, y6_ref, out_ref, sem):
+    del y2_ref
+    prow_at = lax.axis_index("prow")
+    for at, ref in ((0, matrix_ref), (4, y4_ref), (6, y6_ref)):
+
+        @pl.when(prow_at == at)
+        def _():
+            copy = pltpu.make_async_copy(ref, out_ref, sem)
+            copy.start()
+            copy.wait()
+
+
+def merge(y2, blocks):
     vmem = pl.BlockSpec(memory_space=pltpu.VMEM)
     return pl.pallas_call(
         merge_kernel,
-        out_shape=pltpu.VMEM(held.shape, BF),
-        in_specs=[vmem, pl.BlockSpec(memory_space=pl.ANY)],
+        out_shape=pltpu.VMEM(y2.shape, BF),
+        in_specs=[vmem] + [pl.BlockSpec(memory_space=pl.ANY)] * 3,
         out_specs=vmem,
         scratch_shapes=[pltpu.SemaphoreType.DMA],
         input_output_aliases={0: 0},
         compiler_params=pltpu.CompilerParams(vmem_limit_bytes=2**20),
         cost_estimate=pl.CostEstimate(flops=0, bytes_accessed=0, transcendentals=0),
-    )(held, far)
+    )(y2, *blocks)
 
 
 def update_kernel(
@@ -274,7 +276,7 @@
     corner = [(0, 0)]
     prow_at = lax.axis_index("prow")
     low = pack(matrix)
-    low_y = [along_prow(low, [(0, p)], corner) for p in (4, 2, 6)]
+    low_y = [along_prow(low, [(0, p)], corner) for p in (2, 6, 4)]
     own, *low_y = lax.optimization_barrier((matrix, *low_y))
     low = low + low_y[0] + low_y[1] + low_y[2]
     low_swap = along_prow(low, [(p, p ^ 1) for p in range(8)], corner)
@@ -289,11 +291,10 @@
     q3, q5 = along_z(q, [(0, 3)]), along_z(q, [(0, 5)])
     q = q + q3 + q5
     q, y2, y6 = lax.optimization_barrier((q, y2, y6))
-    even = jnp.where(prow_at == 0, matrix, y2 + y6)
     up_z, down_z = along_z(q, [(0, 1), (3, 4), (5, 6)]), along_z(q, [(0, 7), (3, 2)])
     q = q + up_z + down_z
-    q, even, y4 = lax.optimization_barrier((q, even, y4))
-    even = merge(even, y4)
+    q, y2, y4, y6 = lax.optimization_barrier((q, y2, y4, y6))
+    even = merge(y2, (matrix, y4, y6))
     odd = along_prow(even, [(0, 1), (2, 3), (4, 5), (6, 7)], everywhere)
     q2 = along_x(q, [(a, (a + 2) % XS) for a in range(XS)], range(ZS))
     q1 = along_x(q, [(a, (a + 1) % XS) for a in range(XS)], range(ZS))

time: 60 us -> 58.8 us (0.980)
  waiting for transfers between devices: 31.4 us -> 33.1 us
  other arithmetic: 1.59 us -> 0.15 us
  starting transfers between devices: 23 us -> 21.7 us
    ppermute x18, waiting for transfers between devices: 31.4 us -> 33.1 us  [send(): return lax.ppermute(value, ('prow', 'pcol'), flat)]
    select_n x1 -> x0, other arithmetic: 1.42 us -> none  [on_device(): even = jnp.where(prow_at == 0, matrix, y2 + y6)]
    ppermute x18, starting transfers between devices: 23 us -> 21.7 us  [send(): return lax.ppermute(value, ('prow', 'pcol'), flat)]
  transfers between devices with their start and end apart: 18 -> 18, of which waited for: 5 -> 6; matrix products, arithmetic and copies ran while one was open for 3% -> 0% of each run, Pallas kernels for 1% -> 1%
where the time goes in v4:
time: 58.8 us; the launch traced here: 58.4 us
  waiting for transfers between devices  33.1 us (56%)
  starting transfers between devices  21.7 us (37%)
  Pallas kernels  3.14 us (5%)
    ppermute x18, waiting for transfers between devices, send(): return lax.ppermute(value, ('prow', 'pcol'), flat)  33.1 us
    ppermute x18, starting transfers between devices, send(): return lax.ppermute(value, ('prow', 'pcol'), flat)  21.7 us
    pallas_call x1, Pallas kernels, update(): pl.pallas_call(update_kernel, out_shape=jax.ShapeDtypeStruct((NB, 2 * NB)...  2.3 us
  transfers between devices with their start and end apart: 18, of which 6 were waited for; matrix products, arithmetic and copies ran while one was open for 0% of the time, Pallas kernels for 1%

profile of v4, /device:TPU:64, one launch (start us, length us, event | category | flops | bytes accessed | tf_op | source)
XLA Modules:
  0.0 58.4 jit_solution(1788702241215792621)
XLA Ops:
  0.0 0.1 shard_map.28
  0.1 0.0 copy-start
  0.1 0.8 %collective-permute-start.2 = (bf16[320,512]{1,0:T(8,128)(2,1)S(1)}, bf16[320,512]{1,0:T(8,128)(2,1)S(1)}, u32[]{:S(2)}, u32[]{:S(2)}) collective-permute-start(bf16[320,512]{1,0:T(8,128)(2,1)S(1)} %shard_map.28), channel_id=1, source_target_pairs={{0,128}} | collective-permute-start | bytes 983048 | tf_op jit(solution)/shard_map/ppermute | solution.py:255
  0.9 0.7 %collective-permute-start.1 = (bf16[320,512]{1,0:T(8,128)(2,1)S(1)}, bf16[320,512]{1,0:T(8,128)(2,1)S(1)}, u32[]{:S(2)}, u32[]{:S(2)}) collective-permute-start(bf16[320,512]{1,0:T(8,128)(2,1)S(1)} %shard_map.28), channel_id=1, source_target_pairs={{0,192}} | collective-permute-start | bytes 983048 | tf_op jit(solution)/shard_map/ppermute | solution.py:255
  1.6 0.7 %collective-permute-start = (bf16[320,512]{1,0:T(8,128)(2,1)S(1)}, bf16[320,512]{1,0:T(8,128)(2,1)S(1)}, u32[]{:S(2)}, u32[]{:S(2)}) collective-permute-start(bf16[320,512]{1,0:T(8,128)(2,1)S(1)} %shard_map.28), channel_id=1, source_target_pairs={{0,64}} | collective-permute-start | bytes 983048 | tf_op jit(solution)/shard_map/ppermute | solution.py:255
  2.3 0.0 collective-permute-done.2
  2.3 0.0 collective-permute-done.1
  2.3 0.0 collective-permute-done
  2.3 0.0 copy-start.1
  2.4 0.1 broadcast_select_fusion
  2.4 0.7 %collective-permute-start.3 = (bf16[320,512]{1,0:T(8,128)(2,1)S(1)}, bf16[320,512]{1,0:T(8,128)(2,1)S(1)}, u32[]{:S(2)}, u32[]{:S(2)}) collective-permute-start(bf16[320,512]{1,0:T(8,128)(2,1)S(1)} %get-tuple-element.36), channel_id=1, source_target_pairs={{0,32},{32,0},{64,96},{96,64},{128,160},{160,128},{192,224},{224,1... | collective-permute-start | bytes 983048 | tf_op jit(solution)/shard_map/ppermute | solution.py:255
  3.1 0.0 copy-done
  3.1 5.0 %collective-permute-start.10 = (bf16[512,1024]{1,0:T(8,128)(2,1)S(1)}, bf16[512,1024]{1,0:T(8,128)(2,1)S(1)}, u32[]{:S(2)}, u32[]{:S(2)}) collective-permute-start(bf16[512,1024]{1,0:T(8,128)(2,1)S(1)} %copy-done), channel_id=1, source_target_pairs={{0,192},{1,193},{2,194},{3,195},{4,196},{5,197},{6,198},{7,199},{8... | collective-permute-start | bytes 3145736 | tf_op jit(solution)/shard_map/ppermute | solution.py:255
  8.1 1.4 %collective-permute-start.9 = (bf16[512,1024]{1,0:T(8,128)(2,1)S(1)}, bf16[512,1024]{1,0:T(8,128)(2,1)S(1)}, u32[]{:S(2)}, u32[]{:S(2)}) collective-permute-start(bf16[512,1024]{1,0:T(8,128)(2,1)S(1)} %copy-done), channel_id=1, source_target_pairs={{0,64},{1,65},{2,66},{3,67},{4,68},{5,69},{6,70},{7,71},{8,72},{9,... | collective-permute-start | bytes 3145736 | tf_op jit(solution)/shard_map/ppermute | solution.py:255
  9.5 0.0 collective-permute-done.3.swap_ref
  9.5 0.0 copy-done.1
  9.5 0.6 %shard_map.29 = (bf16[128,512]{1,0:T(8,128)(2,1)S(1)}, bf16[128,512]{1,0:T(8,128)(2,1)S(1)}, bf16[128,512]{1,0:T(8,128)(2,1)S(1)}, bf16[128,512]{1,0:T(8,128)(2,1)S(1)}) custom-call(f32[8,64]{1,0:T(8,128)S(1)} %copy-done.1, bf16[320,512]{1,0:T(8,128)(2,1)S(1)} %get-tuple-element.35.low_ref, bf16[320,512]{1,0:T(8,128)(2,1)S(1)} %collective-permute-done.3.swap_ref, ...), custom_call_target="tpu_custom_call" | custom-call | tf_op jit(solution)/shard_map/pallas_call | solution.py:158
  10.2 0.7 %collective-permute-start.4 = (bf16[128,512]{1,0:T(8,128)(2,1)S(1)}, bf16[128,512]{1,0:T(8,128)(2,1)S(1)}, u32[]{:S(2)}, u32[]{:S(2)}) collective-permute-start(bf16[128,512]{1,0:T(8,128)(2,1)S(1)} %get-tuple-element.24), channel_id=1, source_target_pairs={{0,16},{32,48},{64,80},{96,112},{128,144},{160,176},{192,208},{224... | collective-permute-start | bytes 393224 | tf_op jit(solution)/shard_map/ppermute | solution.py:255
  10.8 0.7 %collective-permute-start.5 = (bf16[128,512]{1,0:T(8,128)(2,1)S(1)}, bf16[128,512]{1,0:T(8,128)(2,1)S(1)}, u32[]{:S(2)}, u32[]{:S(2)}) collective-permute-start(bf16[128,512]{1,0:T(8,128)(2,1)S(1)} %get-tuple-element.25), channel_id=1, source_target_pairs={{0,8},{32,40},{64,72},{96,104},{128,136},{160,168},{192,200},{224,... | collective-permute-start | bytes 393224 | tf_op jit(solution)/shard_map/ppermute | solution.py:255
  11.5 0.7 %collective-permute-start.6 = (bf16[128,512]{1,0:T(8,128)(2,1)S(1)}, bf16[128,512]{1,0:T(8,128)(2,1)S(1)}, u32[]{:S(2)}, u32[]{:S(2)}) collective-permute-start(bf16[128,512]{1,0:T(8,128)(2,1)S(1)} %get-tuple-element.26), channel_id=1, source_target_pairs={{0,24},{32,56},{64,88},{96,120},{128,152},{160,184},{192,216},{224... | collective-permute-start | bytes 393224 | tf_op jit(solution)/shard_map/ppermute | solution.py:255
  12.2 0.0 collective-permute-done.4
  12.2 1.4 %collective-permute-start.13 = (bf16[512,1024]{1,0:T(8,128)(2,1)S(1)}, bf16[512,1024]{1,0:T(8,128)(2,1)S(1)}, u32[]{:S(2)}, u32[]{:S(2)}) collective-permute-start(bf16[512,1024]{1,0:T(8,128)(2,1)S(1)} %copy-done), channel_id=1, source_target_pairs={{0,128},{1,129},{2,130},{3,131},{4,132},{5,133},{6,134},{7,135},{8... | collective-permute-start | bytes 3145736 | tf_op jit(solution)/shard_map/ppermute | solution.py:255
  13.6 0.0 collective-permute-done.5
  13.6 0.0 collective-permute-done.6
  13.6 0.7 %collective-permute-start.8 = (bf16[128,512]{1,0:T(8,128)(2,1)S(1)}, bf16[128,512]{1,0:T(8,128)(2,1)S(1)}, u32[]{:S(2)}, u32[]{:S(2)}) collective-permute-start(bf16[128,512]{1,0:T(8,128)(2,1)S(1)} %add_add_fusion.3), channel_id=1, source_target_pairs={{0,5},{8,13},{16,21},{24,29},{32,37},{40,45},{48,53},{56,61},{64,6... | collective-permute-start | bytes 393224 | tf_op jit(solution)/shard_map/ppermute | solution.py:255
  14.3 0.7 %collective-permute-start.7 = (bf16[128,512]{1,0:T(8,128)(2,1)S(1)}, bf16[128,512]{1,0:T(8,128)(2,1)S(1)}, u32[]{:S(2)}, u32[]{:S(2)}) collective-permute-start(bf16[128,512]{1,0:T(8,128)(2,1)S(1)} %add_add_fusion.3), channel_id=1, source_target_pairs={{0,3},{8,11},{16,19},{24,27},{32,35},{40,43},{48,51},{56,59},{64,6... | collective-permute-start | bytes 393224 | tf_op jit(solution)/shard_map/ppermute | solution.py:255
  15.0 0.0 collective-permute-done.8
  15.0 0.0 collective-permute-done.7
  15.0 5.3 %collective-permute-done.10.y6_ref = bf16[512,1024]{1,0:T(8,128)(2,1)S(1)} collective-permute-done((bf16[512,1024]{1,0:T(8,128)(2,1)S(1)}, bf16[512,1024]{1,0:T(8,128)(2,1)S(1)}, u32[]{:S(2)}, u32[]{:S(2)}) %collective-permute-start.10) | collective-permute-done | bytes 1048608 | tf_op jit(solution)/shard_map/ppermute | solution.py:255
  20.4 1.4 %collective-permute-done.9.y2_ref = bf16[512,1024]{1,0:T(8,128)(2,1)S(1)} collective-permute-done((bf16[512,1024]{1,0:T(8,128)(2,1)S(1)}, bf16[512,1024]{1,0:T(8,128)(2,1)S(1)}, u32[]{:S(2)}, u32[]{:S(2)}) %collective-permute-start.9) | collective-permute-done | bytes 1048608 | tf_op jit(solution)/shard_map/ppermute | solution.py:255
  21.7 1.3 %collective-permute-start.12 = (bf16[128,512]{1,0:T(8,128)(2,1)S(1)}, bf16[128,512]{1,0:T(8,128)(2,1)S(1)}, u32[]{:S(2)}, u32[]{:S(2)}) collective-permute-start(bf16[128,512]{1,0:T(8,128)(2,1)S(1)} %add_add_fusion.2), channel_id=1, source_target_pairs={{0,7},{8,15},{16,23},{24,31},{32,39},{40,47},{48,55},{56,63},{64,7... | collective-permute-start | bytes 393224 | tf_op jit(solution)/shard_map/ppermute | solution.py:255
  23.0 0.7 %collective-permute-start.11 = (bf16[128,512]{1,0:T(8,128)(2,1)S(1)}, bf16[128,512]{1,0:T(8,128)(2,1)S(1)}, u32[]{:S(2)}, u32[]{:S(2)}) collective-permute-start(bf16[128,512]{1,0:T(8,128)(2,1)S(1)} %add_add_fusion.2), channel_id=1, source_target_pairs={{0,1},{8,9},{16,17},{24,25},{32,33},{40,41},{48,49},{56,57},{64,65... | collective-permute-start | bytes 393224 | tf_op jit(solution)/shard_map/ppermute | solution.py:255
  23.7 20.8 %collective-permute-done.12 = bf16[128,512]{1,0:T(8,128)(2,1)S(1)} collective-permute-done((bf16[128,512]{1,0:T(8,128)(2,1)S(1)}, bf16[128,512]{1,0:T(8,128)(2,1)S(1)}, u32[]{:S(2)}, u32[]{:S(2)}) %collective-permute-start.12) | collective-permute-done | bytes 131104 | tf_op jit(solution)/shard_map/ppermute | solution.py:255
  44.5 0.0 collective-permute-done.11
  44.6 0.0 collective-permute-done.13.y4_ref
  44.6 0.1 shard_map.30.even_ref
  44.7 1.4 %collective-permute-start.14 = (bf16[512,1024]{1,0:T(8,128)(2,1)S(1)}, bf16[512,1024]{1,0:T(8,128)(2,1)S(1)}, u32[]{:S(2)}, u32[]{:S(2)}) collective-permute-start(bf16[512,1024]{1,0:T(8,128)(2,1)S(1)} %shard_map.30.even_ref), channel_id=1, source_target_pairs={{0,32},{1,33},{2,34},{3,35},{4,36},{5,37},{6,38},{7,39},{8,40},{9,... | collective-permute-start | bytes 3145736 | tf_op jit(solution)/shard_map/ppermute | solution.py:255
  46.0 2.0 %collective-permute-start.17 = (bf16[128,512]{1,0:T(8,128)(2,1)S(1)}, bf16[128,512]{1,0:T(8,128)(2,1)S(1)}, u32[]{:S(2)}, u32[]{:S(2)}) collective-permute-start(bf16[128,512]{1,0:T(8,128)(2,1)S(1)} %add_add_fusion.1.q0_ref), channel_id=1, source_target_pairs={{0,16},{1,17},{2,18},{3,19},{4,20},{5,21},{6,22},{7,23},{32,48},{3... | collective-permute-start | bytes 393224 | tf_op jit(solution)/shard_map/ppermute | solution.py:255
  48.1 1.8 %collective-permute-start.16 = (bf16[128,512]{1,0:T(8,128)(2,1)S(1)}, bf16[128,512]{1,0:T(8,128)(2,1)S(1)}, u32[]{:S(2)}, u32[]{:S(2)}) collective-permute-start(bf16[128,512]{1,0:T(8,128)(2,1)S(1)} %add_add_fusion.1.q0_ref), channel_id=1, source_target_pairs={{0,24},{1,25},{2,26},{3,27},{4,28},{5,29},{6,30},{7,31},{32,56},{3... | collective-permute-start | bytes 393224 | tf_op jit(solution)/shard_map/ppermute | solution.py:255
  49.9 0.6 %collective-permute-start.15 = (bf16[128,512]{1,0:T(8,128)(2,1)S(1)}, bf16[128,512]{1,0:T(8,128)(2,1)S(1)}, u32[]{:S(2)}, u32[]{:S(2)}) collective-permute-start(bf16[128,512]{1,0:T(8,128)(2,1)S(1)} %add_add_fusion.1.q0_ref), channel_id=1, source_target_pairs={{0,8},{1,9},{2,10},{3,11},{4,12},{5,13},{6,14},{7,15},{32,40},{33,... | collective-permute-start | bytes 393224 | tf_op jit(solution)/shard_map/ppermute | solution.py:255
  50.5 2.1 %collective-permute-done.17.q2_ref = bf16[128,512]{1,0:T(8,128)(2,1)S(1)} collective-permute-done((bf16[128,512]{1,0:T(8,128)(2,1)S(1)}, bf16[128,512]{1,0:T(8,128)(2,1)S(1)}, u32[]{:S(2)}, u32[]{:S(2)}) %collective-permute-start.17) | collective-permute-done | bytes 131104 | tf_op jit(solution)/shard_map/ppermute | solution.py:255
  52.6 2.3 %collective-permute-done.16.q3_ref = bf16[128,512]{1,0:T(8,128)(2,1)S(1)} collective-permute-done((bf16[128,512]{1,0:T(8,128)(2,1)S(1)}, bf16[128,512]{1,0:T(8,128)(2,1)S(1)}, u32[]{:S(2)}, u32[]{:S(2)}) %collective-permute-start.16) | collective-permute-done | bytes 131104 | tf_op jit(solution)/shard_map/ppermute | solution.py:255
  54.9 1.2 %collective-permute-done.15.q1_ref = bf16[128,512]{1,0:T(8,128)(2,1)S(1)} collective-permute-done((bf16[128,512]{1,0:T(8,128)(2,1)S(1)}, bf16[128,512]{1,0:T(8,128)(2,1)S(1)}, u32[]{:S(2)}, u32[]{:S(2)}) %collective-permute-start.15) | collective-permute-done | bytes 131104 | tf_op jit(solution)/shard_map/ppermute | solution.py:255
  56.1 0.0 collective-permute-done.14.odd_ref
  56.1 2.3 %shard_map.31 = bf16[512,1024]{1,0:T(8,128)(2,1)} custom-call(f32[8,64]{1,0:T(8,128)S(1)} %copy-done.1, bf16[512,1024]{1,0:T(8,128)(2,1)S(1)} %copy-done, bf16[512,1024]{1,0:T(8,128)(2,1)S(1)} %shard_map.30.even_ref, bf16[512,1024]{1,0:T(8,128)(2,1)S(1)} %collective-permute-done.14.odd_ref, bf16[128,512]{1,0:T(8,128)(2,1)S(1)} %add_add_fusion.1.q0_ref, ...), custom_call_target="tpu_custom_call" | custom-call | flops 536870912 | bytes 4194304 | tf_op jit(solution)/shard_map/pallas_call | solution.py:236
  (3 shorter events, 0.1 us)
Async XLA Ops:
  0.1 3.0 %copy-start = (bf16[512,1024]{1,0:T(8,128)(2,1)S(1)}, bf16[512,1024]{1,0:T(8,128)(2,1)}, u32[]{:S(2)}) copy-start(bf16[512,1024]{1,0:T(8,128)(2,1)} %own_ref.3) | copy-start | bytes 3145732
  0.1 2.2 %collective-permute-start.2 = (bf16[320,512]{1,0:T(8,128)(2,1)S(1)}, bf16[320,512]{1,0:T(8,128)(2,1)S(1)}, u32[]{:S(2)}, u32[]{:S(2)}) collective-permute-start(bf16[320,512]{1,0:T(8,128)(2,1)S(1)} %shard_map.28), channel_id=1, source_target_pairs={{0,128}} | collective-permute-start | bytes 983048 | tf_op jit(solution)/shard_map/ppermute | solution.py:255
  0.9 1.4 %collective-permute-start.1 = (bf16[320,512]{1,0:T(8,128)(2,1)S(1)}, bf16[320,512]{1,0:T(8,128)(2,1)S(1)}, u32[]{:S(2)}, u32[]{:S(2)}) collective-permute-start(bf16[320,512]{1,0:T(8,128)(2,1)S(1)} %shard_map.28), channel_id=1, source_target_pairs={{0,192}} | collective-permute-start | bytes 983048 | tf_op jit(solution)/shard_map/ppermute | solution.py:255
  1.6 0.7 %collective-permute-start = (bf16[320,512]{1,0:T(8,128)(2,1)S(1)}, bf16[320,512]{1,0:T(8,128)(2,1)S(1)}, u32[]{:S(2)}, u32[]{:S(2)}) collective-permute-start(bf16[320,512]{1,0:T(8,128)(2,1)S(1)} %shard_map.28), channel_id=1, source_target_pairs={{0,64}} | collective-permute-start | bytes 983048 | tf_op jit(solution)/shard_map/ppermute | solution.py:255
  2.3 7.2 %copy-start.1 = (f32[8,64]{1,0:T(8,128)S(1)}, f32[8,64]{1,0:T(8,128)}, u32[]{:S(2)}) copy-start(f32[8,64]{1,0:T(8,128)} %scales_ref.3) | copy-start | bytes 6148
  2.4 7.1 %collective-permute-start.3 = (bf16[320,512]{1,0:T(8,128)(2,1)S(1)}, bf16[320,512]{1,0:T(8,128)(2,1)S(1)}, u32[]{:S(2)}, u32[]{:S(2)}) collective-permute-start(bf16[320,512]{1,0:T(8,128)(2,1)S(1)} %get-tuple-element.36), channel_id=1, source_target_pairs={{0,32},{32,0},{64,96},{96,64},{128,160},{160,128},{192,224},{224,1... | collective-permute-start | bytes 983048 | tf_op jit(solution)/shard_map/ppermute | solution.py:255
  3.1 17.2 %collective-permute-start.10 = (bf16[512,1024]{1,0:T(8,128)(2,1)S(1)}, bf16[512,1024]{1,0:T(8,128)(2,1)S(1)}, u32[]{:S(2)}, u32[]{:S(2)}) collective-permute-start(bf16[512,1024]{1,0:T(8,128)(2,1)S(1)} %copy-done), channel_id=1, source_target_pairs={{0,192},{1,193},{2,194},{3,195},{4,196},{5,197},{6,198},{7,199},{8... | collective-permute-start | bytes 3145736 | tf_op jit(solution)/shard_map/ppermute | solution.py:255
  8.1 13.6 %collective-permute-start.9 = (bf16[512,1024]{1,0:T(8,128)(2,1)S(1)}, bf16[512,1024]{1,0:T(8,128)(2,1)S(1)}, u32[]{:S(2)}, u32[]{:S(2)}) collective-permute-start(bf16[512,1024]{1,0:T(8,128)(2,1)S(1)} %copy-done), channel_id=1, source_target_pairs={{0,64},{1,65},{2,66},{3,67},{4,68},{5,69},{6,70},{7,71},{8,72},{9,... | collective-permute-start | bytes 3145736 | tf_op jit(solution)/shard_map/ppermute | solution.py:255
  10.2 2.0 %collective-permute-start.4 = (bf16[128,512]{1,0:T(8,128)(2,1)S(1)}, bf16[128,512]{1,0:T(8,128)(2,1)S(1)}, u32[]{:S(2)}, u32[]{:S(2)}) collective-permute-start(bf16[128,512]{1,0:T(8,128)(2,1)S(1)} %get-tuple-element.24), channel_id=1, source_target_pairs={{0,16},{32,48},{64,80},{96,112},{128,144},{160,176},{192,208},{224... | collective-permute-start | bytes 393224 | tf_op jit(solution)/shard_map/ppermute | solution.py:255
  10.8 2.7 %collective-permute-start.5 = (bf16[128,512]{1,0:T(8,128)(2,1)S(1)}, bf16[128,512]{1,0:T(8,128)(2,1)S(1)}, u32[]{:S(2)}, u32[]{:S(2)}) collective-permute-start(bf16[128,512]{1,0:T(8,128)(2,1)S(1)} %get-tuple-element.25), channel_id=1, source_target_pairs={{0,8},{32,40},{64,72},{96,104},{128,136},{160,168},{192,200},{224,... | collective-permute-start | bytes 393224 | tf_op jit(solution)/shard_map/ppermute | solution.py:255
  11.5 2.1 %collective-permute-start.6 = (bf16[128,512]{1,0:T(8,128)(2,1)S(1)}, bf16[128,512]{1,0:T(8,128)(2,1)S(1)}, u32[]{:S(2)}, u32[]{:S(2)}) collective-permute-start(bf16[128,512]{1,0:T(8,128)(2,1)S(1)} %get-tuple-element.26), channel_id=1, source_target_pairs={{0,24},{32,56},{64,88},{96,120},{128,152},{160,184},{192,216},{224... | collective-permute-start | bytes 393224 | tf_op jit(solution)/shard_map/ppermute | solution.py:255
  12.2 32.3 %collective-permute-start.13 = (bf16[512,1024]{1,0:T(8,128)(2,1)S(1)}, bf16[512,1024]{1,0:T(8,128)(2,1)S(1)}, u32[]{:S(2)}, u32[]{:S(2)}) collective-permute-start(bf16[512,1024]{1,0:T(8,128)(2,1)S(1)} %copy-done), channel_id=1, source_target_pairs={{0,128},{1,129},{2,130},{3,131},{4,132},{5,133},{6,134},{7,135},{8... | collective-permute-start | bytes 3145736 | tf_op jit(solution)/shard_map/ppermute | solution.py:255
  13.6 1.4 %collective-permute-start.8 = (bf16[128,512]{1,0:T(8,128)(2,1)S(1)}, bf16[128,512]{1,0:T(8,128)(2,1)S(1)}, u32[]{:S(2)}, u32[]{:S(2)}) collective-permute-start(bf16[128,512]{1,0:T(8,128)(2,1)S(1)} %add_add_fusion.3), channel_id=1, source_target_pairs={{0,5},{8,13},{16,21},{24,29},{32,37},{40,45},{48,53},{56,61},{64,6... | collective-permute-start | bytes 393224 | tf_op jit(solution)/shard_map/ppermute | solution.py:255
  14.3 0.7 %collective-permute-start.7 = (bf16[128,512]{1,0:T(8,128)(2,1)S(1)}, bf16[128,512]{1,0:T(8,128)(2,1)S(1)}, u32[]{:S(2)}, u32[]{:S(2)}) collective-permute-start(bf16[128,512]{1,0:T(8,128)(2,1)S(1)} %add_add_fusion.3), channel_id=1, source_target_pairs={{0,3},{8,11},{16,19},{24,27},{32,35},{40,43},{48,51},{56,59},{64,6... | collective-permute-start | bytes 393224 | tf_op jit(solution)/shard_map/ppermute | solution.py:255
  21.7 22.8 %collective-permute-start.12 = (bf16[128,512]{1,0:T(8,128)(2,1)S(1)}, bf16[128,512]{1,0:T(8,128)(2,1)S(1)}, u32[]{:S(2)}, u32[]{:S(2)}) collective-permute-start(bf16[128,512]{1,0:T(8,128)(2,1)S(1)} %add_add_fusion.2), channel_id=1, source_target_pairs={{0,7},{8,15},{16,23},{24,31},{32,39},{40,47},{48,55},{56,63},{64,7... | collective-permute-start | bytes 393224 | tf_op jit(solution)/shard_map/ppermute | solution.py:255
  23.0 21.5 %collective-permute-start.11 = (bf16[128,512]{1,0:T(8,128)(2,1)S(1)}, bf16[128,512]{1,0:T(8,128)(2,1)S(1)}, u32[]{:S(2)}, u32[]{:S(2)}) collective-permute-start(bf16[128,512]{1,0:T(8,128)(2,1)S(1)} %add_add_fusion.2), channel_id=1, source_target_pairs={{0,1},{8,9},{16,17},{24,25},{32,33},{40,41},{48,49},{56,57},{64,65... | collective-permute-start | bytes 393224 | tf_op jit(solution)/shard_map/ppermute | solution.py:255
  44.7 11.4 %collective-permute-start.14 = (bf16[512,1024]{1,0:T(8,128)(2,1)S(1)}, bf16[512,1024]{1,0:T(8,128)(2,1)S(1)}, u32[]{:S(2)}, u32[]{:S(2)}) collective-permute-start(bf16[512,1024]{1,0:T(8,128)(2,1)S(1)} %shard_map.30.even_ref), channel_id=1, source_target_pairs={{0,32},{1,33},{2,34},{3,35},{4,36},{5,37},{6,38},{7,39},{8,40},{9,... | collective-permute-start | bytes 3145736 | tf_op jit(solution)/shard_map/ppermute | solution.py:255
  46.0 6.6 %collective-permute-start.17 = (bf16[128,512]{1,0:T(8,128)(2,1)S(1)}, bf16[128,512]{1,0:T(8,128)(2,1)S(1)}, u32[]{:S(2)}, u32[]{:S(2)}) collective-permute-start(bf16[128,512]{1,0:T(8,128)(2,1)S(1)} %add_add_fusion.1.q0_ref), channel_id=1, source_target_pairs={{0,16},{1,17},{2,18},{3,19},{4,20},{5,21},{6,22},{7,23},{32,48},{3... | collective-permute-start | bytes 393224 | tf_op jit(solution)/shard_map/ppermute | solution.py:255
  48.1 6.8 %collective-permute-start.16 = (bf16[128,512]{1,0:T(8,128)(2,1)S(1)}, bf16[128,512]{1,0:T(8,128)(2,1)S(1)}, u32[]{:S(2)}, u32[]{:S(2)}) collective-permute-start(bf16[128,512]{1,0:T(8,128)(2,1)S(1)} %add_add_fusion.1.q0_ref), channel_id=1, source_target_pairs={{0,24},{1,25},{2,26},{3,27},{4,28},{5,29},{6,30},{7,31},{32,56},{3... | collective-permute-start | bytes 393224 | tf_op jit(solution)/shard_map/ppermute | solution.py:255
  49.9 6.2 %collective-permute-start.15 = (bf16[128,512]{1,0:T(8,128)(2,1)S(1)}, bf16[128,512]{1,0:T(8,128)(2,1)S(1)}, u32[]{:S(2)}, u32[]{:S(2)}) collective-permute-start(bf16[128,512]{1,0:T(8,128)(2,1)S(1)} %add_add_fusion.1.q0_ref), channel_id=1, source_target_pairs={{0,8},{1,9},{2,10},{3,11},{4,12},{5,13},{6,14},{7,15},{32,40},{33,... | collective-permute-start | bytes 393224 | tf_op jit(solution)/shard_map/ppermute | solution.py:255

commit v5 on v4

--- a/solution.py
+++ b/solution.py
@@ -117,7 +117,7 @@
 
     @pl.when(holder)
     def _():
-        s = scales_ref[0, 0]
+        s = scales_ref[:1, :1]
         packed = low_ref[...] + swap_ref[...]
         t = [[None] * 4 for _ in range(4)]
         for j in range(4):
@@ -158,7 +158,7 @@
     return pl.pallas_call(
         solve_kernel,
         out_shape=[chunk] * 4,
-        in_specs=[pl.BlockSpec(memory_space=pltpu.SMEM)] + [vmem] * 3,
+        in_specs=[vmem] * 4,
         out_specs=[vmem] * 4,
         scratch_shapes=[pltpu.VMEM((NB, NB), F32)],
         compiler_params=pltpu.CompilerParams(vmem_limit_bytes=12 * 2**20),
@@ -193,42 +193,42 @@
 
 
 def update_kernel(
-    scales_ref, own_ref, even_ref, odd_ref, q0_ref, q1_ref, q3_ref, q2_ref, out_ref,
-    w_ref, result_ref, sems,
+    scales_ref, own_ref, even_ref, odd_ref, q0_ref, q1_ref, q3_ref, q2_ref, out_ref, result_ref, sems
 ):
     prow_at = lax.axis_index("prow")
     pcol_at = lax.axis_index("pcol")
-    for ref, shift in ((q0_ref, 0), (q1_ref, 3), (q3_ref, 1), (q2_ref, 2)):
-        row = pl.multiple_of(lax.rem(pcol_at // ZS + shift, XS) * 128, 128)
-        w_ref[pl.ds(row, 128), :] = ref[...]
-    copies = [
-        pltpu.make_async_copy(
-            result_ref.at[:, 256 * t : 256 * (t + 1)], out_ref.at[:, 256 * t : 256 * (t + 1)], sems.at[t]
-        )
-        for t in range(4)
-    ]
+    lanes = lax.broadcasted_iota(jnp.int32, (1, 2 * TILE_COLS), 1)
+    own_scales = scales_ref[pl.ds(prow_at, 1), :]
+    head_scales = scales_ref[:1, :]
+
+    def pick(row, col):
+        return jnp.sum(jnp.where(lanes == col, row, 0.0), axis=1, keepdims=True)
+
+    factors = []
+    for t in range(2):
+        col = TILE_COLS * t + pcol_at
+        value = (pick(own_scales, 0) * pick(head_scales, col)) / pick(own_scales, col)
+        factors.append(jnp.broadcast_to(value, (1, NB)))
+    factor = jnp.concatenate(factors, 1)
+    in_panel = (lax.broadcasted_iota(jnp.int32, (1, 2 * NB), 1) < NB) & (pcol_at == 0)
 
     def run(head_ref):
-        for t in range(4):
-            cols = slice(256 * t, 256 * (t + 1))
-            col = TILE_COLS * (t // 2) + pcol_at
-            scale = jnp.full((1, 256), scales_ref[prow_at, col], F32)
-            factor = (scales_ref[prow_at, 0] * scales_ref[0, col]) / scale
-            product = bdot(w_ref[...], head_ref[:, cols])
-            own = own_ref[:, cols]
+        copies = []
+        for at, (ref, shift) in enumerate(((q0_ref, 0), (q1_ref, 3), (q3_ref, 1), (q2_ref, 2))):
+            rows = pl.ds(pl.multiple_of(lax.rem(pcol_at // ZS + shift, XS) * 128, 128), 128)
+            product = bdot(ref[...], head_ref[...])
+            own = own_ref[rows, :]
             updated = (own.astype(F32) - factor * product).astype(BF)
             result = jnp.where(prow_at == 0, product.astype(BF), updated)
-            if t < 2:
-                result = jnp.where(pcol_at == 0, own, result)
-            result_ref[:, cols] = result
-            copies[t].start()
+            result_ref[at] = jnp.where(in_panel, own, result)
+            copies.append(pltpu.make_async_copy(result_ref.at[at], out_ref.at[rows, :], sems.at[at]))
+            copies[-1].start()
+        for copy in copies:
+            copy.wait()
 
     even = lax.rem(prow_at, 2) == 0
-    cases = ((even, even_ref), (jnp.logical_not(even), odd_ref))
-    for here, head_ref in cases:
-        pl.when(here)(functools.partial(run, head_ref))
-    for copy in copies:
-        copy.wait()
+    pl.when(even)(functools.partial(run, even_ref))
+    pl.when(jnp.logical_not(even))(functools.partial(run, odd_ref))
 
 
 def update(scales, own, heads, chunks):
@@ -236,12 +236,11 @@
     return pl.pallas_call(
         update_kernel,
         out_shape=jax.ShapeDtypeStruct((NB, 2 * NB), BF),
-        in_specs=[pl.BlockSpec(memory_space=pltpu.SMEM)] + [vmem] * 7,
+        in_specs=[vmem] * 8,
         out_specs=pl.BlockSpec(memory_space=pl.ANY),
         scratch_shapes=[
-            pltpu.VMEM((NB, NB), BF),
-            pltpu.VMEM((NB, 2 * NB), BF),
-            pltpu.SemaphoreType.DMA((4,)),
+            pltpu.VMEM((XS, 128, 2 * NB), BF),
+            pltpu.SemaphoreType.DMA((XS,)),
         ],
         compiler_params=pltpu.CompilerParams(vmem_limit_bytes=8 * 2**20),
         cost_estimate=pl.CostEstimate(flops=2**29, bytes_accessed=4 * 2**20, transcendentals=0),

time: 58.8 us -> 57.7 us (0.981)
  Pallas kernels: 3.14 us -> 2.02 us
    pallas_call x1, Pallas kernels: 0.65 us -> 0.05 us  [solve(): pl.pallas_call(solve_kernel, out_shape=[chunk] * 4, in_specs=[vmem] * 4,...]
  transfers between devices with their start and end apart: 18 -> 18, of which waited for: 6 -> 6; matrix products, arithmetic and copies ran while one was open for 0% -> 0% of each run, Pallas kernels for 1% -> 0%
where the time goes in v5:
time: 57.7 us; the launch traced here: 57.3 us
  waiting for transfers between devices  33.1 us (57%)
  starting transfers between devices  21.7 us (38%)
  Pallas kernels  2.02 us (4%)
    ppermute x18, waiting for transfers between devices, send(): return lax.ppermute(value, ('prow', 'pcol'), flat)  33.1 us
    ppermute x18, starting transfers between devices, send(): return lax.ppermute(value, ('prow', 'pcol'), flat)  21.7 us
    pallas_call x1, Pallas kernels, update(): pl.pallas_call(update_kernel, out_shape=jax.ShapeDtypeStruct((NB, 2 * NB)...  1.78 us
  transfers between devices with their start and end apart: 18, of which 6 were waited for; matrix products, arithmetic and copies ran while one was open for 0% of the time, Pallas kernels for 0%

profile of v5, /device:TPU:64, one launch (start us, length us, event | category | flops | bytes accessed | tf_op | source)
XLA Modules:
  0.0 57.3 jit_solution(4841875021300023009)
XLA Ops:
  0.0 0.1 shard_map.28
  0.1 0.0 copy-start
  0.1 0.8 %collective-permute-start.2 = (bf16[320,512]{1,0:T(8,128)(2,1)S(1)}, bf16[320,512]{1,0:T(8,128)(2,1)S(1)}, u32[]{:S(2)}, u32[]{:S(2)}) collective-permute-start(bf16[320,512]{1,0:T(8,128)(2,1)S(1)} %shard_map.28), channel_id=1, source_target_pairs={{0,128}} | collective-permute-start | bytes 983048 | tf_op jit(solution)/shard_map/ppermute | solution.py:254
  0.9 0.7 %collective-permute-start.1 = (bf16[320,512]{1,0:T(8,128)(2,1)S(1)}, bf16[320,512]{1,0:T(8,128)(2,1)S(1)}, u32[]{:S(2)}, u32[]{:S(2)}) collective-permute-start(bf16[320,512]{1,0:T(8,128)(2,1)S(1)} %shard_map.28), channel_id=1, source_target_pairs={{0,192}} | collective-permute-start | bytes 983048 | tf_op jit(solution)/shard_map/ppermute | solution.py:254
  1.6 0.7 %collective-permute-start = (bf16[320,512]{1,0:T(8,128)(2,1)S(1)}, bf16[320,512]{1,0:T(8,128)(2,1)S(1)}, u32[]{:S(2)}, u32[]{:S(2)}) collective-permute-start(bf16[320,512]{1,0:T(8,128)(2,1)S(1)} %shard_map.28), channel_id=1, source_target_pairs={{0,64}} | collective-permute-start | bytes 983048 | tf_op jit(solution)/shard_map/ppermute | solution.py:254
  2.3 0.0 collective-permute-done.2
  2.3 0.0 collective-permute-done.1
  2.3 0.0 collective-permute-done
  2.3 0.0 copy-start.1
  2.4 0.1 broadcast_select_fusion
  2.4 0.7 %collective-permute-start.3 = (bf16[320,512]{1,0:T(8,128)(2,1)S(1)}, bf16[320,512]{1,0:T(8,128)(2,1)S(1)}, u32[]{:S(2)}, u32[]{:S(2)}) collective-permute-start(bf16[320,512]{1,0:T(8,128)(2,1)S(1)} %get-tuple-element.36), channel_id=1, source_target_pairs={{0,32},{32,0},{64,96},{96,64},{128,160},{160,128},{192,224},{224,1... | collective-permute-start | bytes 983048 | tf_op jit(solution)/shard_map/ppermute | solution.py:254
  3.1 0.0 copy-done
  3.1 5.0 %collective-permute-start.10 = (bf16[512,1024]{1,0:T(8,128)(2,1)S(1)}, bf16[512,1024]{1,0:T(8,128)(2,1)S(1)}, u32[]{:S(2)}, u32[]{:S(2)}) collective-permute-start(bf16[512,1024]{1,0:T(8,128)(2,1)S(1)} %copy-done), channel_id=1, source_target_pairs={{0,192},{1,193},{2,194},{3,195},{4,196},{5,197},{6,198},{7,199},{8... | collective-permute-start | bytes 3145736 | tf_op jit(solution)/shard_map/ppermute | solution.py:254
  8.1 1.4 %collective-permute-start.9 = (bf16[512,1024]{1,0:T(8,128)(2,1)S(1)}, bf16[512,1024]{1,0:T(8,128)(2,1)S(1)}, u32[]{:S(2)}, u32[]{:S(2)}) collective-permute-start(bf16[512,1024]{1,0:T(8,128)(2,1)S(1)} %copy-done), channel_id=1, source_target_pairs={{0,64},{1,65},{2,66},{3,67},{4,68},{5,69},{6,70},{7,71},{8,72},{9,... | collective-permute-start | bytes 3145736 | tf_op jit(solution)/shard_map/ppermute | solution.py:254
  9.5 0.0 collective-permute-done.3.swap_ref
  9.5 0.0 copy-done.1
  9.5 0.1 shard_map.29
  9.6 0.7 %collective-permute-start.4 = (bf16[128,512]{1,0:T(8,128)(2,1)S(1)}, bf16[128,512]{1,0:T(8,128)(2,1)S(1)}, u32[]{:S(2)}, u32[]{:S(2)}) collective-permute-start(bf16[128,512]{1,0:T(8,128)(2,1)S(1)} %get-tuple-element.24), channel_id=1, source_target_pairs={{0,16},{32,48},{64,80},{96,112},{128,144},{160,176},{192,208},{224... | collective-permute-start | bytes 393224 | tf_op jit(solution)/shard_map/ppermute | solution.py:254
  10.3 0.7 %collective-permute-start.5 = (bf16[128,512]{1,0:T(8,128)(2,1)S(1)}, bf16[128,512]{1,0:T(8,128)(2,1)S(1)}, u32[]{:S(2)}, u32[]{:S(2)}) collective-permute-start(bf16[128,512]{1,0:T(8,128)(2,1)S(1)} %get-tuple-element.25), channel_id=1, source_target_pairs={{0,8},{32,40},{64,72},{96,104},{128,136},{160,168},{192,200},{224,... | collective-permute-start | bytes 393224 | tf_op jit(solution)/shard_map/ppermute | solution.py:254
  10.9 0.7 %collective-permute-start.6 = (bf16[128,512]{1,0:T(8,128)(2,1)S(1)}, bf16[128,512]{1,0:T(8,128)(2,1)S(1)}, u32[]{:S(2)}, u32[]{:S(2)}) collective-permute-start(bf16[128,512]{1,0:T(8,128)(2,1)S(1)} %get-tuple-element.26), channel_id=1, source_target_pairs={{0,24},{32,56},{64,88},{96,120},{128,152},{160,184},{192,216},{224... | collective-permute-start | bytes 393224 | tf_op jit(solution)/shard_map/ppermute | solution.py:254
  11.6 0.0 collective-permute-done.4
  11.6 1.4 %collective-permute-start.13 = (bf16[512,1024]{1,0:T(8,128)(2,1)S(1)}, bf16[512,1024]{1,0:T(8,128)(2,1)S(1)}, u32[]{:S(2)}, u32[]{:S(2)}) collective-permute-start(bf16[512,1024]{1,0:T(8,128)(2,1)S(1)} %copy-done), channel_id=1, source_target_pairs={{0,128},{1,129},{2,130},{3,131},{4,132},{5,133},{6,134},{7,135},{8... | collective-permute-start | bytes 3145736 | tf_op jit(solution)/shard_map/ppermute | solution.py:254
  13.0 0.0 collective-permute-done.5
  13.0 0.0 collective-permute-done.6
  13.0 0.7 %collective-permute-start.8 = (bf16[128,512]{1,0:T(8,128)(2,1)S(1)}, bf16[128,512]{1,0:T(8,128)(2,1)S(1)}, u32[]{:S(2)}, u32[]{:S(2)}) collective-permute-start(bf16[128,512]{1,0:T(8,128)(2,1)S(1)} %add_add_fusion.3), channel_id=1, source_target_pairs={{0,5},{8,13},{16,21},{24,29},{32,37},{40,45},{48,53},{56,61},{64,6... | collective-permute-start | bytes 393224 | tf_op jit(solution)/shard_map/ppermute | solution.py:254
  13.7 0.7 %collective-permute-start.7 = (bf16[128,512]{1,0:T(8,128)(2,1)S(1)}, bf16[128,512]{1,0:T(8,128)(2,1)S(1)}, u32[]{:S(2)}, u32[]{:S(2)}) collective-permute-start(bf16[128,512]{1,0:T(8,128)(2,1)S(1)} %add_add_fusion.3), channel_id=1, source_target_pairs={{0,3},{8,11},{16,19},{24,27},{32,35},{40,43},{48,51},{56,59},{64,6... | collective-permute-start | bytes 393224 | tf_op jit(solution)/shard_map/ppermute | solution.py:254
  14.4 0.0 collective-permute-done.8
  14.4 0.0 collective-permute-done.7
  14.4 5.9 %collective-permute-done.10.y6_ref = bf16[512,1024]{1,0:T(8,128)(2,1)S(1)} collective-permute-done((bf16[512,1024]{1,0:T(8,128)(2,1)S(1)}, bf16[512,1024]{1,0:T(8,128)(2,1)S(1)}, u32[]{:S(2)}, u32[]{:S(2)}) %collective-permute-start.10) | collective-permute-done | bytes 1048608 | tf_op jit(solution)/shard_map/ppermute | solution.py:254
  20.4 1.4 %collective-permute-done.9.y2_ref = bf16[512,1024]{1,0:T(8,128)(2,1)S(1)} collective-permute-done((bf16[512,1024]{1,0:T(8,128)(2,1)S(1)}, bf16[512,1024]{1,0:T(8,128)(2,1)S(1)}, u32[]{:S(2)}, u32[]{:S(2)}) %collective-permute-start.9) | collective-permute-done | bytes 1048608 | tf_op jit(solution)/shard_map/ppermute | solution.py:254
  21.7 1.3 %collective-permute-start.12 = (bf16[128,512]{1,0:T(8,128)(2,1)S(1)}, bf16[128,512]{1,0:T(8,128)(2,1)S(1)}, u32[]{:S(2)}, u32[]{:S(2)}) collective-permute-start(bf16[128,512]{1,0:T(8,128)(2,1)S(1)} %add_add_fusion.2), channel_id=1, source_target_pairs={{0,7},{8,15},{16,23},{24,31},{32,39},{40,47},{48,55},{56,63},{64,7... | collective-permute-start | bytes 393224 | tf_op jit(solution)/shard_map/ppermute | solution.py:254
  23.0 0.7 %collective-permute-start.11 = (bf16[128,512]{1,0:T(8,128)(2,1)S(1)}, bf16[128,512]{1,0:T(8,128)(2,1)S(1)}, u32[]{:S(2)}, u32[]{:S(2)}) collective-permute-start(bf16[128,512]{1,0:T(8,128)(2,1)S(1)} %add_add_fusion.2), channel_id=1, source_target_pairs={{0,1},{8,9},{16,17},{24,25},{32,33},{40,41},{48,49},{56,57},{64,65... | collective-permute-start | bytes 393224 | tf_op jit(solution)/shard_map/ppermute | solution.py:254
  23.7 20.2 %collective-permute-done.12 = bf16[128,512]{1,0:T(8,128)(2,1)S(1)} collective-permute-done((bf16[128,512]{1,0:T(8,128)(2,1)S(1)}, bf16[128,512]{1,0:T(8,128)(2,1)S(1)}, u32[]{:S(2)}, u32[]{:S(2)}) %collective-permute-start.12) | collective-permute-done | bytes 131104 | tf_op jit(solution)/shard_map/ppermute | solution.py:254
  43.9 0.0 collective-permute-done.11
  43.9 0.0 collective-permute-done.13.y4_ref
  44.0 0.1 shard_map.30.even_ref
  44.1 1.4 %collective-permute-start.14 = (bf16[512,1024]{1,0:T(8,128)(2,1)S(1)}, bf16[512,1024]{1,0:T(8,128)(2,1)S(1)}, u32[]{:S(2)}, u32[]{:S(2)}) collective-permute-start(bf16[512,1024]{1,0:T(8,128)(2,1)S(1)} %shard_map.30.even_ref), channel_id=1, source_target_pairs={{0,32},{1,33},{2,34},{3,35},{4,36},{5,37},{6,38},{7,39},{8,40},{9,... | collective-permute-start | bytes 3145736 | tf_op jit(solution)/shard_map/ppermute | solution.py:254
  45.4 2.1 %collective-permute-start.17 = (bf16[128,512]{1,0:T(8,128)(2,1)S(1)}, bf16[128,512]{1,0:T(8,128)(2,1)S(1)}, u32[]{:S(2)}, u32[]{:S(2)}) collective-permute-start(bf16[128,512]{1,0:T(8,128)(2,1)S(1)} %add_add_fusion.1.q0_ref), channel_id=1, source_target_pairs={{0,16},{1,17},{2,18},{3,19},{4,20},{5,21},{6,22},{7,23},{32,48},{3... | collective-permute-start | bytes 393224 | tf_op jit(solution)/shard_map/ppermute | solution.py:254
  47.5 1.8 %collective-permute-start.16 = (bf16[128,512]{1,0:T(8,128)(2,1)S(1)}, bf16[128,512]{1,0:T(8,128)(2,1)S(1)}, u32[]{:S(2)}, u32[]{:S(2)}) collective-permute-start(bf16[128,512]{1,0:T(8,128)(2,1)S(1)} %add_add_fusion.1.q0_ref), channel_id=1, source_target_pairs={{0,24},{1,25},{2,26},{3,27},{4,28},{5,29},{6,30},{7,31},{32,56},{3... | collective-permute-start | bytes 393224 | tf_op jit(solution)/shard_map/ppermute | solution.py:254
  49.3 0.6 %collective-permute-start.15 = (bf16[128,512]{1,0:T(8,128)(2,1)S(1)}, bf16[128,512]{1,0:T(8,128)(2,1)S(1)}, u32[]{:S(2)}, u32[]{:S(2)}) collective-permute-start(bf16[128,512]{1,0:T(8,128)(2,1)S(1)} %add_add_fusion.1.q0_ref), channel_id=1, source_target_pairs={{0,8},{1,9},{2,10},{3,11},{4,12},{5,13},{6,14},{7,15},{32,40},{33,... | collective-permute-start | bytes 393224 | tf_op jit(solution)/shard_map/ppermute | solution.py:254
  49.9 2.1 %collective-permute-done.17.q2_ref = bf16[128,512]{1,0:T(8,128)(2,1)S(1)} collective-permute-done((bf16[128,512]{1,0:T(8,128)(2,1)S(1)}, bf16[128,512]{1,0:T(8,128)(2,1)S(1)}, u32[]{:S(2)}, u32[]{:S(2)}) %collective-permute-start.17) | collective-permute-done | bytes 131104 | tf_op jit(solution)/shard_map/ppermute | solution.py:254
  52.0 2.3 %collective-permute-done.16.q3_ref = bf16[128,512]{1,0:T(8,128)(2,1)S(1)} collective-permute-done((bf16[128,512]{1,0:T(8,128)(2,1)S(1)}, bf16[128,512]{1,0:T(8,128)(2,1)S(1)}, u32[]{:S(2)}, u32[]{:S(2)}) %collective-permute-start.16) | collective-permute-done | bytes 131104 | tf_op jit(solution)/shard_map/ppermute | solution.py:254
  54.3 1.2 %collective-permute-done.15.q1_ref = bf16[128,512]{1,0:T(8,128)(2,1)S(1)} collective-permute-done((bf16[128,512]{1,0:T(8,128)(2,1)S(1)}, bf16[128,512]{1,0:T(8,128)(2,1)S(1)}, u32[]{:S(2)}, u32[]{:S(2)}) %collective-permute-start.15) | collective-permute-done | bytes 131104 | tf_op jit(solution)/shard_map/ppermute | solution.py:254
  55.5 0.0 collective-permute-done.14.odd_ref
  55.5 1.8 %shard_map.31 = bf16[512,1024]{1,0:T(8,128)(2,1)} custom-call(f32[8,64]{1,0:T(8,128)S(1)} %copy-done.1, bf16[512,1024]{1,0:T(8,128)(2,1)S(1)} %copy-done, bf16[512,1024]{1,0:T(8,128)(2,1)S(1)} %shard_map.30.even_ref, bf16[512,1024]{1,0:T(8,128)(2,1)S(1)} %collective-permute-done.14.odd_ref, bf16[128,512]{1,0:T(8,128)(2,1)S(1)} %add_add_fusion.1.q0_ref, ...), custom_call_target="tpu_custom_call" | custom-call | flops 536870912 | bytes 4194304 | tf_op jit(solution)/shard_map/pallas_call | solution.py:236
  (3 shorter events, 0.1 us)
Async XLA Ops:
  0.1 3.0 %copy-start = (bf16[512,1024]{1,0:T(8,128)(2,1)S(1)}, bf16[512,1024]{1,0:T(8,128)(2,1)}, u32[]{:S(2)}) copy-start(bf16[512,1024]{1,0:T(8,128)(2,1)} %own_ref.3) | copy-start | bytes 3145732
  0.1 2.2 %collective-permute-start.2 = (bf16[320,512]{1,0:T(8,128)(2,1)S(1)}, bf16[320,512]{1,0:T(8,128)(2,1)S(1)}, u32[]{:S(2)}, u32[]{:S(2)}) collective-permute-start(bf16[320,512]{1,0:T(8,128)(2,1)S(1)} %shard_map.28), channel_id=1, source_target_pairs={{0,128}} | collective-permute-start | bytes 983048 | tf_op jit(solution)/shard_map/ppermute | solution.py:254
  0.9 1.4 %collective-permute-start.1 = (bf16[320,512]{1,0:T(8,128)(2,1)S(1)}, bf16[320,512]{1,0:T(8,128)(2,1)S(1)}, u32[]{:S(2)}, u32[]{:S(2)}) collective-permute-start(bf16[320,512]{1,0:T(8,128)(2,1)S(1)} %shard_map.28), channel_id=1, source_target_pairs={{0,192}} | collective-permute-start | bytes 983048 | tf_op jit(solution)/shard_map/ppermute | solution.py:254
  1.6 0.7 %collective-permute-start = (bf16[320,512]{1,0:T(8,128)(2,1)S(1)}, bf16[320,512]{1,0:T(8,128)(2,1)S(1)}, u32[]{:S(2)}, u32[]{:S(2)}) collective-permute-start(bf16[320,512]{1,0:T(8,128)(2,1)S(1)} %shard_map.28), channel_id=1, source_target_pairs={{0,64}} | collective-permute-start | bytes 983048 | tf_op jit(solution)/shard_map/ppermute | solution.py:254
  2.3 7.2 %copy-start.1 = (f32[8,64]{1,0:T(8,128)S(1)}, f32[8,64]{1,0:T(8,128)}, u32[]{:S(2)}) copy-start(f32[8,64]{1,0:T(8,128)} %scales_ref.3) | copy-start | bytes 6148
  2.4 7.1 %collective-permute-start.3 = (bf16[320,512]{1,0:T(8,128)(2,1)S(1)}, bf16[320,512]{1,0:T(8,128)(2,1)S(1)}, u32[]{:S(2)}, u32[]{:S(2)}) collective-permute-start(bf16[320,512]{1,0:T(8,128)(2,1)S(1)} %get-tuple-element.36), channel_id=1, source_target_pairs={{0,32},{32,0},{64,96},{96,64},{128,160},{160,128},{192,224},{224,1... | collective-permute-start | bytes 983048 | tf_op jit(solution)/shard_map/ppermute | solution.py:254
  3.1 17.2 %collective-permute-start.10 = (bf16[512,1024]{1,0:T(8,128)(2,1)S(1)}, bf16[512,1024]{1,0:T(8,128)(2,1)S(1)}, u32[]{:S(2)}, u32[]{:S(2)}) collective-permute-start(bf16[512,1024]{1,0:T(8,128)(2,1)S(1)} %copy-done), channel_id=1, source_target_pairs={{0,192},{1,193},{2,194},{3,195},{4,196},{5,197},{6,198},{7,199},{8... | collective-permute-start | bytes 3145736 | tf_op jit(solution)/shard_map/ppermute | solution.py:254
  8.1 13.6 %collective-permute-start.9 = (bf16[512,1024]{1,0:T(8,128)(2,1)S(1)}, bf16[512,1024]{1,0:T(8,128)(2,1)S(1)}, u32[]{:S(2)}, u32[]{:S(2)}) collective-permute-start(bf16[512,1024]{1,0:T(8,128)(2,1)S(1)} %copy-done), channel_id=1, source_target_pairs={{0,64},{1,65},{2,66},{3,67},{4,68},{5,69},{6,70},{7,71},{8,72},{9,... | collective-permute-start | bytes 3145736 | tf_op jit(solution)/shard_map/ppermute | solution.py:254
  9.6 2.0 %collective-permute-start.4 = (bf16[128,512]{1,0:T(8,128)(2,1)S(1)}, bf16[128,512]{1,0:T(8,128)(2,1)S(1)}, u32[]{:S(2)}, u32[]{:S(2)}) collective-permute-start(bf16[128,512]{1,0:T(8,128)(2,1)S(1)} %get-tuple-element.24), channel_id=1, source_target_pairs={{0,16},{32,48},{64,80},{96,112},{128,144},{160,176},{192,208},{224... | collective-permute-start | bytes 393224 | tf_op jit(solution)/shard_map/ppermute | solution.py:254
  10.3 2.7 %collective-permute-start.5 = (bf16[128,512]{1,0:T(8,128)(2,1)S(1)}, bf16[128,512]{1,0:T(8,128)(2,1)S(1)}, u32[]{:S(2)}, u32[]{:S(2)}) collective-permute-start(bf16[128,512]{1,0:T(8,128)(2,1)S(1)} %get-tuple-element.25), channel_id=1, source_target_pairs={{0,8},{32,40},{64,72},{96,104},{128,136},{160,168},{192,200},{224,... | collective-permute-start | bytes 393224 | tf_op jit(solution)/shard_map/ppermute | solution.py:254
  10.9 2.1 %collective-permute-start.6 = (bf16[128,512]{1,0:T(8,128)(2,1)S(1)}, bf16[128,512]{1,0:T(8,128)(2,1)S(1)}, u32[]{:S(2)}, u32[]{:S(2)}) collective-permute-start(bf16[128,512]{1,0:T(8,128)(2,1)S(1)} %get-tuple-element.26), channel_id=1, source_target_pairs={{0,24},{32,56},{64,88},{96,120},{128,152},{160,184},{192,216},{224... | collective-permute-start | bytes 393224 | tf_op jit(solution)/shard_map/ppermute | solution.py:254
  11.6 32.3 %collective-permute-start.13 = (bf16[512,1024]{1,0:T(8,128)(2,1)S(1)}, bf16[512,1024]{1,0:T(8,128)(2,1)S(1)}, u32[]{:S(2)}, u32[]{:S(2)}) collective-permute-start(bf16[512,1024]{1,0:T(8,128)(2,1)S(1)} %copy-done), channel_id=1, source_target_pairs={{0,128},{1,129},{2,130},{3,131},{4,132},{5,133},{6,134},{7,135},{8... | collective-permute-start | bytes 3145736 | tf_op jit(solution)/shard_map/ppermute | solution.py:254
  13.0 1.4 %collective-permute-start.8 = (bf16[128,512]{1,0:T(8,128)(2,1)S(1)}, bf16[128,512]{1,0:T(8,128)(2,1)S(1)}, u32[]{:S(2)}, u32[]{:S(2)}) collective-permute-start(bf16[128,512]{1,0:T(8,128)(2,1)S(1)} %add_add_fusion.3), channel_id=1, source_target_pairs={{0,5},{8,13},{16,21},{24,29},{32,37},{40,45},{48,53},{56,61},{64,6... | collective-permute-start | bytes 393224 | tf_op jit(solution)/shard_map/ppermute | solution.py:254
  13.7 0.7 %collective-permute-start.7 = (bf16[128,512]{1,0:T(8,128)(2,1)S(1)}, bf16[128,512]{1,0:T(8,128)(2,1)S(1)}, u32[]{:S(2)}, u32[]{:S(2)}) collective-permute-start(bf16[128,512]{1,0:T(8,128)(2,1)S(1)} %add_add_fusion.3), channel_id=1, source_target_pairs={{0,3},{8,11},{16,19},{24,27},{32,35},{40,43},{48,51},{56,59},{64,6... | collective-permute-start | bytes 393224 | tf_op jit(solution)/shard_map/ppermute | solution.py:254
  21.7 22.2 %collective-permute-start.12 = (bf16[128,512]{1,0:T(8,128)(2,1)S(1)}, bf16[128,512]{1,0:T(8,128)(2,1)S(1)}, u32[]{:S(2)}, u32[]{:S(2)}) collective-permute-start(bf16[128,512]{1,0:T(8,128)(2,1)S(1)} %add_add_fusion.2), channel_id=1, source_target_pairs={{0,7},{8,15},{16,23},{24,31},{32,39},{40,47},{48,55},{56,63},{64,7... | collective-permute-start | bytes 393224 | tf_op jit(solution)/shard_map/ppermute | solution.py:254
  23.0 20.9 %collective-permute-start.11 = (bf16[128,512]{1,0:T(8,128)(2,1)S(1)}, bf16[128,512]{1,0:T(8,128)(2,1)S(1)}, u32[]{:S(2)}, u32[]{:S(2)}) collective-permute-start(bf16[128,512]{1,0:T(8,128)(2,1)S(1)} %add_add_fusion.2), channel_id=1, source_target_pairs={{0,1},{8,9},{16,17},{24,25},{32,33},{40,41},{48,49},{56,57},{64,65... | collective-permute-start | bytes 393224 | tf_op jit(solution)/shard_map/ppermute | solution.py:254
  44.1 11.4 %collective-permute-start.14 = (bf16[512,1024]{1,0:T(8,128)(2,1)S(1)}, bf16[512,1024]{1,0:T(8,128)(2,1)S(1)}, u32[]{:S(2)}, u32[]{:S(2)}) collective-permute-start(bf16[512,1024]{1,0:T(8,128)(2,1)S(1)} %shard_map.30.even_ref), channel_id=1, source_target_pairs={{0,32},{1,33},{2,34},{3,35},{4,36},{5,37},{6,38},{7,39},{8,40},{9,... | collective-permute-start | bytes 3145736 | tf_op jit(solution)/shard_map/ppermute | solution.py:254
  45.4 6.6 %collective-permute-start.17 = (bf16[128,512]{1,0:T(8,128)(2,1)S(1)}, bf16[128,512]{1,0:T(8,128)(2,1)S(1)}, u32[]{:S(2)}, u32[]{:S(2)}) collective-permute-start(bf16[128,512]{1,0:T(8,128)(2,1)S(1)} %add_add_fusion.1.q0_ref), channel_id=1, source_target_pairs={{0,16},{1,17},{2,18},{3,19},{4,20},{5,21},{6,22},{7,23},{32,48},{3... | collective-permute-start | bytes 393224 | tf_op jit(solution)/shard_map/ppermute | solution.py:254
  47.5 6.8 %collective-permute-start.16 = (bf16[128,512]{1,0:T(8,128)(2,1)S(1)}, bf16[128,512]{1,0:T(8,128)(2,1)S(1)}, u32[]{:S(2)}, u32[]{:S(2)}) collective-permute-start(bf16[128,512]{1,0:T(8,128)(2,1)S(1)} %add_add_fusion.1.q0_ref), channel_id=1, source_target_pairs={{0,24},{1,25},{2,26},{3,27},{4,28},{5,29},{6,30},{7,31},{32,56},{3... | collective-permute-start | bytes 393224 | tf_op jit(solution)/shard_map/ppermute | solution.py:254
  49.3 6.2 %collective-permute-start.15 = (bf16[128,512]{1,0:T(8,128)(2,1)S(1)}, bf16[128,512]{1,0:T(8,128)(2,1)S(1)}, u32[]{:S(2)}, u32[]{:S(2)}) collective-permute-start(bf16[128,512]{1,0:T(8,128)(2,1)S(1)} %add_add_fusion.1.q0_ref), channel_id=1, source_target_pairs={{0,8},{1,9},{2,10},{3,11},{4,12},{5,13},{6,14},{7,15},{32,40},{33,... | collective-permute-start | bytes 393224 | tf_op jit(solution)/shard_map/ppermute | solution.py:254

commit v6 on v5

--- a/solution.py
+++ b/solution.py
@@ -29,16 +29,20 @@
     return high, mid, low
 
 
+def joined(left, right):
+    return bdot(jnp.concatenate(left, 1), jnp.concatenate(right, 0))
+
+
 def dot_exact_left(t, x):
     high, mid, low = split3(x)
-    return bdot(t, high) + (bdot(t, mid) + bdot(t, low))
+    return joined([t, t], [high, mid]) + bdot(t, low)
 
 
 def dot_full(a, b):
     ah, am, al = split3(a)
     bh, bm, bl = split3(b)
-    return bdot(ah, bh) + (
-        (bdot(ah, bm) + bdot(am, bh)) + (bdot(am, bm) + (bdot(ah, bl) + bdot(al, bh)))
+    return joined([ah, ah], [bh, bm]) + (
+        joined([am, ah], [bh, bl]) + joined([am, al], [bm, bh])
     )
 
 

time: 57.7 us -> 57.7 us (level)
  no operation moved by 1% of the time
where the time goes in v6:
time: 57.7 us; the launch traced here: 57.3 us
  waiting for transfers between devices  33.1 us (57%)
  starting transfers between devices  21.7 us (38%)
  Pallas kernels  2.01 us (3%)
    ppermute x18, waiting for transfers between devices, send(): return lax.ppermute(value, ('prow', 'pcol'), flat)  33.1 us
    ppermute x18, starting transfers between devices, send(): return lax.ppermute(value, ('prow', 'pcol'), flat)  21.7 us
    pallas_call x1, Pallas kernels, update(): pl.pallas_call(update_kernel, out_shape=jax.ShapeDtypeStruct((NB, 2 * NB)...  1.78 us
  transfers between devices with their start and end apart: 18, of which 6 were waited for; matrix products, arithmetic and copies ran while one was open for 0% of the time, Pallas kernels for 0%

profile of v6, /device:TPU:64, one launch (start us, length us, event | category | flops | bytes accessed | tf_op | source)
XLA Modules:
  0.0 57.3 jit_solution(14165392552818231072)
XLA Ops:
  0.0 0.1 shard_map.28
  0.1 0.0 copy-start
  0.1 0.8 %collective-permute-start.2 = (bf16[320,512]{1,0:T(8,128)(2,1)S(1)}, bf16[320,512]{1,0:T(8,128)(2,1)S(1)}, u32[]{:S(2)}, u32[]{:S(2)}) collective-permute-start(bf16[320,512]{1,0:T(8,128)(2,1)S(1)} %shard_map.28), channel_id=1, source_target_pairs={{0,128}} | collective-permute-start | bytes 983048 | tf_op jit(solution)/shard_map/ppermute | solution.py:258
  0.9 0.7 %collective-permute-start.1 = (bf16[320,512]{1,0:T(8,128)(2,1)S(1)}, bf16[320,512]{1,0:T(8,128)(2,1)S(1)}, u32[]{:S(2)}, u32[]{:S(2)}) collective-permute-start(bf16[320,512]{1,0:T(8,128)(2,1)S(1)} %shard_map.28), channel_id=1, source_target_pairs={{0,192}} | collective-permute-start | bytes 983048 | tf_op jit(solution)/shard_map/ppermute | solution.py:258
  1.6 0.7 %collective-permute-start = (bf16[320,512]{1,0:T(8,128)(2,1)S(1)}, bf16[320,512]{1,0:T(8,128)(2,1)S(1)}, u32[]{:S(2)}, u32[]{:S(2)}) collective-permute-start(bf16[320,512]{1,0:T(8,128)(2,1)S(1)} %shard_map.28), channel_id=1, source_target_pairs={{0,64}} | collective-permute-start | bytes 983048 | tf_op jit(solution)/shard_map/ppermute | solution.py:258
  2.3 0.0 collective-permute-done.2
  2.3 0.0 collective-permute-done.1
  2.3 0.0 collective-permute-done
  2.3 0.0 copy-start.1
  2.4 0.1 broadcast_select_fusion
  2.4 0.7 %collective-permute-start.3 = (bf16[320,512]{1,0:T(8,128)(2,1)S(1)}, bf16[320,512]{1,0:T(8,128)(2,1)S(1)}, u32[]{:S(2)}, u32[]{:S(2)}) collective-permute-start(bf16[320,512]{1,0:T(8,128)(2,1)S(1)} %get-tuple-element.36), channel_id=1, source_target_pairs={{0,32},{32,0},{64,96},{96,64},{128,160},{160,128},{192,224},{224,1... | collective-permute-start | bytes 983048 | tf_op jit(solution)/shard_map/ppermute | solution.py:258
  3.1 0.0 copy-done
  3.1 5.0 %collective-permute-start.10 = (bf16[512,1024]{1,0:T(8,128)(2,1)S(1)}, bf16[512,1024]{1,0:T(8,128)(2,1)S(1)}, u32[]{:S(2)}, u32[]{:S(2)}) collective-permute-start(bf16[512,1024]{1,0:T(8,128)(2,1)S(1)} %copy-done), channel_id=1, source_target_pairs={{0,192},{1,193},{2,194},{3,195},{4,196},{5,197},{6,198},{7,199},{8... | collective-permute-start | bytes 3145736 | tf_op jit(solution)/shard_map/ppermute | solution.py:258
  8.1 1.4 %collective-permute-start.9 = (bf16[512,1024]{1,0:T(8,128)(2,1)S(1)}, bf16[512,1024]{1,0:T(8,128)(2,1)S(1)}, u32[]{:S(2)}, u32[]{:S(2)}) collective-permute-start(bf16[512,1024]{1,0:T(8,128)(2,1)S(1)} %copy-done), channel_id=1, source_target_pairs={{0,64},{1,65},{2,66},{3,67},{4,68},{5,69},{6,70},{7,71},{8,72},{9,... | collective-permute-start | bytes 3145736 | tf_op jit(solution)/shard_map/ppermute | solution.py:258
  9.5 0.0 collective-permute-done.3.swap_ref
  9.5 0.0 copy-done.1
  9.5 0.1 shard_map.29
  9.6 0.7 %collective-permute-start.4 = (bf16[128,512]{1,0:T(8,128)(2,1)S(1)}, bf16[128,512]{1,0:T(8,128)(2,1)S(1)}, u32[]{:S(2)}, u32[]{:S(2)}) collective-permute-start(bf16[128,512]{1,0:T(8,128)(2,1)S(1)} %get-tuple-element.24), channel_id=1, source_target_pairs={{0,16},{32,48},{64,80},{96,112},{128,144},{160,176},{192,208},{224... | collective-permute-start | bytes 393224 | tf_op jit(solution)/shard_map/ppermute | solution.py:258
  10.3 0.7 %collective-permute-start.5 = (bf16[128,512]{1,0:T(8,128)(2,1)S(1)}, bf16[128,512]{1,0:T(8,128)(2,1)S(1)}, u32[]{:S(2)}, u32[]{:S(2)}) collective-permute-start(bf16[128,512]{1,0:T(8,128)(2,1)S(1)} %get-tuple-element.25), channel_id=1, source_target_pairs={{0,8},{32,40},{64,72},{96,104},{128,136},{160,168},{192,200},{224,... | collective-permute-start | bytes 393224 | tf_op jit(solution)/shard_map/ppermute | solution.py:258
  10.9 0.7 %collective-permute-start.6 = (bf16[128,512]{1,0:T(8,128)(2,1)S(1)}, bf16[128,512]{1,0:T(8,128)(2,1)S(1)}, u32[]{:S(2)}, u32[]{:S(2)}) collective-permute-start(bf16[128,512]{1,0:T(8,128)(2,1)S(1)} %get-tuple-element.26), channel_id=1, source_target_pairs={{0,24},{32,56},{64,88},{96,120},{128,152},{160,184},{192,216},{224... | collective-permute-start | bytes 393224 | tf_op jit(solution)/shard_map/ppermute | solution.py:258
  11.6 0.0 collective-permute-done.4
  11.6 1.4 %collective-permute-start.13 = (bf16[512,1024]{1,0:T(8,128)(2,1)S(1)}, bf16[512,1024]{1,0:T(8,128)(2,1)S(1)}, u32[]{:S(2)}, u32[]{:S(2)}) collective-permute-start(bf16[512,1024]{1,0:T(8,128)(2,1)S(1)} %copy-done), channel_id=1, source_target_pairs={{0,128},{1,129},{2,130},{3,131},{4,132},{5,133},{6,134},{7,135},{8... | collective-permute-start | bytes 3145736 | tf_op jit(solution)/shard_map/ppermute | solution.py:258
  13.0 0.0 collective-permute-done.5
  13.0 0.0 collective-permute-done.6
  13.0 0.7 %collective-permute-start.8 = (bf16[128,512]{1,0:T(8,128)(2,1)S(1)}, bf16[128,512]{1,0:T(8,128)(2,1)S(1)}, u32[]{:S(2)}, u32[]{:S(2)}) collective-permute-start(bf16[128,512]{1,0:T(8,128)(2,1)S(1)} %add_add_fusion.3), channel_id=1, source_target_pairs={{0,5},{8,13},{16,21},{24,29},{32,37},{40,45},{48,53},{56,61},{64,6... | collective-permute-start | bytes 393224 | tf_op jit(solution)/shard_map/ppermute | solution.py:258
  13.7 0.7 %collective-permute-start.7 = (bf16[128,512]{1,0:T(8,128)(2,1)S(1)}, bf16[128,512]{1,0:T(8,128)(2,1)S(1)}, u32[]{:S(2)}, u32[]{:S(2)}) collective-permute-start(bf16[128,512]{1,0:T(8,128)(2,1)S(1)} %add_add_fusion.3), channel_id=1, source_target_pairs={{0,3},{8,11},{16,19},{24,27},{32,35},{40,43},{48,51},{56,59},{64,6... | collective-permute-start | bytes 393224 | tf_op jit(solution)/shard_map/ppermute | solution.py:258
  14.4 0.0 collective-permute-done.8
  14.4 0.0 collective-permute-done.7
  14.4 5.9 %collective-permute-done.10.y6_ref = bf16[512,1024]{1,0:T(8,128)(2,1)S(1)} collective-permute-done((bf16[512,1024]{1,0:T(8,128)(2,1)S(1)}, bf16[512,1024]{1,0:T(8,128)(2,1)S(1)}, u32[]{:S(2)}, u32[]{:S(2)}) %collective-permute-start.10) | collective-permute-done | bytes 1048608 | tf_op jit(solution)/shard_map/ppermute | solution.py:258
  20.4 1.4 %collective-permute-done.9.y2_ref = bf16[512,1024]{1,0:T(8,128)(2,1)S(1)} collective-permute-done((bf16[512,1024]{1,0:T(8,128)(2,1)S(1)}, bf16[512,1024]{1,0:T(8,128)(2,1)S(1)}, u32[]{:S(2)}, u32[]{:S(2)}) %collective-permute-start.9) | collective-permute-done | bytes 1048608 | tf_op jit(solution)/shard_map/ppermute | solution.py:258
  21.7 1.3 %collective-permute-start.12 = (bf16[128,512]{1,0:T(8,128)(2,1)S(1)}, bf16[128,512]{1,0:T(8,128)(2,1)S(1)}, u32[]{:S(2)}, u32[]{:S(2)}) collective-permute-start(bf16[128,512]{1,0:T(8,128)(2,1)S(1)} %add_add_fusion.2), channel_id=1, source_target_pairs={{0,7},{8,15},{16,23},{24,31},{32,39},{40,47},{48,55},{56,63},{64,7... | collective-permute-start | bytes 393224 | tf_op jit(solution)/shard_map/ppermute | solution.py:258
  23.0 0.7 %collective-permute-start.11 = (bf16[128,512]{1,0:T(8,128)(2,1)S(1)}, bf16[128,512]{1,0:T(8,128)(2,1)S(1)}, u32[]{:S(2)}, u32[]{:S(2)}) collective-permute-start(bf16[128,512]{1,0:T(8,128)(2,1)S(1)} %add_add_fusion.2), channel_id=1, source_target_pairs={{0,1},{8,9},{16,17},{24,25},{32,33},{40,41},{48,49},{56,57},{64,65... | collective-permute-start | bytes 393224 | tf_op jit(solution)/shard_map/ppermute | solution.py:258
  23.7 20.2 %collective-permute-done.12 = bf16[128,512]{1,0:T(8,128)(2,1)S(1)} collective-permute-done((bf16[128,512]{1,0:T(8,128)(2,1)S(1)}, bf16[128,512]{1,0:T(8,128)(2,1)S(1)}, u32[]{:S(2)}, u32[]{:S(2)}) %collective-permute-start.12) | collective-permute-done | bytes 131104 | tf_op jit(solution)/shard_map/ppermute | solution.py:258
  43.9 0.0 collective-permute-done.11
  43.9 0.0 collective-permute-done.13.y4_ref
  43.9 0.1 shard_map.30.even_ref
  44.1 1.4 %collective-permute-start.14 = (bf16[512,1024]{1,0:T(8,128)(2,1)S(1)}, bf16[512,1024]{1,0:T(8,128)(2,1)S(1)}, u32[]{:S(2)}, u32[]{:S(2)}) collective-permute-start(bf16[512,1024]{1,0:T(8,128)(2,1)S(1)} %shard_map.30.even_ref), channel_id=1, source_target_pairs={{0,32},{1,33},{2,34},{3,35},{4,36},{5,37},{6,38},{7,39},{8,40},{9,... | collective-permute-start | bytes 3145736 | tf_op jit(solution)/shard_map/ppermute | solution.py:258
  45.4 2.1 %collective-permute-start.17 = (bf16[128,512]{1,0:T(8,128)(2,1)S(1)}, bf16[128,512]{1,0:T(8,128)(2,1)S(1)}, u32[]{:S(2)}, u32[]{:S(2)}) collective-permute-start(bf16[128,512]{1,0:T(8,128)(2,1)S(1)} %add_add_fusion.1.q0_ref), channel_id=1, source_target_pairs={{0,16},{1,17},{2,18},{3,19},{4,20},{5,21},{6,22},{7,23},{32,48},{3... | collective-permute-start | bytes 393224 | tf_op jit(solution)/shard_map/ppermute | solution.py:258
  47.5 1.8 %collective-permute-start.16 = (bf16[128,512]{1,0:T(8,128)(2,1)S(1)}, bf16[128,512]{1,0:T(8,128)(2,1)S(1)}, u32[]{:S(2)}, u32[]{:S(2)}) collective-permute-start(bf16[128,512]{1,0:T(8,128)(2,1)S(1)} %add_add_fusion.1.q0_ref), channel_id=1, source_target_pairs={{0,24},{1,25},{2,26},{3,27},{4,28},{5,29},{6,30},{7,31},{32,56},{3... | collective-permute-start | bytes 393224 | tf_op jit(solution)/shard_map/ppermute | solution.py:258
  49.3 0.6 %collective-permute-start.15 = (bf16[128,512]{1,0:T(8,128)(2,1)S(1)}, bf16[128,512]{1,0:T(8,128)(2,1)S(1)}, u32[]{:S(2)}, u32[]{:S(2)}) collective-permute-start(bf16[128,512]{1,0:T(8,128)(2,1)S(1)} %add_add_fusion.1.q0_ref), channel_id=1, source_target_pairs={{0,8},{1,9},{2,10},{3,11},{4,12},{5,13},{6,14},{7,15},{32,40},{33,... | collective-permute-start | bytes 393224 | tf_op jit(solution)/shard_map/ppermute | solution.py:258
  49.9 2.1 %collective-permute-done.17.q2_ref = bf16[128,512]{1,0:T(8,128)(2,1)S(1)} collective-permute-done((bf16[128,512]{1,0:T(8,128)(2,1)S(1)}, bf16[128,512]{1,0:T(8,128)(2,1)S(1)}, u32[]{:S(2)}, u32[]{:S(2)}) %collective-permute-start.17) | collective-permute-done | bytes 131104 | tf_op jit(solution)/shard_map/ppermute | solution.py:258
  52.0 2.3 %collective-permute-done.16.q3_ref = bf16[128,512]{1,0:T(8,128)(2,1)S(1)} collective-permute-done((bf16[128,512]{1,0:T(8,128)(2,1)S(1)}, bf16[128,512]{1,0:T(8,128)(2,1)S(1)}, u32[]{:S(2)}, u32[]{:S(2)}) %collective-permute-start.16) | collective-permute-done | bytes 131104 | tf_op jit(solution)/shard_map/ppermute | solution.py:258
  54.3 1.2 %collective-permute-done.15.q1_ref = bf16[128,512]{1,0:T(8,128)(2,1)S(1)} collective-permute-done((bf16[128,512]{1,0:T(8,128)(2,1)S(1)}, bf16[128,512]{1,0:T(8,128)(2,1)S(1)}, u32[]{:S(2)}, u32[]{:S(2)}) %collective-permute-start.15) | collective-permute-done | bytes 131104 | tf_op jit(solution)/shard_map/ppermute | solution.py:258
  55.5 0.0 collective-permute-done.14.odd_ref
  55.5 1.8 %shard_map.31 = bf16[512,1024]{1,0:T(8,128)(2,1)} custom-call(f32[8,64]{1,0:T(8,128)S(1)} %copy-done.1, bf16[512,1024]{1,0:T(8,128)(2,1)S(1)} %copy-done, bf16[512,1024]{1,0:T(8,128)(2,1)S(1)} %shard_map.30.even_ref, bf16[512,1024]{1,0:T(8,128)(2,1)S(1)} %collective-permute-done.14.odd_ref, bf16[128,512]{1,0:T(8,128)(2,1)S(1)} %add_add_fusion.1.q0_ref, ...), custom_call_target="tpu_custom_call" | custom-call | flops 536870912 | bytes 4194304 | tf_op jit(solution)/shard_map/pallas_call | solution.py:240
  (3 shorter events, 0.1 us)
Async XLA Ops:
  0.1 3.0 %copy-start = (bf16[512,1024]{1,0:T(8,128)(2,1)S(1)}, bf16[512,1024]{1,0:T(8,128)(2,1)}, u32[]{:S(2)}) copy-start(bf16[512,1024]{1,0:T(8,128)(2,1)} %own_ref.3) | copy-start | bytes 3145732
  0.1 2.2 %collective-permute-start.2 = (bf16[320,512]{1,0:T(8,128)(2,1)S(1)}, bf16[320,512]{1,0:T(8,128)(2,1)S(1)}, u32[]{:S(2)}, u32[]{:S(2)}) collective-permute-start(bf16[320,512]{1,0:T(8,128)(2,1)S(1)} %shard_map.28), channel_id=1, source_target_pairs={{0,128}} | collective-permute-start | bytes 983048 | tf_op jit(solution)/shard_map/ppermute | solution.py:258
  0.9 1.4 %collective-permute-start.1 = (bf16[320,512]{1,0:T(8,128)(2,1)S(1)}, bf16[320,512]{1,0:T(8,128)(2,1)S(1)}, u32[]{:S(2)}, u32[]{:S(2)}) collective-permute-start(bf16[320,512]{1,0:T(8,128)(2,1)S(1)} %shard_map.28), channel_id=1, source_target_pairs={{0,192}} | collective-permute-start | bytes 983048 | tf_op jit(solution)/shard_map/ppermute | solution.py:258
  1.6 0.7 %collective-permute-start = (bf16[320,512]{1,0:T(8,128)(2,1)S(1)}, bf16[320,512]{1,0:T(8,128)(2,1)S(1)}, u32[]{:S(2)}, u32[]{:S(2)}) collective-permute-start(bf16[320,512]{1,0:T(8,128)(2,1)S(1)} %shard_map.28), channel_id=1, source_target_pairs={{0,64}} | collective-permute-start | bytes 983048 | tf_op jit(solution)/shard_map/ppermute | solution.py:258
  2.3 7.2 %copy-start.1 = (f32[8,64]{1,0:T(8,128)S(1)}, f32[8,64]{1,0:T(8,128)}, u32[]{:S(2)}) copy-start(f32[8,64]{1,0:T(8,128)} %scales_ref.3) | copy-start | bytes 6148
  2.4 7.1 %collective-permute-start.3 = (bf16[320,512]{1,0:T(8,128)(2,1)S(1)}, bf16[320,512]{1,0:T(8,128)(2,1)S(1)}, u32[]{:S(2)}, u32[]{:S(2)}) collective-permute-start(bf16[320,512]{1,0:T(8,128)(2,1)S(1)} %get-tuple-element.36), channel_id=1, source_target_pairs={{0,32},{32,0},{64,96},{96,64},{128,160},{160,128},{192,224},{224,1... | collective-permute-start | bytes 983048 | tf_op jit(solution)/shard_map/ppermute | solution.py:258
  3.1 17.2 %collective-permute-start.10 = (bf16[512,1024]{1,0:T(8,128)(2,1)S(1)}, bf16[512,1024]{1,0:T(8,128)(2,1)S(1)}, u32[]{:S(2)}, u32[]{:S(2)}) collective-permute-start(bf16[512,1024]{1,0:T(8,128)(2,1)S(1)} %copy-done), channel_id=1, source_target_pairs={{0,192},{1,193},{2,194},{3,195},{4,196},{5,197},{6,198},{7,199},{8... | collective-permute-start | bytes 3145736 | tf_op jit(solution)/shard_map/ppermute | solution.py:258
  8.1 13.6 %collective-permute-start.9 = (bf16[512,1024]{1,0:T(8,128)(2,1)S(1)}, bf16[512,1024]{1,0:T(8,128)(2,1)S(1)}, u32[]{:S(2)}, u32[]{:S(2)}) collective-permute-start(bf16[512,1024]{1,0:T(8,128)(2,1)S(1)} %copy-done), channel_id=1, source_target_pairs={{0,64},{1,65},{2,66},{3,67},{4,68},{5,69},{6,70},{7,71},{8,72},{9,... | collective-permute-start | bytes 3145736 | tf_op jit(solution)/shard_map/ppermute | solution.py:258
  9.6 2.0 %collective-permute-start.4 = (bf16[128,512]{1,0:T(8,128)(2,1)S(1)}, bf16[128,512]{1,0:T(8,128)(2,1)S(1)}, u32[]{:S(2)}, u32[]{:S(2)}) collective-permute-start(bf16[128,512]{1,0:T(8,128)(2,1)S(1)} %get-tuple-element.24), channel_id=1, source_target_pairs={{0,16},{32,48},{64,80},{96,112},{128,144},{160,176},{192,208},{224... | collective-permute-start | bytes 393224 | tf_op jit(solution)/shard_map/ppermute | solution.py:258
  10.3 2.7 %collective-permute-start.5 = (bf16[128,512]{1,0:T(8,128)(2,1)S(1)}, bf16[128,512]{1,0:T(8,128)(2,1)S(1)}, u32[]{:S(2)}, u32[]{:S(2)}) collective-permute-start(bf16[128,512]{1,0:T(8,128)(2,1)S(1)} %get-tuple-element.25), channel_id=1, source_target_pairs={{0,8},{32,40},{64,72},{96,104},{128,136},{160,168},{192,200},{224,... | collective-permute-start | bytes 393224 | tf_op jit(solution)/shard_map/ppermute | solution.py:258
  10.9 2.1 %collective-permute-start.6 = (bf16[128,512]{1,0:T(8,128)(2,1)S(1)}, bf16[128,512]{1,0:T(8,128)(2,1)S(1)}, u32[]{:S(2)}, u32[]{:S(2)}) collective-permute-start(bf16[128,512]{1,0:T(8,128)(2,1)S(1)} %get-tuple-element.26), channel_id=1, source_target_pairs={{0,24},{32,56},{64,88},{96,120},{128,152},{160,184},{192,216},{224... | collective-permute-start | bytes 393224 | tf_op jit(solution)/shard_map/ppermute | solution.py:258
  11.6 32.3 %collective-permute-start.13 = (bf16[512,1024]{1,0:T(8,128)(2,1)S(1)}, bf16[512,1024]{1,0:T(8,128)(2,1)S(1)}, u32[]{:S(2)}, u32[]{:S(2)}) collective-permute-start(bf16[512,1024]{1,0:T(8,128)(2,1)S(1)} %copy-done), channel_id=1, source_target_pairs={{0,128},{1,129},{2,130},{3,131},{4,132},{5,133},{6,134},{7,135},{8... | collective-permute-start | bytes 3145736 | tf_op jit(solution)/shard_map/ppermute | solution.py:258
  13.0 1.4 %collective-permute-start.8 = (bf16[128,512]{1,0:T(8,128)(2,1)S(1)}, bf16[128,512]{1,0:T(8,128)(2,1)S(1)}, u32[]{:S(2)}, u32[]{:S(2)}) collective-permute-start(bf16[128,512]{1,0:T(8,128)(2,1)S(1)} %add_add_fusion.3), channel_id=1, source_target_pairs={{0,5},{8,13},{16,21},{24,29},{32,37},{40,45},{48,53},{56,61},{64,6... | collective-permute-start | bytes 393224 | tf_op jit(solution)/shard_map/ppermute | solution.py:258
  13.7 0.7 %collective-permute-start.7 = (bf16[128,512]{1,0:T(8,128)(2,1)S(1)}, bf16[128,512]{1,0:T(8,128)(2,1)S(1)}, u32[]{:S(2)}, u32[]{:S(2)}) collective-permute-start(bf16[128,512]{1,0:T(8,128)(2,1)S(1)} %add_add_fusion.3), channel_id=1, source_target_pairs={{0,3},{8,11},{16,19},{24,27},{32,35},{40,43},{48,51},{56,59},{64,6... | collective-permute-start | bytes 393224 | tf_op jit(solution)/shard_map/ppermute | solution.py:258
  21.7 22.2 %collective-permute-start.12 = (bf16[128,512]{1,0:T(8,128)(2,1)S(1)}, bf16[128,512]{1,0:T(8,128)(2,1)S(1)}, u32[]{:S(2)}, u32[]{:S(2)}) collective-permute-start(bf16[128,512]{1,0:T(8,128)(2,1)S(1)} %add_add_fusion.2), channel_id=1, source_target_pairs={{0,7},{8,15},{16,23},{24,31},{32,39},{40,47},{48,55},{56,63},{64,7... | collective-permute-start | bytes 393224 | tf_op jit(solution)/shard_map/ppermute | solution.py:258
  23.0 20.9 %collective-permute-start.11 = (bf16[128,512]{1,0:T(8,128)(2,1)S(1)}, bf16[128,512]{1,0:T(8,128)(2,1)S(1)}, u32[]{:S(2)}, u32[]{:S(2)}) collective-permute-start(bf16[128,512]{1,0:T(8,128)(2,1)S(1)} %add_add_fusion.2), channel_id=1, source_target_pairs={{0,1},{8,9},{16,17},{24,25},{32,33},{40,41},{48,49},{56,57},{64,65... | collective-permute-start | bytes 393224 | tf_op jit(solution)/shard_map/ppermute | solution.py:258
  44.1 11.4 %collective-permute-start.14 = (bf16[512,1024]{1,0:T(8,128)(2,1)S(1)}, bf16[512,1024]{1,0:T(8,128)(2,1)S(1)}, u32[]{:S(2)}, u32[]{:S(2)}) collective-permute-start(bf16[512,1024]{1,0:T(8,128)(2,1)S(1)} %shard_map.30.even_ref), channel_id=1, source_target_pairs={{0,32},{1,33},{2,34},{3,35},{4,36},{5,37},{6,38},{7,39},{8,40},{9,... | collective-permute-start | bytes 3145736 | tf_op jit(solution)/shard_map/ppermute | solution.py:258
  45.4 6.6 %collective-permute-start.17 = (bf16[128,512]{1,0:T(8,128)(2,1)S(1)}, bf16[128,512]{1,0:T(8,128)(2,1)S(1)}, u32[]{:S(2)}, u32[]{:S(2)}) collective-permute-start(bf16[128,512]{1,0:T(8,128)(2,1)S(1)} %add_add_fusion.1.q0_ref), channel_id=1, source_target_pairs={{0,16},{1,17},{2,18},{3,19},{4,20},{5,21},{6,22},{7,23},{32,48},{3... | collective-permute-start | bytes 393224 | tf_op jit(solution)/shard_map/ppermute | solution.py:258
  47.5 6.8 %collective-permute-start.16 = (bf16[128,512]{1,0:T(8,128)(2,1)S(1)}, bf16[128,512]{1,0:T(8,128)(2,1)S(1)}, u32[]{:S(2)}, u32[]{:S(2)}) collective-permute-start(bf16[128,512]{1,0:T(8,128)(2,1)S(1)} %add_add_fusion.1.q0_ref), channel_id=1, source_target_pairs={{0,24},{1,25},{2,26},{3,27},{4,28},{5,29},{6,30},{7,31},{32,56},{3... | collective-permute-start | bytes 393224 | tf_op jit(solution)/shard_map/ppermute | solution.py:258
  49.3 6.2 %collective-permute-start.15 = (bf16[128,512]{1,0:T(8,128)(2,1)S(1)}, bf16[128,512]{1,0:T(8,128)(2,1)S(1)}, u32[]{:S(2)}, u32[]{:S(2)}) collective-permute-start(bf16[128,512]{1,0:T(8,128)(2,1)S(1)} %add_add_fusion.1.q0_ref), channel_id=1, source_target_pairs={{0,8},{1,9},{2,10},{3,11},{4,12},{5,13},{6,14},{7,15},{32,40},{33,... | collective-permute-start | bytes 393224 | tf_op jit(solution)/shard_map/ppermute | solution.py:258
